TPU v7x, 128 devices: a whole 4x4x4 slice. The times are simulated.
128 devices in a mesh: dp: 4 (over z), proto: 32 (over y, x, core).
Axes of the slice: x: 4, y: 4, z: 4, core: 2. Of those that a mesh axis runs over, the one named last changes fastest.
Arguments:
- teacher_hidden: bfloat16 [3072, 2048], P(('dp', 'proto')), may hold values from -6 to 6
- teacher_proj: bfloat16 [2048, 384], replicated, may hold values from -5.524272 to 5.524272
- student_hidden: bfloat16 [3072, 384], P(('dp', 'proto')), may hold values from -8 to 8
- teacher_protos: bfloat16 [384, 131072], P(None, ('dp', 'proto')), may hold values from -8 to 8
- student_protos: bfloat16 [384, 131072], P(None, ('dp', 'proto')), may hold values from -8 to 8
Outputs:
- loss_mean: float32 [], replicated
- d_student: float32 [3072, 384], P(('dp', 'proto'))
- d_protos: float32 [384, 131072], P(None, ('dp', 'proto'))
All inputs are finite; a program needn't handle non-finite values.
Results may differ from a plain program's by a relative error of at most 0.0021.
Values may be sent and summed in bfloat16 or wider, within the bound.
No kernel may reach another device: no remote copies, remote signals or barrier semaphores. Data moves between devices by JAX's collectives and lax.ppermute only.
A program may use at most 128 MiB of HBM per device.

v0:
```python
import jax
import jax.numpy as jnp
from jax import lax
from jax.sharding import PartitionSpec as P

ITERS = 3


EPS = 1e-06
teacher_temp = 0.07
student_temp = 0.1


def unit_columns(weights):
    widened = weights.astype(jnp.float32)
    inv_norm = lax.rsqrt(jnp.sum(widened * widened, axis=0, keepdims=True) + EPS)
    return (widened * inv_norm, inv_norm)


def body(teacher_hidden, teacher_proj, student_hidden, teacher_protos, student_protos):
    devices = lax.axis_size(("dp", "proto"))
    rows_dev = student_hidden.shape[0]
    images = rows_dev * devices
    total_cols = teacher_protos.shape[1] * devices
    t_hid = jnp.dot(teacher_hidden, teacher_proj, preferred_element_type=jnp.float32)
    t_bot = (t_hid * lax.rsqrt(jnp.sum(t_hid * t_hid, axis=1, keepdims=True) + EPS)).astype(
        jnp.bfloat16
    )
    s_hid = student_hidden.astype(jnp.float32)
    s_inv = lax.rsqrt(jnp.sum(s_hid * s_hid, axis=1, keepdims=True) + EPS)
    s_unit = s_hid * s_inv
    s_bot = s_unit.astype(jnp.bfloat16)
    t_unitcols, _ = unit_columns(teacher_protos)
    t_cols = t_unitcols.astype(jnp.bfloat16)
    s_unitcols, s_winv = unit_columns(student_protos)
    s_cols = s_unitcols.astype(jnp.bfloat16)
    t_all, s_all = (
        lax.all_gather(t_bot, ("dp", "proto"), axis=0, tiled=True),
        lax.all_gather(s_bot, ("dp", "proto"), axis=0, tiled=True),
    )
    exp_teacher = jnp.exp(jnp.dot(t_all, t_cols, preferred_element_type=jnp.float32) / teacher_temp)
    logits = jnp.dot(s_all, s_cols, preferred_element_type=jnp.float32) / student_temp
    powers = jnp.exp(logits)
    weight = jnp.ones((images,), jnp.float32)
    partition = lax.psum(jnp.sum(powers, axis=1), ("dp", "proto"))
    for sweep in range(ITERS):
        col_scale = 1.0 / (total_cols * jnp.sum(exp_teacher * weight[:, None], axis=0))
        row_total = lax.psum(jnp.sum(exp_teacher * col_scale[None, :], axis=1), ("dp", "proto"))
        weight = 1.0 / (images * row_total)
    target = exp_teacher * col_scale[None, :] / row_total[:, None]
    log_total = jnp.log(partition)
    local_loss = jnp.sum(target * (log_total[:, None] - logits))
    loss_mean = lax.psum(local_loss, ("dp", "proto")) / images
    grad_logits = ((powers / partition[:, None] - target) / student_temp).astype(jnp.bfloat16)
    d_unit = lax.dot_general(
        s_all, grad_logits, (((0,), (0,)), ((), ())), preferred_element_type=jnp.float32
    )
    d_protos = s_winv * (d_unit - s_unitcols * jnp.sum(s_unitcols * d_unit, axis=0, keepdims=True))
    local_terms = lax.dot_general(
        grad_logits, s_cols, (((1,), (1,)), ((), ())), preferred_element_type=jnp.float32
    )
    summed = lax.psum(local_terms, ("dp", "proto"))
    d_bot = lax.dynamic_slice_in_dim(
        summed, lax.axis_index(("dp", "proto")) * rows_dev, rows_dev, 0
    )
    d_student = s_inv * (d_bot - s_unit * jnp.sum(s_unit * d_bot, axis=1, keepdims=True))
    return (loss_mean, d_student, d_protos)


def solution(mesh):
    return jax.shard_map(
        body,
        mesh=mesh,
        in_specs=(
            P(("dp", "proto"), None),
            P(),
            P(("dp", "proto"), None),
            P(None, ("dp", "proto")),
            P(None, ("dp", "proto")),
        ),
        out_specs=(P(), P(("dp", "proto"), None), P(None, ("dp", "proto"))),
        check_vma=False,
    )
```

profile of v0, /device:TPU:0, one launch (start us, length us, event | category | flops | bytes accessed | tf_op | source)
XLA Modules:
  0.0 493.8 jit_solution(13251873489222309102)
XLA Ops:
  7.2 0.0 all-gather.3.cloned.1.call-start
  7.2 1.4 copy-done
  8.6 1.3 multiply_reduce_fusion.6
  9.9 0.7 multiply_convert_fusion.1
  10.6 0.0 all-gather.5.cloned.1.call-start
  10.7 0.8 fusion.21
  11.5 1.4 fusion.17
  13.0 0.0 all-reduce.3.cloned.1.call-start
  13.0 1.3 fusion.3
  14.3 1.3 fusion.8
  15.7 63.7 %all-gather.3.cloned.1.call-done = bf16[3072,384]{1,0:T(8,128)(2,1)} async-done(((bf16[24,384]{1,0:T(8,128)(2,1)}), bf16[3072,384]{1,0:T(8,128)(2,1)}) %all-gather.3.cloned.1.call-update) | async-done | bytes 2359312 | tf_op jit(solution)/shard_map/all_gather | solution.py:38
  79.4 5.9 %fusion.22 = (f32[1024]{0:T(1024)S(1)}, f32[3072,1024]{1,0:T(8,128)S(1)}) fusion(bf16[3072,384]{1,0:T(8,128)(2,1)} %all-gather.3.cloned.1.call-done, bf16[384,1024]{1,0:T(8,128)(2,1)} %param.8, f32[1024]{0:T(1024)S(1)} %add_rsqrt_fusion.1), kind=kOutput, calls=%fused_computation.46 | convolution fusion | flops 2423389184 | bytes 15736832 | tf_op jit(solution)/shard_map/dot_general | solution.py:41
  85.3 4.5 copy-done.1
  89.8 0.9 multiply_reduce_fusion.4
  90.7 63.3 %psum.42 = f32[3072]{0:T(1024)S(1)} all-reduce(f32[3072]{0:T(1024)S(1)} %multiply_reduce_fusion.4), channel_id=1, replica_groups=mesh['dp'=4,'proto'=32] {'dp','proto'}, use_global_device_ids=true, to_apply=%region_4.0 | all-reduce | flops 3072 | bytes 24576 | tf_op jit(solution)/shard_map/psum | solution.py:48
  154.0 5.6 %multiply_reduce_fusion.3 = f32[1024]{0:T(1024)S(1)} fusion(f32[3072,1024]{1,0:T(8,128)} %copy-done.1, f32[3072]{0:T(1024)S(1)} %multiply_divide_fusion.2), kind=kLoop, calls=%fused_computation.4 | loop fusion | flops 6290432 | bytes 12599296 | tf_op jit(solution)/shard_map/reduce_sum | solution.py:47
  159.6 2.5 copy-done.2
  162.1 0.9 multiply_reduce_fusion.2
  163.0 65.0 %psum.43 = f32[3072]{0:T(1024)S(1)} all-reduce(f32[3072]{0:T(1024)S(1)} %multiply_reduce_fusion.2), channel_id=1, replica_groups=mesh['dp'=4,'proto'=32] {'dp','proto'}, use_global_device_ids=true, to_apply=%region_7.0 | all-reduce | flops 3072 | bytes 24576 | tf_op jit(solution)/shard_map/psum | solution.py:48
  228.0 5.5 %multiply_reduce_fusion.1 = f32[1024]{0:T(1024)S(1)} fusion(f32[3072,1024]{1,0:T(8,128)} %copy-done.1, f32[3072]{0:T(1024)S(1)} %multiply_divide_fusion.1), kind=kLoop, calls=%fused_computation.2 | loop fusion | flops 6290432 | bytes 12599296 | tf_op jit(solution)/shard_map/reduce_sum | solution.py:47
  233.5 5.6 %multiply_reduce_fusion.5 = f32[3072]{0:T(1024)S(1)} fusion(f32[3072,1024]{1,0:T(8,128)} %copy-done.1, f32[1024]{0:T(1024)S(1)} %multiply_divide_fusion.3), kind=kLoop, calls=%fused_computation.9 | loop fusion | flops 6288384 | bytes 12599296 | tf_op jit(solution)/shard_map/reduce_sum | solution.py:48
  239.1 8.4 %exponential_reduce_fusion = (f32[3072]{0:T(1024)S(1)}, f32[3072,1024]{1,0:T(8,128)}) fusion(bf16[3072,384]{1,0:T(8,128)(2,1)} %all-gather.5.cloned.1.call-done, bf16[384,1024]{1,0:T(8,128)(2,1)S(1)} %copy-done.4, f32[1024]{0:T(1024)S(1)} %add_rsqrt_fusion), kind=kOutput, calls=%fused_computation.7 | convolution fusion | flops 2423387136 | bytes 15745024 | tf_op jit(solution)/shard_map/dot_general | solution.py:42
  247.5 62.4 %all-reduce = (f32[3072]{0:T(1024)S(1)}, f32[3072]{0:T(1024)S(1)}) all-reduce(f32[3072]{0:T(1024)S(1)} %get-tuple-element.7, f32[3072]{0:T(1024)S(1)} %multiply_reduce_fusion.5), channel_id=1, replica_groups=mesh['dp'=4,'proto'=32] {'dp','proto'}, use_global_device_ids=true, to_apply=%region_14.0 | all-reduce | flops 6144 | bytes 49152 | tf_op jit(solution)/shard_map/psum | solution.py:45
  310.0 12.8 %multiply_convert_fusion = (bf16[3072,1024]{1,0:T(8,128)(2,1)S(1)}, f32[]{:T(128)}) fusion(f32[3072,1024]{1,0:T(8,128)} %get-tuple-element.8, f32[3072]{0:T(1024)S(1)} %get-tuple-element.3, f32[3072]{0:T(1024)S(1)} %get-tuple-element.4, f32[3072,1024]{1,0:T(8,128)} %copy-done.1, f32[1024]{0:T(1024)S(1)} %multiply_divide_fusion.3, f32[3072]{0:T(1024)S(1)} %log.3), kind=kLoop, calls=%fused_computation | loop fusion | flops 31457280 | bytes 31498244 | tf_op jit(solution)/shard_map/convert_element_type | solution.py:54
  322.7 2.7 copy-done.3
  325.4 5.1 %fusion.11 = f32[3072,384]{1,0:T(8,128)} fusion(bf16[3072,1024]{1,0:T(8,128)(2,1)S(1)} %get-tuple-element.5, bf16[384,1024]{1,0:T(8,128)(2,1)S(1)} %copy-done.4, f32[1024]{0:T(1024)S(1)} %add_rsqrt_fusion), kind=kOutput, calls=%fused_computation.24 | convolution fusion | flops 2417098752 | bytes 11800576 | tf_op jit(solution)/shard_map/dot_general | solution.py:59
  330.5 64.9 %psum.46 = f32[]{:T(128)} all-reduce(f32[]{:T(128)} %get-tuple-element.6), channel_id=1, replica_groups=mesh['dp'=4,'proto'=32] {'dp','proto'}, use_global_device_ids=true, to_apply=%region_16.0 | all-reduce | flops 1 | bytes 8 | tf_op jit(solution)/shard_map/psum | solution.py:53
  396.1 5.5 %fusion.5 = (f32[1024]{0:T(1024)S(1)}, f32[384,1024]{1,0:T(8,128)S(1)}) fusion(bf16[384,1024]{1,0:T(8,128)(2,1)S(1)} %copy-done.4, f32[1024]{0:T(1024)S(1)} %add_rsqrt_fusion, bf16[3072,384]{1,0:T(8,128)(2,1)} %all-gather.5.cloned.1.call-done, bf16[3072,1024]{1,0:T(8,128)(2,1)} %copy-done.3), kind=kOutput, calls=%fused_computation.19 | convolution fusion | flops 2417490944 | bytes 11018240 | tf_op jit(solution)/shard_map/dot_general | solution.py:55
  401.6 1.4 fusion.7
  403.1 80.6 %all-reduce.3.cloned.1.call-done = f32[3072,384]{1,0:T(8,128)} async-done(((f32[3072,384]{1,0:T(8,128)}), f32[3072,384]{1,0:T(8,128)}) %all-reduce.3.cloned.1.call-update) | async-done | bytes 4718608 | tf_op jit(solution)/shard_map/psum | solution.py:62
  483.7 0.9 fusion.18
  484.7 1.5 fusion.20
  (22 shorter events, 0.2 us)
Async XLA Ops:
  7.2 1.4 copy-start
  7.2 72.2 %all-gather.3.cloned.1.call-start = ((), (), s32[]{:S(2)}) async-start(), calls=%async_computation | async-start | bytes 2377728 | tf_op jit(solution)/shard_map/all_gather | solution.py:38
  10.6 228.4 %all-gather.5.cloned.1.call-start = ((), (), s32[]{:S(2)}) async-start(), calls=%async_computation.1 | async-start | bytes 2377728 | tf_op jit(solution)/shard_map/all_gather | solution.py:39
  13.0 470.8 %all-reduce.3.cloned.1.call-start = ((), (), s32[]{:S(2)}) async-start(), calls=%async_computation.2 | async-start | bytes 9437184 | tf_op jit(solution)/shard_map/psum | solution.py:62
  85.3 4.5 copy-start.1
  154.0 8.2 %copy-start.2 = (f32[3072,1024]{1,0:T(8,128)S(1)}, f32[3072,1024]{1,0:T(8,128)}, u32[]{:S(2)}) copy-start(f32[3072,1024]{1,0:T(8,128)} %copy-done.1) | copy-start | bytes 37748740
  233.5 5.6 %copy-start.4 = (bf16[384,1024]{1,0:T(8,128)(2,1)S(1)}, bf16[384,1024]{1,0:T(8,128)(2,1)}, u32[]{:S(2)}) copy-start(bf16[384,1024]{1,0:T(8,128)(2,1)} %param.9) | copy-start | bytes 2359300
  322.7 2.7 copy-start.3
  396.1 87.7 %copy-start.5 = (bf16[24,384]{1,0:T(8,128)(2,1)S(1)}, bf16[24,384]{1,0:T(8,128)(2,1)}, u32[]{:S(2)}) copy-start(bf16[24,384]{1,0:T(8,128)(2,1)} %param.7) | copy-start | bytes 55300
Sparse Core Ops, SparseCore 0:
  11.6 67.7 all-gather.2
  82.9 62.6 all-gather.4
  330.6 153.0 all-reduce.2
where the time goes:
time: 495 us; the launch traced here: 494 us
  blocking collectives  256 us (52%)
  waiting for transfers between devices  144 us (29%)
  other arithmetic  40.7 us (8%)
  matrix products  26.3 us (5%)
  between operations  15.7 us (3%)
  local copies, waits for them, and re-layouts  11 us (2%)
    psum x2, blocking collectives, body(): lax.psum(jnp.sum(exp_teacher * col_scale[None, :], axis=1), ('dp', 'proto'))  128 us
    psum x1, waiting for transfers between devices, body(): summed = lax.psum(local_terms, ('dp', 'proto'))  80.6 us
    psum x1, blocking collectives, body(): loss_mean = lax.psum(local_loss, ('dp', 'proto')) / images  64.9 us
    all_gather x1, waiting for transfers between devices, body(): lax.all_gather(t_bot, ('dp', 'proto'), axis=0, tiled=True)  63.7 us
    psum x1, blocking collectives, body(): partition = lax.psum(jnp.sum(powers, axis=1), ('dp', 'proto'))  62.4 us
    convert_element_type x1, other arithmetic, body(): ((powers / partition[:, None] - target) / student_temp).astype(jnp.bfloat16)  12.8 us
    reduce_sum x2, other arithmetic, body(): jnp.sum(exp_teacher * weight[:, None], axis=0)  11.1 us
    unnamed x12, local copies, waits for them, and re-layouts  11 us
  transfers between devices with their start and end apart: 3, of which 2 were waited for; matrix products, arithmetic and copies ran while one was open for 7% of the time, Pallas kernels for 0%

commit v1 on v0

v1 whole, which is shorter than its diff:
```python
import jax
import jax.numpy as jnp
from jax import lax
from jax.experimental import pallas as pl
from jax.experimental.pallas import tpu as pltpu
from jax.sharding import Mesh
from jax.sharding import PartitionSpec as P

ITERS = 3
EPS = 1e-06
teacher_temp = 0.07
student_temp = 0.1

ALL = ("z", "y", "x", "c")
CHIPS = ("z", "y", "x")
SWAP = [(0, 1), (1, 0)]
F32 = jnp.float32
BF16 = jnp.bfloat16
MB = 1024 * 1024
NT = (((1,), (1,)), ((), ()))
VM = pl.BlockSpec(memory_space=pltpu.VMEM)
CHUNK = 256
PASS = 64


def call(kernel, out_shape, operands, vmem, scratch=(), flops=0, nbytes=0, trans=0):
    outs = out_shape if isinstance(out_shape, (tuple, list)) else (out_shape,)
    specs = tuple(VM for _ in outs)
    return pl.pallas_call(
        kernel,
        out_shape=out_shape,
        in_specs=[VM] * len(operands),
        out_specs=specs if isinstance(out_shape, (tuple, list)) else VM,
        scratch_shapes=list(scratch),
        compiler_params=pltpu.CompilerParams(vmem_limit_bytes=vmem * MB),
        cost_estimate=pl.CostEstimate(flops=flops, bytes_accessed=nbytes, transcendentals=trans),
    )(*operands)


def fold(row):
    width = row.shape[1] // 8
    return jnp.concatenate([row[:, j * width : (j + 1) * width] for j in range(8)], axis=0)


def spread(piece, ref):
    for i in range(ref.shape[0]):
        ref[i] = piece


def flat(block):
    return jnp.concatenate([block[j : j + 1, :] for j in range(8)], axis=1)


def total_row(mine, theirs):
    return flat(mine + jnp.concatenate([theirs[4:8, :], theirs[0:4, :]], axis=0))


def columns(w_block):
    wide = w_block.astype(F32)
    inv = lax.rsqrt(jnp.sum(wide * wide, axis=0, keepdims=True) + EPS)
    return wide * inv, inv


def teacher_rows_kernel(hid_ref, proj_ref, out_ref):
    t_hid = jnp.dot(hid_ref[...], proj_ref[...], preferred_element_type=F32)
    t_bot = (t_hid * lax.rsqrt(jnp.sum(t_hid * t_hid, axis=1, keepdims=True) + EPS)).astype(BF16)
    for i in range(out_ref.shape[0]):
        out_ref[i] = t_bot


def student_rows_kernel(hid_ref, out_ref):
    wide = hid_ref[...].astype(F32)
    out_ref[...] = (wide * lax.rsqrt(jnp.sum(wide * wide, axis=1, keepdims=True) + EPS)).astype(BF16)


def teacher_kernel(total_cols, w_ref, own_ref, other_ref, e_ref, out_ref, acc):
    half = own_ref.shape[0]
    cols = w_ref.shape[1]
    acc[...] = jnp.zeros_like(acc)

    def step(j, _):
        at = pl.ds(pl.multiple_of(j * CHUNK, CHUNK), CHUNK)
        unit, _inv = columns(w_ref[:, at])
        lhs = unit.T.astype(BF16)
        sums = jnp.zeros((CHUNK, 1), F32)
        for h, rows in enumerate((own_ref, other_ref)):
            prod = lax.dot_general(lhs, rows[...], NT, preferred_element_type=F32)
            expo = jnp.exp(prod * (1.0 / teacher_temp))
            e_ref[at, h * half : (h + 1) * half] = expo
            sums = sums + jnp.sum(expo, axis=1, keepdims=True)
        scale = 1.0 / (total_cols * sums)
        scaled = e_ref[at, :] * scale
        acc[...] += jnp.sum(scaled.reshape(CHUNK // 8, 8, 2 * half), axis=0)
        return 0

    lax.fori_loop(0, cols // CHUNK, step, 0)
    spread(fold(jnp.sum(acc[...], axis=0, keepdims=True)), out_ref)


def pass_kernel(total_cols, images, e_ref, mine_ref, theirs_ref, *rest):
    *extra, out_ref, cs_ref, weight, acc = rest
    total = total_row(mine_ref[...], theirs_ref[...])
    weight[...] = jnp.broadcast_to(1.0 / (images * total), weight.shape)
    acc[...] = jnp.zeros_like(acc)
    protos = e_ref.shape[0]
    n = e_ref.shape[1]

    def step(j, _):
        at = pl.ds(pl.multiple_of(j * PASS, PASS), PASS)
        expo = e_ref[at, :]
        weighted = expo.reshape(PASS // 8, 8, n) * weight[...][None]
        sums = jnp.sum(weighted.reshape(PASS, n), axis=1, keepdims=True)
        scale = 1.0 / (total_cols * sums)
        cs_ref[at, :] = scale
        acc[...] += jnp.sum((expo * scale).reshape(PASS // 8, 8, n), axis=0)
        return 0

    lax.fori_loop(0, protos // PASS, step, 0)
    piece = fold(jnp.sum(acc[...], axis=0, keepdims=True))
    spread(jnp.concatenate([piece] + [ref[...] for ref in extra], axis=0), out_ref)


def student_kernel(w_ref, own_ref, other_ref, lg_ref, cols_ref, out_ref, acc):
    half = own_ref.shape[0]
    cols = w_ref.shape[1]
    acc[...] = jnp.zeros_like(acc)

    def step(j, _):
        at = pl.ds(pl.multiple_of(j * CHUNK, CHUNK), CHUNK)
        unit, _inv = columns(w_ref[:, at])
        cols_ref[:, at] = unit.astype(BF16)
        lhs = unit.T.astype(BF16)
        for h, rows in enumerate((own_ref, other_ref)):
            lanes = slice(h * half, (h + 1) * half)
            prod = lax.dot_general(lhs, rows[...], NT, preferred_element_type=F32)
            logits = prod * (1.0 / student_temp)
            lg_ref[at, lanes] = logits
            acc[:, lanes] += jnp.sum(jnp.exp(logits).reshape(CHUNK // 8, 8, half), axis=0)
        return 0

    lax.fori_loop(0, cols // CHUNK, step, 0)
    out_ref[...] = fold(jnp.sum(acc[...], axis=0, keepdims=True))


def grad_kernel(
    e_ref, lg_ref, cs_ref, cols_ref, mine_ref, theirs_ref, g_ref, other_ref, loss_ref, rows
):
    protos, n = e_ref.shape
    half = n // 2
    part = total_row(mine_ref[8:16, :], theirs_ref[8:16, :])
    rows[0:1, :] = 1.0 / part
    rows[1:2, :] = 1.0 / total_row(mine_ref[0:8, :], theirs_ref[0:8, :])
    rows[2:3, :] = jnp.log(part)
    loss_ref[...] = jnp.zeros_like(loss_ref)

    def step(j, _):
        at = pl.ds(pl.multiple_of(j * PASS, PASS), PASS)
        logits = lg_ref[at, :]
        target = e_ref[at, :] * cs_ref[at, :] * rows[1:2, :]
        powers = jnp.exp(logits) * rows[0:1, :]
        g_ref[at, :] = ((powers - target) * (1.0 / student_temp)).astype(BF16)
        terms = target * (rows[2:3, :] - logits)
        folded = jnp.sum(terms.reshape(PASS // 8, 8, n), axis=0)
        loss_ref[...] += jnp.sum(folded.reshape(8, n // 128, 128), axis=1)
        return 0

    lax.fori_loop(0, protos // PASS, step, 0)
    bottleneck(cols_ref, g_ref, half, other_ref)


def bottleneck(cols_ref, g_ref, start, out_ref):
    for i in range(out_ref.shape[0] // CHUNK):
        lanes = slice(start + i * CHUNK, start + (i + 1) * CHUNK)
        block = jnp.dot(cols_ref[...], g_ref[:, lanes], preferred_element_type=F32)
        out_ref[i * CHUNK : (i + 1) * CHUNK, :] = block.T


def protos_kernel(g_ref, cols_ref, w_ref, own_ref, other_ref, dp_ref, db_ref):
    half = own_ref.shape[0]
    bottleneck(cols_ref, g_ref, 0, db_ref)

    def step(j, _):
        at = pl.ds(pl.multiple_of(j * CHUNK, CHUNK), CHUNK)
        d_unit = jnp.dot(g_ref[at, :half], own_ref[...], preferred_element_type=F32)
        d_unit = d_unit + jnp.dot(g_ref[at, half:], other_ref[...], preferred_element_type=F32)
        d_unit = d_unit.T
        unit, inv = columns(w_ref[:, at])
        dp_ref[:, at] = inv * (d_unit - unit * jnp.sum(unit * d_unit, axis=0, keepdims=True))
        return 0

    lax.fori_loop(0, w_ref.shape[1] // CHUNK, step, 0)


def pack_kernel(mine_ref, theirs_ref, loss_a, loss_b, out_ref):
    total = jnp.sum(jnp.sum(loss_a[...] + loss_b[...], axis=0, keepdims=True), axis=1, keepdims=True)
    high = total.astype(BF16).astype(F32)
    mid = (total - high).astype(BF16).astype(F32)
    low = total - high - mid
    row = lax.broadcasted_iota(jnp.int32, (8, 128), 0)
    tail = jnp.where(row == 0, high, jnp.where(row == 1, mid, jnp.where(row == 2, low, 0.0)))
    tail = tail.astype(BF16)

    def step(i, _):
        at = pl.ds(pl.multiple_of(i * 24, 8), 24)
        block = mine_ref[at, :] + theirs_ref[at, :]
        for k in range(3):
            out_ref[i, 24 * k : 24 * (k + 1), :] = block[:, 128 * k : 128 * (k + 1)].astype(BF16)
        out_ref[i, 72:80, :] = tail
        return 0

    lax.fori_loop(0, out_ref.shape[0], step, 0, unroll=4)


def finish_kernel(images, got_ref, hid_ref, ds_ref, loss_ref):
    total = jnp.sum(got_ref[...].astype(F32), axis=0)
    d_bot = jnp.concatenate([total[24 * k : 24 * (k + 1), :] for k in range(3)], axis=1)
    wide = hid_ref[...].astype(F32)
    inv = lax.rsqrt(jnp.sum(wide * wide, axis=1, keepdims=True) + EPS)
    unit = wide * inv
    ds_ref[...] = inv * (d_bot - unit * jnp.sum(unit * d_bot, axis=1, keepdims=True))
    loss_ref[...] = (total[72:73, :] + total[73:74, :] + total[74:75, :]) * (1.0 / images)


def body(teacher_hidden, teacher_proj, student_hidden, teacher_protos, student_protos):
    chips = lax.axis_size(CHIPS)
    rows_dev, bot = student_hidden.shape
    half = rows_dev * chips
    images = 2 * half
    protos = teacher_protos.shape[1]
    total_cols = protos * lax.axis_size(ALL)
    sds = jax.ShapeDtypeStruct

    def swap(x):
        return lax.ppermute(x, "c", SWAP)

    def exchange(x):
        return lax.all_to_all(x, CHIPS, 0, 0)

    def row_sums(x):
        mine = jnp.sum(exchange(x), axis=0)
        return mine, swap(mine)

    s_bot = call(student_rows_kernel, sds((rows_dev, bot), BF16), (student_hidden,), 2)
    s_own = lax.all_gather(s_bot, CHIPS, axis=0, tiled=True)
    s_bot, teacher_hidden = lax.optimization_barrier((s_bot, teacher_hidden))

    t_send = call(
        teacher_rows_kernel, sds((chips, rows_dev, bot), BF16), (teacher_hidden, teacher_proj), 6
    )
    t_own = exchange(t_send).reshape(half, bot)
    t_other = swap(t_own)

    vec = sds((chips, 8, images // 8), F32)
    expo, sent = call(
        lambda *r: teacher_kernel(total_cols, *r),
        (sds((protos, images), F32), vec),
        (teacher_protos, t_own, t_other),
        12,
        [pltpu.VMEM((8, images), F32)],
    )
    for sweep in range(1, ITERS):
        mine, theirs = row_sums(sent)
        extra = ()
        if sweep == 1:
            mine, s_own = lax.optimization_barrier((mine, s_own))
            s_other = swap(s_own)
        if sweep == ITERS - 1:
            logits, s_cols, part = call(
                student_kernel,
                (sds((protos, images), F32), sds((bot, protos), BF16), sds((8, images // 8), F32)),
                (student_protos, s_own, s_other),
                12,
                [pltpu.VMEM((8, images), F32)],
            )
            extra = (part,)
        sent, col_scale = call(
            lambda *r: pass_kernel(total_cols, images, *r),
            (sds((chips, 8 + 8 * len(extra), images // 8), F32), sds((protos, 1), F32)),
            (expo, mine, theirs) + extra,
            6,
            [pltpu.VMEM((8, images), F32), pltpu.VMEM((8, images), F32)],
        )
    mine, theirs = row_sums(sent)
    grads, d_other, loss_mine = call(
        grad_kernel,
        (sds((protos, images), BF16), sds((half, bot), F32), sds((8, 128), F32)),
        (expo, logits, col_scale, s_cols, mine, theirs),
        12,
        [pltpu.VMEM((8, images), F32)],
    )
    d_theirs = swap(d_other)
    loss_theirs = swap(loss_mine)
    d_protos, d_mine = call(
        protos_kernel,
        (sds((bot, protos), F32), sds((half, bot), F32)),
        (grads, s_cols, student_protos, s_own, s_other),
        12,
    )
    packed = call(
        pack_kernel,
        sds((chips, 80, 128), BF16),
        (d_mine, d_theirs, loss_mine, loss_theirs),
        4,
    )
    got = exchange(packed)
    d_student, loss = call(
        lambda *r: finish_kernel(images, *r),
        (sds((rows_dev, bot), F32), sds((1, 128), F32)),
        (got, student_hidden),
        4,
    )
    return loss[0, 0], d_student, d_protos


def solution(mesh):
    grid = Mesh(mesh.devices.reshape(4, 4, 4, 2), ALL)
    return jax.shard_map(
        body,
        mesh=grid,
        in_specs=(P(ALL, None), P(), P(ALL, None), P(None, ALL), P(None, ALL)),
        out_specs=(P(), P(ALL, None), P(None, ALL)),
        check_vma=False,
    )
```

time: 495 us -> 249 us (0.50)
  blocking collectives: 256 us -> 102 us
  waiting for transfers between devices: 144 us -> 45 us
  Pallas kernels: 0 us -> 39.4 us
  other arithmetic: 40.7 us -> 1.7 us
  matrix products: 26.3 us -> 0 us
  local copies, waits for them, and re-layouts: 11 us -> 33.3 us
  starting transfers between devices: 0.12 us -> 12.9 us
    psum x4 -> x0, blocking collectives: 256 us -> none  [the longest x2 128 us: body(): lax.psum(jnp.sum(exp_teacher * col_scale[None, :], axis=1), ('dp', 'proto'))]
    all_to_all x0 -> x4, blocking collectives: none -> 102 us  [exchange(): return lax.all_to_all(x, CHIPS, 0, 0)]
    psum x1 -> x0, waiting for transfers between devices: 80.6 us -> none  [body(): summed = lax.psum(local_terms, ('dp', 'proto'))]
    all_gather x2 -> x1, waiting for transfers between devices: 63.7 us -> 18.7 us  [body(): s_own = lax.all_gather(s_bot, CHIPS, axis=0, tiled=True)]
    pallas_call x0 -> x10, Pallas kernels: none -> 39.4 us  [call(): pl.pallas_call(kernel, out_shape=out_shape, in_specs=[VM] * len(operands)...]
    dot_general x5 -> x0, matrix products: 26.3 us -> none  [the longest x1 8.42 us: body(): jnp.dot(s_all, s_cols, preferred_element_type=jnp.float32) / student_temp]
    unnamed x12 -> x32, local copies, waits for them, and re-layouts: 11 us -> 33.3 us
    reduce_sum x9 -> x3, other arithmetic: 22.9 us -> 1.7 us  [row_sums(): mine = jnp.sum(exchange(x), axis=0)]
  transfers between devices with their start and end apart: 3 -> 9, of which waited for: 2 -> 5; matrix products, arithmetic and copies ran while one was open for 7% -> 0% of each run, Pallas kernels for 0% -> 9%
where the time goes in v1:
time: 249 us; the launch traced here: 248 us
  blocking collectives  102 us (41%)
  waiting for transfers between devices  45 us (18%)
  Pallas kernels  39.4 us (16%)
  local copies, waits for them, and re-layouts  33.3 us (13%)
  between operations  14.2 us (6%)
  starting transfers between devices  12.9 us (5%)
    all_to_all x4, blocking collectives, exchange(): return lax.all_to_all(x, CHIPS, 0, 0)  102 us
    pallas_call x10, Pallas kernels, call(): pl.pallas_call(kernel, out_shape=out_shape, in_specs=[VM] * len(operands)...  39.4 us
    unnamed x32, local copies, waits for them, and re-layouts  33.3 us
    all_to_all x1, waiting for transfers between devices, exchange(): return lax.all_to_all(x, CHIPS, 0, 0)  19.5 us
    all_gather x1, waiting for transfers between devices, body(): s_own = lax.all_gather(s_bot, CHIPS, axis=0, tiled=True)  18.7 us
    all_to_all x1, starting transfers between devices, exchange(): return lax.all_to_all(x, CHIPS, 0, 0)  11.6 us
    ppermute x7, waiting for transfers between devices, swap(): return lax.ppermute(x, 'c', SWAP)  6.02 us
  transfers between devices with their start and end apart: 9, of which 5 were waited for; matrix products, arithmetic and copies ran while one was open for 0% of the time, Pallas kernels for 9%

profile of v1, /device:TPU:0, one launch (start us, length us, event | category | flops | bytes accessed | tf_op | source)
XLA Modules:
  0.0 248.1 jit_solution(9013866798778627611)
XLA Ops:
  7.2 0.7 copy-done.14
  7.9 0.7 shard_map.76
  8.6 1.4 copy-done.9
  10.0 0.9 copy-done.13
  10.9 1.5 shard_map.77
  12.4 11.6 %all-to-all-start = ((bf16[64,24,384]{2,1,0:T(8,128)(2,1)}), bf16[64,24,384]{2,1,0:T(8,128)(2,1)S(1)}, u32[]{:S(2)}, u32[]{:S(2)}) async-start(bf16[64,24,384]{2,1,0:T(8,128)(2,1)} %shard_map.77), calls=%async_computation | async-start | bytes 2359296 | tf_op jit(solution)/shard_map/all_to_all | solution.py:237
  24.8 19.5 %all-to-all-done = bf16[64,24,384]{2,1,0:T(8,128)(2,1)S(1)} async-done(((bf16[64,24,384]{2,1,0:T(8,128)(2,1)}), bf16[64,24,384]{2,1,0:T(8,128)(2,1)S(1)}, u32[]{:S(2)}, u32[]{:S(2)}) %all-to-all-start) | async-done | bytes 1179680 | tf_op jit(solution)/shard_map/all_to_all | solution.py:237
  44.4 2.8 %collective-permute-done.r_2_ = bf16[1536,384]{1,0:T(8,128)(2,1)S(1)} collective-permute-done((bf16[1536,384]{1,0:T(8,128)(2,1)S(1)}, bf16[1536,384]{1,0:T(8,128)(2,1)S(1)}, u32[]{:S(2)}, u32[]{:S(2)}) %collective-permute-start) | collective-permute-done | bytes 1179680 | tf_op jit(solution)/shard_map/ppermute | solution.py:234
  47.2 5.6 %shard_map.78 = (f32[1024,3072]{1,0:T(8,128)S(1)}, f32[64,8,384]{2,1,0:T(8,128)S(1)}) custom-call(bf16[384,1024]{1,0:T(8,128)(2,1)S(1)} %copy-done.10, bf16[1536,384]{1,0:T(8,128)(2,1)S(1)} %bitcast.4, bf16[1536,384]{1,0:T(8,128)(2,1)S(1)} %collective-permute-done.r_2_), custom_call_target="tpu_custom_call" | custom-call | tf_op jit(solution)/shard_map/pallas_call | solution.py:29
  52.8 4.5 %copy-done = f32[1024,3072]{1,0:T(8,128)} copy-done((f32[1024,3072]{1,0:T(8,128)}, f32[1024,3072]{1,0:T(8,128)S(1)}, u32[]{:S(2)}) %copy-start) | copy-done | bytes 12582936
  57.3 21.6 %all_to_all.25 = f32[64,8,384]{2,1,0:T(8,128)S(1)} all-to-all(f32[64,8,384]{2,1,0:T(8,128)S(1)} %get-tuple-element.23), channel_id=1, replica_groups=mesh['z'=4,'y'=4,'x'=4,'c'=2] {'z','y','x'}, dimensions={0} | all-to-all | bytes 1572864 | tf_op jit(solution)/shard_map/all_to_all | solution.py:237
  79.0 18.7 %all-gather.2.cloned.1.call-done.own_ref = bf16[1536,384]{1,0:T(8,128)(2,1)} async-done(((bf16[24,384]{1,0:T(8,128)(2,1)}), bf16[1536,384]{1,0:T(8,128)(2,1)}) %all-gather.2.cloned.1.call-update) | async-done | bytes 1179664 | tf_op jit(solution)/shard_map/all_gather | solution.py:244
  98.3 2.0 collective-permute-done.2.r_2_
  100.3 4.6 %copy-done.1 = f32[1024,3072]{1,0:T(8,128)S(1)} copy-done((f32[1024,3072]{1,0:T(8,128)S(1)}, f32[1024,3072]{1,0:T(8,128)}, u32[]{:S(2)}) %copy-start.1) | copy-done | bytes 12582936
  104.8 4.0 %shard_map.80 = (f32[64,8,384]{2,1,0:T(8,128)S(1)}, f32[1024,1]{1,0:T(8,128)}) custom-call(f32[1024,3072]{1,0:T(8,128)S(1)} %copy-done.1, f32[8,384]{1,0:T(8,128)S(1)} %reduce_sum.27.r_1_, f32[8,384]{1,0:T(8,128)S(1)} %collective-permute-done.2.r_2_), custom_call_target="tpu_custom_call" | custom-call | tf_op jit(solution)/shard_map/pallas_call | solution.py:29
  108.9 23.0 %all_to_all.26 = f32[64,8,384]{2,1,0:T(8,128)S(1)} all-to-all(f32[64,8,384]{2,1,0:T(8,128)S(1)} %get-tuple-element.27), channel_id=1, replica_groups=mesh['z'=4,'y'=4,'x'=4,'c'=2] {'z','y','x'}, dimensions={0} | all-to-all | bytes 1572864 | tf_op jit(solution)/shard_map/all_to_all | solution.py:237
  132.0 1.1 copy-done.7
  133.2 4.5 %shard_map.79 = (f32[1024,3072]{1,0:T(8,128)S(1)}, bf16[384,1024]{1,0:T(8,128)(2,1)S(1)}, f32[8,384]{1,0:T(8,128)S(1)}) custom-call(bf16[384,1024]{1,0:T(8,128)(2,1)S(1)} %copy-done.7, bf16[1536,384]{1,0:T(8,128)(2,1)S(1)} %copy-done.6, bf16[1536,384]{1,0:T(8,128)(2,1)S(1)} %collective-permute-done.1.other_ref), custom_call_target="tpu_custom_call" | custom-call | tf_op jit(solution)/shard_map/pallas_call | solution.py:29
  137.6 4.5 %copy-done.4 = f32[1024,3072]{1,0:T(8,128)} copy-done((f32[1024,3072]{1,0:T(8,128)}, f32[1024,3072]{1,0:T(8,128)S(1)}, u32[]{:S(2)}) %copy-start.4) | copy-done | bytes 12582936
  142.2 4.6 %copy-done.2 = f32[1024,3072]{1,0:T(8,128)S(1)} copy-done((f32[1024,3072]{1,0:T(8,128)S(1)}, f32[1024,3072]{1,0:T(8,128)}, u32[]{:S(2)}) %copy-start.2) | copy-done | bytes 12582936
  146.7 3.2 %shard_map.81 = (f32[64,16,384]{2,1,0:T(8,128)S(1)}, f32[1024,1]{1,0:T(8,128)S(1)}) custom-call(f32[1024,3072]{1,0:T(8,128)S(1)} %copy-done.2, f32[8,384]{1,0:T(8,128)S(1)} %reduce_sum.28.r_1_, f32[8,384]{1,0:T(8,128)S(1)} %collective-permute-done.3.r_2_, f32[8,384]{1,0:T(8,128)S(1)} %get-tuple-element.28.r_3_), custom_call_target="tpu_custom_call" | custom-call | tf_op jit(solution)/shard_map/pallas_call | solution.py:29
  150.0 0.8 copy-done.11
  150.8 29.9 %all_to_all.27 = f32[64,16,384]{2,1,0:T(8,128)} all-to-all(f32[64,16,384]{2,1,0:T(8,128)S(1)} %get-tuple-element.31), channel_id=1, replica_groups=mesh['z'=4,'y'=4,'x'=4,'c'=2] {'z','y','x'}, dimensions={0} | all-to-all | bytes 3145728 | tf_op jit(solution)/shard_map/all_to_all | solution.py:237
  180.6 1.5 reduce_sum.29.mine_ref
  182.3 1.2 collective-permute-done.4.theirs_ref
  183.4 4.6 %copy-done.3 = f32[1024,3072]{1,0:T(8,128)S(1)} copy-done((f32[1024,3072]{1,0:T(8,128)S(1)}, f32[1024,3072]{1,0:T(8,128)}, u32[]{:S(2)}) %copy-start.3) | copy-done | bytes 12582936
  188.0 4.6 %copy-done.5 = f32[1024,3072]{1,0:T(8,128)S(1)} copy-done((f32[1024,3072]{1,0:T(8,128)S(1)}, f32[1024,3072]{1,0:T(8,128)}, u32[]{:S(2)}) %copy-start.5) | copy-done | bytes 12582936
  192.6 1.0 copy-done.12
  193.6 10.9 %shard_map.82 = (bf16[1024,3072]{1,0:T(8,128)(2,1)S(1)}, f32[1536,384]{1,0:T(8,128)S(1)}, f32[8,128]{1,0:T(8,128)S(1)}) custom-call(f32[1024,3072]{1,0:T(8,128)S(1)} %copy-done.3, f32[1024,3072]{1,0:T(8,128)S(1)} %copy-done.5, f32[1024,1]{1,0:T(8,128)S(1)} %copy-done.12, bf16[384,1024]{1,0:T(8,128)(2,1)S(1)} %get-tuple-element.30.cols_ref, ...), custom_call_target="tpu_custom_call" | custom-call | tf_op jit(solution)/shard_map/pallas_call | solution.py:29
  205.2 7.5 %shard_map.83 = (f32[384,1024]{1,0:T(8,128)}, f32[1536,384]{1,0:T(8,128)S(1)}) custom-call(bf16[1024,3072]{1,0:T(8,128)(2,1)S(1)} %get-tuple-element.32.g_ref, bf16[384,1024]{1,0:T(8,128)(2,1)S(1)} %get-tuple-element.30.cols_ref, bf16[384,1024]{1,0:T(8,128)(2,1)S(1)} %copy-done.8, bf16[1536,384]{1,0:T(8,128)(2,1)S(1)} %copy-done.6, ...), custom_call_target="tpu_custom_call" | custom-call | tf_op jit(solution)/shard_map/pallas_call | solution.py:29
  213.2 27.2 %all_to_all.28.r_0_ = bf16[64,80,128]{2,1,0:T(8,128)(2,1)S(1)} all-to-all(bf16[64,80,128]{2,1,0:T(8,128)(2,1)S(1)} %shard_map.84), channel_id=1, replica_groups=mesh['z'=4,'y'=4,'x'=4,'c'=2] {'z','y','x'}, dimensions={0} | all-to-all | bytes 2621440 | tf_op jit(solution)/shard_map/all_to_all | solution.py:237
  240.4 0.9 shard_map.85
  (36 shorter events, 2.7 us)
Async XLA Ops:
  7.2 0.7 copy-start.14
  8.6 1.4 copy-start.9
  10.0 0.9 copy-start.13
  12.4 34.8 %copy-start.10 = (bf16[384,1024]{1,0:T(8,128)(2,1)S(1)}, bf16[384,1024]{1,0:T(8,128)(2,1)}, u32[]{:S(2)}) copy-start(bf16[384,1024]{1,0:T(8,128)(2,1)} %r_0_.1) | copy-start | bytes 2359300
  12.4 31.9 %all-to-all-start = ((bf16[64,24,384]{2,1,0:T(8,128)(2,1)}), bf16[64,24,384]{2,1,0:T(8,128)(2,1)S(1)}, u32[]{:S(2)}, u32[]{:S(2)}) async-start(bf16[64,24,384]{2,1,0:T(8,128)(2,1)} %shard_map.77), calls=%async_computation | async-start | bytes 2359296 | tf_op jit(solution)/shard_map/all_to_all | solution.py:237
  24.1 73.7 %all-gather.2.cloned.1.call-start = ((), (), s32[]{:S(2)}) async-start(), calls=%async_computation.5 | async-start | bytes 1198080 | tf_op jit(solution)/shard_map/all_gather | solution.py:244
  44.4 2.8 %collective-permute-start = (bf16[1536,384]{1,0:T(8,128)(2,1)S(1)}, bf16[1536,384]{1,0:T(8,128)(2,1)S(1)}, u32[]{:S(2)}, u32[]{:S(2)}) collective-permute-start(bf16[1536,384]{1,0:T(8,128)(2,1)S(1)} %bitcast.3), channel_id=1, source_target_pairs={{0,1},{1,0},{2,3},{3,2},{4,5},{5,4},{6,7},{7,6},{8,9},{9,8},{10,11... | collective-permute-start | bytes 3538952 | tf_op jit(solution)/shard_map/ppermute | solution.py:234
  52.8 4.5 %copy-start = (f32[1024,3072]{1,0:T(8,128)}, f32[1024,3072]{1,0:T(8,128)S(1)}, u32[]{:S(2)}) copy-start(f32[1024,3072]{1,0:T(8,128)S(1)} %get-tuple-element.22.r_0_.e_ref) | copy-start | bytes 37748740
  97.8 34.2 %collective-permute-start.1 = (bf16[1536,384]{1,0:T(8,128)(2,1)}, bf16[1536,384]{1,0:T(8,128)(2,1)S(1)}, u32[]{:S(2)}, u32[]{:S(2)}) collective-permute-start(bf16[1536,384]{1,0:T(8,128)(2,1)} %all-gather.2.cloned.1.call-done.own_ref), channel_id=1, source_target_pairs={{0,1},{1,0},{2,3},{3,2},{4,5},{5,4},{6,7},{7,6},{8,9},{9,8},{10,11... | collective-permute-start | bytes 3538952 | tf_op jit(solution)/shard_map/ppermute | solution.py:234
  97.8 2.5 %collective-permute-start.2 = (f32[8,384]{1,0:T(8,128)S(1)}, f32[8,384]{1,0:T(8,128)S(1)}, u32[]{:S(2)}, u32[]{:S(2)}) collective-permute-start(f32[8,384]{1,0:T(8,128)S(1)} %reduce_sum.27.r_1_), channel_id=1, source_target_pairs={{0,1},{1,0},{2,3},{3,2},{4,5},{5,4},{6,7},{7,6},{8,9},{9,8},{10,11... | collective-permute-start | bytes 36872 | tf_op jit(solution)/shard_map/ppermute | solution.py:234
  100.3 4.6 %copy-start.1 = (f32[1024,3072]{1,0:T(8,128)S(1)}, f32[1024,3072]{1,0:T(8,128)}, u32[]{:S(2)}) copy-start(f32[1024,3072]{1,0:T(8,128)} %copy-done) | copy-start | bytes 37748740
  108.9 23.1 %copy-start.6 = (bf16[1536,384]{1,0:T(8,128)(2,1)S(1)}, bf16[1536,384]{1,0:T(8,128)(2,1)}, u32[]{:S(2)}) copy-start(bf16[1536,384]{1,0:T(8,128)(2,1)} %all-gather.2.cloned.1.call-done.own_ref) | copy-start | bytes 3538948
  131.9 10.3 %collective-permute-start.3 = (f32[8,384]{1,0:T(8,128)S(1)}, f32[8,384]{1,0:T(8,128)S(1)}, u32[]{:S(2)}, u32[]{:S(2)}) collective-permute-start(f32[8,384]{1,0:T(8,128)S(1)} %reduce_sum.28.r_1_), channel_id=1, source_target_pairs={{0,1},{1,0},{2,3},{3,2},{4,5},{5,4},{6,7},{7,6},{8,9},{9,8},{10,11... | collective-permute-start | bytes 36872 | tf_op jit(solution)/shard_map/ppermute | solution.py:234
  132.0 1.1 copy-start.7
  137.6 4.5 %copy-start.4 = (f32[1024,3072]{1,0:T(8,128)}, f32[1024,3072]{1,0:T(8,128)S(1)}, u32[]{:S(2)}) copy-start(f32[1024,3072]{1,0:T(8,128)S(1)} %get-tuple-element.25.lg_ref) | copy-start | bytes 37748740
  142.2 4.6 %copy-start.2 = (f32[1024,3072]{1,0:T(8,128)S(1)}, f32[1024,3072]{1,0:T(8,128)}, u32[]{:S(2)}) copy-start(f32[1024,3072]{1,0:T(8,128)} %copy-done) | copy-start | bytes 37748740
  150.0 0.8 copy-start.11
  182.2 1.3 collective-permute-start.4
  183.4 4.6 %copy-start.3 = (f32[1024,3072]{1,0:T(8,128)S(1)}, f32[1024,3072]{1,0:T(8,128)}, u32[]{:S(2)}) copy-start(f32[1024,3072]{1,0:T(8,128)} %copy-done) | copy-start | bytes 37748740
  188.0 4.6 %copy-start.5 = (f32[1024,3072]{1,0:T(8,128)S(1)}, f32[1024,3072]{1,0:T(8,128)}, u32[]{:S(2)}) copy-start(f32[1024,3072]{1,0:T(8,128)} %copy-done.4) | copy-start | bytes 37748740
  192.6 1.0 copy-start.12
  193.6 11.5 %copy-start.8 = (bf16[384,1024]{1,0:T(8,128)(2,1)S(1)}, bf16[384,1024]{1,0:T(8,128)(2,1)}, u32[]{:S(2)}) copy-start(bf16[384,1024]{1,0:T(8,128)(2,1)} %w_ref.3) | copy-start | bytes 2359300
  204.6 8.1 %collective-permute-start.5 = (f32[1536,384]{1,0:T(8,128)S(1)}, f32[1536,384]{1,0:T(8,128)S(1)}, u32[]{:S(2)}, u32[]{:S(2)}) collective-permute-start(f32[1536,384]{1,0:T(8,128)S(1)} %get-tuple-element.34), channel_id=1, source_target_pairs={{0,1},{1,0},{2,3},{3,2},{4,5},{5,4},{6,7},{7,6},{8,9},{9,8},{10,11... | collective-permute-start | bytes 7077896 | tf_op jit(solution)/shard_map/ppermute | solution.py:234
  204.8 7.9 %collective-permute-start.6 = (f32[8,128]{1,0:T(8,128)S(1)}, f32[8,128]{1,0:T(8,128)S(1)}, u32[]{:S(2)}, u32[]{:S(2)}) collective-permute-start(f32[8,128]{1,0:T(8,128)S(1)} %get-tuple-element.35.loss_a), channel_id=1, source_target_pairs={{0,1},{1,0},{2,3},{3,2},{4,5},{5,4},{6,7},{7,6},{8,9},{9,8},{10,11... | collective-permute-start | bytes 12296 | tf_op jit(solution)/shard_map/ppermute | solution.py:234
  213.2 27.2 %copy-start.15 = (bf16[24,384]{1,0:T(8,128)(2,1)S(1)}, bf16[24,384]{1,0:T(8,128)(2,1)}, u32[]{:S(2)}) copy-start(bf16[24,384]{1,0:T(8,128)(2,1)} %r_1_.1) | copy-start | bytes 55300
Sparse Core Ops, SparseCore 0:
  28.4 69.3 all-gather.1

commit v2 on v1

v2 whole, which is shorter than its diff:
```python
import functools

import jax
import jax.numpy as jnp
from jax import lax
from jax.experimental import pallas as pl
from jax.experimental.pallas import tpu as pltpu
from jax.sharding import Mesh
from jax.sharding import PartitionSpec as P

ITERS = 3
EPS = 1e-06
teacher_temp = 0.07
student_temp = 0.1

ALL = ("z", "y", "x", "c")
CHIPS = ("z", "y", "x")
SWAP = [(0, 1), (1, 0)]
F32 = jnp.float32
BF16 = jnp.bfloat16
MB = 1024 * 1024
NT = (((1,), (1,)), ((), ()))
VM = pl.BlockSpec(memory_space=pltpu.VMEM)
CHUNK = 256
BLOCK = 128
ANY = pl.BlockSpec(memory_space=pltpu.HBM)


def call(kernel, out_shape, operands, vmem, scratch=(), in_any=(), out_any=(), flops=0, nbytes=0):
    many = isinstance(out_shape, (tuple, list))
    outs = out_shape if many else (out_shape,)
    specs = tuple(ANY if i in out_any else VM for i in range(len(outs)))
    return pl.pallas_call(
        kernel,
        out_shape=out_shape,
        in_specs=[ANY if i in in_any else VM for i in range(len(operands))],
        out_specs=specs if many else specs[0],
        scratch_shapes=list(scratch),
        compiler_params=pltpu.CompilerParams(vmem_limit_bytes=vmem * MB),
        cost_estimate=pl.CostEstimate(flops=flops, bytes_accessed=nbytes, transcendentals=0),
    )(*operands)


def fold(row):
    width = row.shape[1] // 8
    return jnp.concatenate([row[:, j * width : (j + 1) * width] for j in range(8)], axis=0)


def spread(piece, ref):
    piece = piece.astype(ref.dtype)
    for i in range(ref.shape[0]):
        ref[i] = piece


def flat(block):
    return jnp.concatenate([block[j : j + 1, :] for j in range(8)], axis=1)


def total_row(mine, theirs):
    return flat(mine + jnp.concatenate([theirs[4:8, :], theirs[0:4, :]], axis=0))


def columns(w_block):
    wide = w_block.astype(F32)
    inv = lax.rsqrt(jnp.sum(wide * wide, axis=0, keepdims=True) + EPS)
    return wide * inv, inv


def rows_kernel(s_ref, hid_ref, proj_ref, send_ref, s_buf, hid_buf, proj_buf, sem):
    parts = proj_buf.shape[0]
    depth = proj_buf.shape[1]
    first = pltpu.make_async_copy(s_ref, s_buf, sem.at[0])
    second = pltpu.make_async_copy(hid_ref, hid_buf, sem.at[1])
    copies = [
        pltpu.make_async_copy(proj_ref.at[pl.ds(i * depth, depth), :], proj_buf.at[i], sem.at[2 + i])
        for i in range(parts)
    ]
    first.start()
    second.start()
    for copy in copies:
        copy.start()
    first.wait()
    wide = s_buf[...].astype(F32)
    unit = wide * lax.rsqrt(jnp.sum(wide * wide, axis=1, keepdims=True) + EPS)
    second.wait()
    t_hid = jnp.zeros((hid_buf.shape[0], proj_buf.shape[2]), F32)
    for i, copy in enumerate(copies):
        copy.wait()
        t_hid = t_hid + jnp.dot(
            hid_buf[:, i * depth : (i + 1) * depth], proj_buf[i], preferred_element_type=F32
        )
    t_bot = t_hid * lax.rsqrt(jnp.sum(t_hid * t_hid, axis=1, keepdims=True) + EPS)
    spread(jnp.concatenate([t_bot, unit], axis=1), send_ref)


def sum_kernel(got_ref, out_ref):
    out_ref[...] = jnp.sum(got_ref[...].astype(F32), axis=0)


def own_kernel(tw_ref, sw_ref, rows_ref, e_ref, lg_ref, t_lhs, s_lhs, s_cols, sums_ref, part_ref):
    part_ref[...] = jnp.zeros_like(part_ref)

    def step(j, _):
        at = pl.ds(pl.multiple_of(j * CHUNK, CHUNK), CHUNK)
        t_lhs[at, :] = columns(tw_ref[:, at])[0].T.astype(BF16)
        unit = columns(sw_ref[:, at])[0]
        s_cols[:, at] = unit.astype(BF16)
        s_lhs[at, :] = unit.T.astype(BF16)
        sums_ref[at, :] = products(at, t_lhs, s_lhs, rows_ref, e_ref, lg_ref, part_ref)
        return 0

    lax.fori_loop(0, tw_ref.shape[1] // CHUNK, step, 0)


def products(at, t_lhs, s_lhs, rows_ref, e_ref, lg_ref, part_ref):
    bot = t_lhs.shape[1]
    expo = jnp.exp(
        lax.dot_general(t_lhs[at, :], rows_ref[:, :bot], NT, preferred_element_type=F32) * (1.0 / teacher_temp)
    )
    e_ref[at, :] = expo
    logits = lax.dot_general(s_lhs[at, :], rows_ref[:, bot:], NT, preferred_element_type=F32) * (1.0 / student_temp)
    lg_ref[at, :] = logits
    part_ref[...] += jnp.sum(jnp.exp(logits).reshape(CHUNK // 8, 8, logits.shape[1]), axis=0)
    return jnp.sum(expo, axis=1, keepdims=True)


def other_kernel(
    total_cols, t_lhs, s_lhs, rows_ref, e_own, sums_ref, part_own, e_ref, lg_ref, out_ref, part, acc
):
    half = rows_ref.shape[0]
    part[...] = jnp.zeros_like(part)
    acc[...] = jnp.zeros_like(acc)

    def step(j, _):
        at = pl.ds(pl.multiple_of(j * CHUNK, CHUNK), CHUNK)
        sums = sums_ref[at, :] + products(at, t_lhs, s_lhs, rows_ref, e_ref, lg_ref, part)
        scale = 1.0 / (total_cols * sums)
        row_pass(e_own.at[at, :], scale, acc.at[:, :half])
        row_pass(e_ref.at[at, :], scale, acc.at[:, half:])
        return 0

    lax.fori_loop(0, t_lhs.shape[0] // CHUNK, step, 0)
    parts = jnp.concatenate([part_own[...], part[...]], axis=1)
    row = fold(jnp.sum(acc[...], axis=0, keepdims=True))
    spread(jnp.concatenate([row, fold(jnp.sum(parts, axis=0, keepdims=True))], axis=0), out_ref)


def row_pass(block_ref, scale, acc):
    rows, n = block_ref.shape
    scale = scale.reshape(rows // 8, 8, 1)
    for start in range(0, n, 512):
        lanes = slice(start, start + 512)
        acc[:, lanes] += jnp.sum(block_ref[:, lanes].reshape(rows // 8, 8, 512) * scale, axis=0)


def pass_kernel(total_cols, images, own_ref, other_ref, mine_ref, theirs_ref, out_ref, cs_ref, weight, acc):
    total = total_row(mine_ref[0:8, :], theirs_ref[0:8, :])
    weight[...] = jnp.broadcast_to(1.0 / (images * total), weight.shape)
    acc[...] = jnp.zeros_like(acc)
    protos, half = own_ref.shape

    def step(j, _):
        at = pl.ds(pl.multiple_of(j * BLOCK, BLOCK), BLOCK)
        sums = jnp.zeros((BLOCK, 1), F32)
        for ref, start in ((own_ref, 0), (other_ref, half)):
            weighted = ref[at, :].reshape(BLOCK // 8, 8, half) * weight[:, start : start + half][None]
            sums = sums + jnp.sum(weighted.reshape(BLOCK, half), axis=1, keepdims=True)
        scale = 1.0 / (total_cols * sums)
        cs_ref[at, :] = scale
        row_pass(own_ref.at[at, :], scale, acc.at[:, :half])
        row_pass(other_ref.at[at, :], scale, acc.at[:, half:])
        return 0

    lax.fori_loop(0, protos // BLOCK, step, 0)
    spread(fold(jnp.sum(acc[...], axis=0, keepdims=True)), out_ref)


STRIP = 32
LANES = 768


def grad_kernel(
    devices, e_own, e_other, lg_own, lg_other, cs_ref, cols_ref, first_a, first_b, last_a, last_b,
    g_own, g_other, other_ref, loss_ref, rows, acc
):
    protos, half = e_own.shape
    n = 2 * half
    part = total_row(first_a[8:16, :], first_b[8:16, :])
    row = total_row(last_a[...], last_b[...])
    rows[0:8, :] = jnp.broadcast_to((1.0 / student_temp) / part, (8, n))
    rows[8:16, :] = jnp.broadcast_to((1.0 / student_temp) / row, (8, n))
    acc[...] = jnp.zeros_like(acc)
    fold_rows = (STRIP // 8, 8, LANES)

    def step(k, _):
        at = pl.ds(pl.multiple_of(k * STRIP, STRIP), STRIP)
        scale = cs_ref[at, :]
        for e_ref, lg_ref, g_ref, offset in ((e_own, lg_own, g_own, 0), (e_other, lg_other, g_other, half)):
            for start in range(0, half, LANES):
                lanes = slice(start, start + LANES)
                wide = slice(offset + start, offset + start + LANES)
                logits = lg_ref[at, lanes]
                scaled = e_ref[at, lanes] * scale
                acc[:, wide] += jnp.sum((scaled * logits).reshape(fold_rows), axis=0)
                powers = jnp.exp(logits).reshape(fold_rows) * rows[0:8, wide][None]
                target = scaled.reshape(fold_rows) * rows[8:16, wide][None]
                g_ref[at, lanes] = (powers - target).reshape(STRIP, LANES).astype(BF16)
        return 0

    lax.fori_loop(0, protos // STRIP, step, 0)
    terms = jnp.log(part) * (1.0 / devices) - jnp.sum(acc[...], axis=0, keepdims=True) / row
    pieces = fold(terms)
    loss_ref[...] = sum(pieces[:, 128 * k : 128 * (k + 1)] for k in range(n // 1024))
    bottleneck(cols_ref, g_other, other_ref)


def bottleneck(cols_ref, g_ref, out_ref):
    for i in range(out_ref.shape[0] // CHUNK):
        at = slice(i * CHUNK, (i + 1) * CHUNK)
        block = jnp.dot(cols_ref[...], g_ref[:, at], preferred_element_type=F32)
        out_ref[at, :] = block.T


def protos_kernel(g_own, g_other, cols_ref, w_ref, own_ref, other_ref, dp_ref, db_ref):
    bot = w_ref.shape[0]
    bottleneck(cols_ref, g_own, db_ref)

    def step(j, _):
        at = pl.ds(pl.multiple_of(j * CHUNK, CHUNK), CHUNK)
        d_unit = jnp.dot(g_own[at, :], own_ref[:, bot:], preferred_element_type=F32)
        d_unit = d_unit + jnp.dot(g_other[at, :], other_ref[:, bot:], preferred_element_type=F32)
        d_unit = d_unit.T
        unit, inv = columns(w_ref[:, at])
        dp_ref[:, at] = inv * (d_unit - unit * jnp.sum(unit * d_unit, axis=0, keepdims=True))
        return 0

    lax.fori_loop(0, w_ref.shape[1] // CHUNK, step, 0)


def pack_kernel(mine_ref, theirs_ref, loss_a, loss_b, out_ref):
    total = jnp.sum(jnp.sum(loss_a[...] + loss_b[...], axis=0, keepdims=True), axis=1, keepdims=True)
    high = total.astype(BF16).astype(F32)
    mid = (total - high).astype(BF16).astype(F32)
    low = total - high - mid
    row = lax.broadcasted_iota(jnp.int32, (8, 128), 0)
    tail = jnp.where(row == 0, high, jnp.where(row == 1, mid, jnp.where(row == 2, low, 0.0)))
    tail = tail.astype(BF16)

    def step(i, _):
        at = pl.ds(pl.multiple_of(i * 24, 8), 24)
        block = mine_ref[at, :] + theirs_ref[at, :]
        for k in range(3):
            out_ref[i, 24 * k : 24 * (k + 1), :] = block[:, 128 * k : 128 * (k + 1)].astype(BF16)
        out_ref[i, 72:80, :] = tail
        return 0

    lax.fori_loop(0, out_ref.shape[0], step, 0, unroll=4)


def finish_kernel(images, got_ref, hid_ref, ds_ref, loss_ref):
    total = jnp.sum(got_ref[...].astype(F32), axis=0)
    d_bot = jnp.concatenate([total[24 * k : 24 * (k + 1), :] for k in range(3)], axis=1)
    wide = hid_ref[...].astype(F32)
    inv = lax.rsqrt(jnp.sum(wide * wide, axis=1, keepdims=True) + EPS)
    unit = wide * inv
    ds_ref[...] = inv * (d_bot - unit * jnp.sum(unit * d_bot, axis=1, keepdims=True))
    loss_ref[...] = (total[72:73, :] + total[73:74, :] + total[74:75, :]) * (1.0 / images)


def body(teacher_hidden, teacher_proj, student_hidden, teacher_protos, student_protos):
    chips = lax.axis_size(CHIPS)
    rows_dev, bot = student_hidden.shape
    half = rows_dev * chips
    images = 2 * half
    protos = teacher_protos.shape[1]
    total_cols = protos * lax.axis_size(ALL)
    sds = jax.ShapeDtypeStruct

    def swap(x):
        return lax.ppermute(x, "c", SWAP)

    def exchange(x):
        return lax.all_to_all(x, CHIPS, 0, 0)

    def row_sums(x, rows):
        mine = call(sum_kernel, sds((rows, images // 8), F32), (exchange(x),), 2)
        return mine, swap(mine)

    both = call(
        rows_kernel,
        sds((chips, rows_dev, 2 * bot), BF16),
        (student_hidden, teacher_hidden, teacher_proj),
        60,
        [
            pltpu.VMEM(student_hidden.shape, BF16),
            pltpu.VMEM(teacher_hidden.shape, BF16),
            pltpu.VMEM((4, teacher_proj.shape[0] // 4, bot), BF16),
            pltpu.SemaphoreType.DMA((6,)),
        ],
        in_any=(0, 1, 2),
    )
    own = exchange(both).reshape(half, 2 * bot)
    other = swap(own)

    matrix = sds((protos, half), F32)
    lhs = sds((protos, bot), BF16)
    column = sds((protos, 1), F32)
    part8 = sds((8, half), F32)
    fold8 = pltpu.VMEM((8, images), F32)
    e_own, lg_own, t_lhs, s_lhs, s_cols, sums, part = call(
        own_kernel,
        (matrix, matrix, lhs, lhs, sds((bot, protos), BF16), column, part8),
        (teacher_protos, student_protos, own),
        8,
    )
    e_other, lg_other, sent = call(
        functools.partial(other_kernel, total_cols),
        (matrix, matrix, sds((chips, 16, images // 8), BF16)),
        (t_lhs, s_lhs, other, e_own, sums, part),
        8,
        [pltpu.VMEM((8, half), F32), fold8],
    )
    first = row_sums(sent, 16)
    sums = first
    for sweep in range(1, ITERS):
        sent, col_scale = call(
            functools.partial(pass_kernel, total_cols, images),
            (sds((chips, 8, images // 8), BF16), column),
            (e_own, e_other) + sums,
            4,
            [fold8, fold8],
        )
        sums = row_sums(sent, 8)
    g_own, g_other, d_other, loss_mine = call(
        functools.partial(grad_kernel, 2 * chips),
        (sds((protos, half), BF16), sds((protos, half), BF16), sds((half, bot), F32), sds((8, 128), F32)),
        (e_own, e_other, lg_own, lg_other, col_scale, s_cols) + first + sums,
        4,
        [pltpu.VMEM((16, images), F32), fold8],
    )
    d_theirs = swap(d_other)
    loss_theirs = swap(loss_mine)
    d_protos, d_mine = call(
        protos_kernel,
        (sds((bot, protos), F32), sds((half, bot), F32)),
        (g_own, g_other, s_cols, student_protos, own, other),
        12,
    )
    packed = call(
        pack_kernel,
        sds((chips, 80, 128), BF16),
        (d_mine, d_theirs, loss_mine, loss_theirs),
        4,
    )
    got = exchange(packed)
    d_student, loss = call(
        functools.partial(finish_kernel, images),
        (sds((rows_dev, bot), F32), sds((1, 128), F32)),
        (got, student_hidden),
        4,
    )
    return loss[0, 0], d_student, d_protos


def solution(mesh):
    grid = Mesh(mesh.devices.reshape(4, 4, 4, 2), ALL)
    return jax.shard_map(
        body,
        mesh=grid,
        in_specs=(P(ALL, None), P(), P(ALL, None), P(None, ALL), P(None, ALL)),
        out_specs=(P(), P(ALL, None), P(None, ALL)),
        check_vma=False,
    )
```

time: 249 us -> 166 us (0.67)
  waiting for transfers between devices: 45 us -> 3.52 us
  local copies, waits for them, and re-layouts: 33.3 us -> 0.02 us
  blocking collectives: 102 us -> 127 us
  between operations: 14.2 us -> 0.74 us
  starting transfers between devices: 12.9 us -> 0.83 us
  Pallas kernels: 39.4 us -> 33.7 us
    unnamed x32 -> x6, local copies, waits for them, and re-layouts: 33.3 us -> 0.02 us
    all_to_all x4 -> x5, blocking collectives: 102 us -> 127 us  [exchange(): return lax.all_to_all(x, CHIPS, 0, 0)]
    all_to_all x1 -> x0, waiting for transfers between devices: 19.5 us -> none  [exchange(): return lax.all_to_all(x, CHIPS, 0, 0)]
    all_gather x1 -> x0, waiting for transfers between devices: 18.7 us -> none  [body(): s_own = lax.all_gather(s_bot, CHIPS, axis=0, tiled=True)]
    all_to_all x1 -> x0, starting transfers between devices: 11.6 us -> none  [exchange(): return lax.all_to_all(x, CHIPS, 0, 0)]
    pallas_call x10 -> x12, Pallas kernels: 39.4 us -> 33.7 us  [call(): pl.pallas_call(kernel, out_shape=out_shape, in_specs=[ANY if i in in_any...]
    ppermute x7 -> x6, waiting for transfers between devices: 6.02 us -> 3.52 us  [swap(): return lax.ppermute(x, 'c', SWAP)]
  transfers between devices with their start and end apart: 9 -> 6, of which waited for: 5 -> 3; matrix products, arithmetic and copies ran while one was open for 0% -> 0% of each run, Pallas kernels for 9% -> 7%
where the time goes in v2:
time: 166 us
  blocking collectives  127 us (77%)
  Pallas kernels  33.7 us (20%)
  waiting for transfers between devices  3.52 us (2%)
    all_to_all x5, blocking collectives, exchange(): return lax.all_to_all(x, CHIPS, 0, 0)  127 us
    pallas_call x12, Pallas kernels, call(): pl.pallas_call(kernel, out_shape=out_shape, in_specs=[ANY if i in in_any...  33.7 us
    ppermute x6, waiting for transfers between devices, swap(): return lax.ppermute(x, 'c', SWAP)  3.52 us
  transfers between devices with their start and end apart: 6, of which 3 were waited for; matrix products, arithmetic and copies ran while one was open for 0% of the time, Pallas kernels for 7%

profile of v2, /device:TPU:0, one launch (start us, length us, event | category | flops | bytes accessed | tf_op | source)
XLA Modules:
  0.0 165.8 jit_solution(10146341228020227737)
XLA Ops:
  0.6 3.4 %shard_map.76 = bf16[64,24,768]{2,1,0:T(8,128)(2,1)} custom-call(bf16[24,384]{1,0:T(8,128)(2,1)} %hid_ref.3, bf16[24,2048]{1,0:T(8,128)(2,1)} %hid_ref.2, bf16[2048,384]{1,0:T(8,128)(2,1)} %proj_ref.1), custom_call_target="tpu_custom_call" | custom-call | tf_op jit(solution)/shard_map/pallas_call | solution.py:33
  4.1 0.0 copy-start
  4.1 0.0 copy-start.1
  4.1 44.7 %all_to_all.25 = bf16[64,24,768]{2,1,0:T(8,128)(2,1)S(1)} all-to-all(bf16[64,24,768]{2,1,0:T(8,128)(2,1)} %shard_map.76), channel_id=1, replica_groups=mesh['z'=4,'y'=4,'x'=4,'c'=2] {'z','y','x'}, dimensions={0} | all-to-all | bytes 4718592 | tf_op jit(solution)/shard_map/all_to_all | solution.py:283
  48.8 0.0 collective-permute-start
  48.8 4.7 %shard_map.77 = (f32[1024,1536]{1,0:T(8,128)S(1)}, f32[1024,1536]{1,0:T(8,128)S(1)}, bf16[1024,384]{1,0:T(8,128)(2,1)S(1)}, bf16[1024,384]{1,0:T(8,128)(2,1)S(1)...) custom-call(bf16[384,1024]{1,0:T(8,128)(2,1)S(1)} %copy-done.1, ...), custom_call_target="tpu_custom_call" | custom-call | tf_op jit(solution)/shard_map/pallas_call | solution.py:33
  53.5 0.0 collective-permute-done.rows_ref.other_ref
  53.6 5.2 %shard_map.78 = (f32[1024,1536]{1,0:T(8,128)S(1)}, f32[1024,1536]{1,0:T(8,128)S(1)}, bf16[64,16,384]{2,1,0:T(8,128)(2,1)S(1)}) custom-call(bf16[1024,384]{1,0:T(8,128)(2,1)S(1)} %get-tuple-element.25.t_lhs, bf16[1024,384]{1,0:T(8,128)(2,1)S(1)} %get-tuple-element.26.s_lhs, bf16[1536,768]{1,0:T(8,128)(2,1)S(1)} %collective-permute-done.rows_ref.other_ref, ...), custom_call_target="tpu_custom_call" | custom-call | tf_op jit(solution)/shard_map/pallas_call | solution.py:33
  58.7 22.0 %all_to_all.26.got_ref = bf16[64,16,384]{2,1,0:T(8,128)(2,1)S(1)} all-to-all(bf16[64,16,384]{2,1,0:T(8,128)(2,1)S(1)} %get-tuple-element.32), channel_id=1, replica_groups=mesh['z'=4,'y'=4,'x'=4,'c'=2] {'z','y','x'}, dimensions={0} | all-to-all | bytes 1572864 | tf_op jit(solution)/shard_map/all_to_all | solution.py:283
  80.7 0.2 shard_map.79.mine_ref.first_a
  80.9 0.1 collective-permute-start.1
  81.0 1.2 collective-permute-done.1.theirs_ref.first_b
  82.2 2.8 %shard_map.80 = (bf16[64,8,384]{2,1,0:T(8,128)(2,1)S(1)}, f32[1024,1]{1,0:T(8,128)}) custom-call(f32[1024,1536]{1,0:T(8,128)S(1)} %get-tuple-element.24.e_own.own_ref, f32[1024,1536]{1,0:T(8,128)S(1)} %get-tuple-element.29.other_ref.e_other, f32[16,384]{1,0:T(8,128)S(1)} %shard_map.79.mine_ref.first_a, f32[16,384]{1,0:T(8,128)S(1)} %collective-permute-done.1.theirs_ref.first_b), custom_call_target="tpu_custom_call" | custom-call | tf_op jit(solution)/shard_map/pallas_call | solution.py:33
  84.9 16.7 %all_to_all.27.got_ref = bf16[64,8,384]{2,1,0:T(8,128)(2,1)S(1)} all-to-all(bf16[64,8,384]{2,1,0:T(8,128)(2,1)S(1)} %get-tuple-element.33), channel_id=1, replica_groups=mesh['z'=4,'y'=4,'x'=4,'c'=2] {'z','y','x'}, dimensions={0} | all-to-all | bytes 786432 | tf_op jit(solution)/shard_map/all_to_all | solution.py:283
  101.7 0.1 shard_map.81.mine_ref
  101.8 0.1 collective-permute-start.2
  101.9 1.2 collective-permute-done.2.theirs_ref
  103.0 2.1 %shard_map.82 = (bf16[64,8,384]{2,1,0:T(8,128)(2,1)S(1)}, f32[1024,1]{1,0:T(8,128)S(1)}) custom-call(f32[1024,1536]{1,0:T(8,128)S(1)} %get-tuple-element.24.e_own.own_ref, f32[1024,1536]{1,0:T(8,128)S(1)} %get-tuple-element.29.other_ref.e_other, f32[8,384]{1,0:T(8,128)S(1)} %shard_map.81.mine_ref, f32[8,384]{1,0:T(8,128)S(1)} %collective-permute-done.2.theirs_ref), custom_call_target="tpu_custom_call" | custom-call | tf_op jit(solution)/shard_map/pallas_call | solution.py:33
  105.1 16.9 %all_to_all.28.got_ref = bf16[64,8,384]{2,1,0:T(8,128)(2,1)S(1)} all-to-all(bf16[64,8,384]{2,1,0:T(8,128)(2,1)S(1)} %get-tuple-element.36), channel_id=1, replica_groups=mesh['z'=4,'y'=4,'x'=4,'c'=2] {'z','y','x'}, dimensions={0} | all-to-all | bytes 786432 | tf_op jit(solution)/shard_map/all_to_all | solution.py:283
  122.0 0.1 shard_map.83.last_a
  122.1 0.1 collective-permute-start.3
  122.2 1.2 collective-permute-done.3.last_b
  123.3 6.5 %shard_map.84 = (bf16[1024,1536]{1,0:T(8,128)(2,1)S(1)}, bf16[1024,1536]{1,0:T(8,128)(2,1)S(1)}, f32[1536,384]{1,0:T(8,128)S(1)}, f32[8,128]{1,0:T(8,128)S(1)}) custom-call(f32[1024,1536]{1,0:T(8,128)S(1)} %get-tuple-element.24.e_own.own_ref, f32[1024,1536]{1,0:T(8,128)S(1)} %get-tuple-element.29.other_ref.e_other, ...), custom_call_target="tpu_custom_call" | custom-call | tf_op jit(solution)/shard_map/pallas_call | solution.py:33
  129.8 0.2 collective-permute-start.4
  130.1 0.3 collective-permute-start.5
  130.4 7.4 %shard_map.85 = (f32[384,1024]{1,0:T(8,128)}, f32[1536,384]{1,0:T(8,128)S(1)}) custom-call(bf16[1024,1536]{1,0:T(8,128)(2,1)S(1)} %get-tuple-element.37.g_own, bf16[1024,1536]{1,0:T(8,128)(2,1)S(1)} %get-tuple-element.38.g_other, bf16[384,1024]{1,0:T(8,128)(2,1)S(1)} %get-tuple-element.35.cols_ref, bf16[384,1024]{1,0:T(8,128)(2,1)S(1)} %copy-done, ...), custom_call_target="tpu_custom_call" | custom-call | tf_op jit(solution)/shard_map/pallas_call | solution.py:33
  137.8 0.0 collective-permute-done.5.loss_b
  137.8 0.0 collective-permute-done.4.theirs_ref
  137.8 0.4 shard_map.86
  138.2 0.0 copy-start.2
  138.2 26.7 %all_to_all.29.got_ref = bf16[64,80,128]{2,1,0:T(8,128)(2,1)S(1)} all-to-all(bf16[64,80,128]{2,1,0:T(8,128)(2,1)S(1)} %shard_map.86), channel_id=1, replica_groups=mesh['z'=4,'y'=4,'x'=4,'c'=2] {'z','y','x'}, dimensions={0} | all-to-all | bytes 2621440 | tf_op jit(solution)/shard_map/all_to_all | solution.py:283
  164.9 0.9 shard_map.87
  (3 shorter events, 0.0 us)
Async XLA Ops:
  4.1 44.7 %copy-start = (bf16[384,1024]{1,0:T(8,128)(2,1)S(1)}, bf16[384,1024]{1,0:T(8,128)(2,1)}, u32[]{:S(2)}) copy-start(bf16[384,1024]{1,0:T(8,128)(2,1)} %w_ref.1) | copy-start | bytes 2359300
  4.1 44.7 %copy-start.1 = (bf16[384,1024]{1,0:T(8,128)(2,1)S(1)}, bf16[384,1024]{1,0:T(8,128)(2,1)}, u32[]{:S(2)}) copy-start(bf16[384,1024]{1,0:T(8,128)(2,1)} %tw_ref.1) | copy-start | bytes 2359300
  48.8 4.7 %collective-permute-start = (bf16[1536,768]{1,0:T(8,128)(2,1)S(1)}, bf16[1536,768]{1,0:T(8,128)(2,1)S(1)}, u32[]{:S(2)}, u32[]{:S(2)}) collective-permute-start(bf16[1536,768]{1,0:T(8,128)(2,1)S(1)} %bitcast.3), channel_id=1, source_target_pairs={{0,1},{1,0},{2,3},{3,2},{4,5},{5,4},{6,7},{7,6},{8,9},{9,8},{10,11... | collective-permute-start | bytes 7077896 | tf_op jit(solution)/shard_map/ppermute | solution.py:280
  80.9 1.3 collective-permute-start.1
  101.8 1.3 collective-permute-start.2
  122.1 1.3 collective-permute-start.3
  129.8 8.0 %collective-permute-start.4 = (f32[1536,384]{1,0:T(8,128)S(1)}, f32[1536,384]{1,0:T(8,128)S(1)}, u32[]{:S(2)}, u32[]{:S(2)}) collective-permute-start(f32[1536,384]{1,0:T(8,128)S(1)} %get-tuple-element.40), channel_id=1, source_target_pairs={{0,1},{1,0},{2,3},{3,2},{4,5},{5,4},{6,7},{7,6},{8,9},{9,8},{10,11... | collective-permute-start | bytes 7077896 | tf_op jit(solution)/shard_map/ppermute | solution.py:280
  130.1 7.7 %collective-permute-start.5 = (f32[8,128]{1,0:T(8,128)S(1)}, f32[8,128]{1,0:T(8,128)S(1)}, u32[]{:S(2)}, u32[]{:S(2)}) collective-permute-start(f32[8,128]{1,0:T(8,128)S(1)} %get-tuple-element.41.loss_a), channel_id=1, source_target_pairs={{0,1},{1,0},{2,3},{3,2},{4,5},{5,4},{6,7},{7,6},{8,9},{9,8},{10,11... | collective-permute-start | bytes 12296 | tf_op jit(solution)/shard_map/ppermute | solution.py:280
  138.2 26.7 %copy-start.2 = (bf16[24,384]{1,0:T(8,128)(2,1)S(1)}, bf16[24,384]{1,0:T(8,128)(2,1)}, u32[]{:S(2)}) copy-start(bf16[24,384]{1,0:T(8,128)(2,1)} %hid_ref.3) | copy-start | bytes 55300

commit v3 on v2

--- a/solution.py
+++ b/solution.py
@@ -22,7 +22,7 @@
 NT = (((1,), (1,)), ((), ()))
 VM = pl.BlockSpec(memory_space=pltpu.VMEM)
 CHUNK = 256
-BLOCK = 128
+BLOCK = 256
 ANY = pl.BlockSpec(memory_space=pltpu.HBM)
 
 
@@ -97,19 +97,18 @@
     out_ref[...] = jnp.sum(got_ref[...].astype(F32), axis=0)
 
 
+def chunks(total, size):
+    return [slice(j, j + size) for j in range(0, total, size)]
+
+
 def own_kernel(tw_ref, sw_ref, rows_ref, e_ref, lg_ref, t_lhs, s_lhs, s_cols, sums_ref, part_ref):
     part_ref[...] = jnp.zeros_like(part_ref)
-
-    def step(j, _):
-        at = pl.ds(pl.multiple_of(j * CHUNK, CHUNK), CHUNK)
+    for at in chunks(tw_ref.shape[1], CHUNK):
         t_lhs[at, :] = columns(tw_ref[:, at])[0].T.astype(BF16)
         unit = columns(sw_ref[:, at])[0]
         s_cols[:, at] = unit.astype(BF16)
         s_lhs[at, :] = unit.T.astype(BF16)
         sums_ref[at, :] = products(at, t_lhs, s_lhs, rows_ref, e_ref, lg_ref, part_ref)
-        return 0
-
-    lax.fori_loop(0, tw_ref.shape[1] // CHUNK, step, 0)
 
 
 def products(at, t_lhs, s_lhs, rows_ref, e_ref, lg_ref, part_ref):
@@ -130,16 +129,11 @@
     half = rows_ref.shape[0]
     part[...] = jnp.zeros_like(part)
     acc[...] = jnp.zeros_like(acc)
-
-    def step(j, _):
-        at = pl.ds(pl.multiple_of(j * CHUNK, CHUNK), CHUNK)
+    for at in chunks(t_lhs.shape[0], CHUNK):
         sums = sums_ref[at, :] + products(at, t_lhs, s_lhs, rows_ref, e_ref, lg_ref, part)
         scale = 1.0 / (total_cols * sums)
         row_pass(e_own.at[at, :], scale, acc.at[:, :half])
         row_pass(e_ref.at[at, :], scale, acc.at[:, half:])
-        return 0
-
-    lax.fori_loop(0, t_lhs.shape[0] // CHUNK, step, 0)
     parts = jnp.concatenate([part_own[...], part[...]], axis=1)
     row = fold(jnp.sum(acc[...], axis=0, keepdims=True))
     spread(jnp.concatenate([row, fold(jnp.sum(parts, axis=0, keepdims=True))], axis=0), out_ref)
@@ -176,7 +170,6 @@
 
 
 STRIP = 32
-LANES = 768
 
 
 def grad_kernel(
@@ -190,51 +183,48 @@
     rows[0:8, :] = jnp.broadcast_to((1.0 / student_temp) / part, (8, n))
     rows[8:16, :] = jnp.broadcast_to((1.0 / student_temp) / row, (8, n))
     acc[...] = jnp.zeros_like(acc)
-    fold_rows = (STRIP // 8, 8, LANES)
+
+    def piece(at, lanes, wide, e_ref, lg_ref, g_ref):
+        logits = lg_ref[at, lanes]
+        scaled = e_ref[at, lanes] * cs_ref[at, :]
+        folded = (STRIP // 8, 8, logits.shape[1])
+        acc[:, wide] += jnp.sum((scaled * logits).reshape(folded), axis=0)
+        powers = jnp.exp(logits).reshape(folded) * rows[0:8, wide][None]
+        target = scaled.reshape(folded) * rows[8:16, wide][None]
+        g_ref[at, lanes] = (powers - target).reshape(logits.shape).astype(BF16)
 
     def step(k, _):
         at = pl.ds(pl.multiple_of(k * STRIP, STRIP), STRIP)
-        scale = cs_ref[at, :]
-        for e_ref, lg_ref, g_ref, offset in ((e_own, lg_own, g_own, 0), (e_other, lg_other, g_other, half)):
-            for start in range(0, half, LANES):
-                lanes = slice(start, start + LANES)
-                wide = slice(offset + start, offset + start + LANES)
-                logits = lg_ref[at, lanes]
-                scaled = e_ref[at, lanes] * scale
-                acc[:, wide] += jnp.sum((scaled * logits).reshape(fold_rows), axis=0)
-                powers = jnp.exp(logits).reshape(fold_rows) * rows[0:8, wide][None]
-                target = scaled.reshape(fold_rows) * rows[8:16, wide][None]
-                g_ref[at, lanes] = (powers - target).reshape(STRIP, LANES).astype(BF16)
+        for lanes in chunks(half, half // 2):
+            piece(at, lanes, slice(half + lanes.start, half + lanes.stop), e_other, lg_other, g_other)
         return 0
 
-    lax.fori_loop(0, protos // STRIP, step, 0)
+    lax.fori_loop(0, protos // STRIP, step, 0, unroll=2)
+    for lanes in chunks(half, CHUNK):
+        for at in chunks(protos, STRIP):
+            piece(at, lanes, lanes, e_own, lg_own, g_own)
+        bottleneck(lanes, cols_ref, g_other, other_ref)
     terms = jnp.log(part) * (1.0 / devices) - jnp.sum(acc[...], axis=0, keepdims=True) / row
     pieces = fold(terms)
-    loss_ref[...] = sum(pieces[:, 128 * k : 128 * (k + 1)] for k in range(n // 1024))
-    bottleneck(cols_ref, g_other, other_ref)
-
-
-def bottleneck(cols_ref, g_ref, out_ref):
-    for i in range(out_ref.shape[0] // CHUNK):
-        at = slice(i * CHUNK, (i + 1) * CHUNK)
-        block = jnp.dot(cols_ref[...], g_ref[:, at], preferred_element_type=F32)
-        out_ref[at, :] = block.T
-
-
-def protos_kernel(g_own, g_other, cols_ref, w_ref, own_ref, other_ref, dp_ref, db_ref):
+    loss_ref[...] = sum(pieces[:, lanes] for lanes in chunks(n // 8, 128))
+
+
+def bottleneck(lanes, cols_ref, g_ref, out_ref):
+    out_ref[lanes, :] = jnp.dot(cols_ref[...], g_ref[:, lanes], preferred_element_type=F32).T
+
+
+def protos_kernel(g_own, g_other, cols_ref, w_ref, own_ref, other_ref, dp_ref, db_ref, rows):
     bot = w_ref.shape[0]
-    bottleneck(cols_ref, g_own, db_ref)
-
-    def step(j, _):
-        at = pl.ds(pl.multiple_of(j * CHUNK, CHUNK), CHUNK)
-        d_unit = jnp.dot(g_own[at, :], own_ref[:, bot:], preferred_element_type=F32)
-        d_unit = d_unit + jnp.dot(g_other[at, :], other_ref[:, bot:], preferred_element_type=F32)
-        d_unit = d_unit.T
+    half = own_ref.shape[0]
+    for lanes in chunks(half, CHUNK):
+        bottleneck(lanes, cols_ref, g_own, db_ref)
+    rows[:, :half] = own_ref[:, bot:].T
+    rows[:, half:] = other_ref[:, bot:].T
+    for at in chunks(w_ref.shape[1], CHUNK):
+        d_unit = lax.dot_general(rows[:, :half], g_own[at, :], NT, preferred_element_type=F32)
+        d_unit = d_unit + lax.dot_general(rows[:, half:], g_other[at, :], NT, preferred_element_type=F32)
         unit, inv = columns(w_ref[:, at])
         dp_ref[:, at] = inv * (d_unit - unit * jnp.sum(unit * d_unit, axis=0, keepdims=True))
-        return 0
-
-    lax.fori_loop(0, w_ref.shape[1] // CHUNK, step, 0)
 
 
 def pack_kernel(mine_ref, theirs_ref, loss_a, loss_b, out_ref):
@@ -345,6 +335,7 @@
         (sds((bot, protos), F32), sds((half, bot), F32)),
         (g_own, g_other, s_cols, student_protos, own, other),
         12,
+        [pltpu.VMEM((bot, images), BF16)],
     )
     packed = call(
         pack_kernel,

time: 166 us -> 162 us (0.976)
  Pallas kernels: 33.7 us -> 29.5 us
    pallas_call x12, Pallas kernels: 33.7 us -> 29.5 us  [call(): pl.pallas_call(kernel, out_shape=out_shape, in_specs=[ANY if i in in_any...]
  transfers between devices with their start and end apart: 6 -> 6, of which waited for: 3 -> 4; matrix products, arithmetic and copies ran while one was open for 0% -> 0% of each run, Pallas kernels for 7% -> 6%
where the time goes in v3:
time: 162 us
  blocking collectives  127 us (78%)
  Pallas kernels  29.5 us (18%)
  waiting for transfers between devices  4.05 us (2%)
    all_to_all x5, blocking collectives, exchange(): return lax.all_to_all(x, CHIPS, 0, 0)  127 us
    pallas_call x12, Pallas kernels, call(): pl.pallas_call(kernel, out_shape=out_shape, in_specs=[ANY if i in in_any...  29.5 us
    ppermute x6, waiting for transfers between devices, swap(): return lax.ppermute(x, 'c', SWAP)  4.05 us
  transfers between devices with their start and end apart: 6, of which 4 were waited for; matrix products, arithmetic and copies ran while one was open for 0% of the time, Pallas kernels for 6%

profile of v3, /device:TPU:0, one launch (start us, length us, event | category | flops | bytes accessed | tf_op | source)
XLA Modules:
  0.0 161.9 jit_solution(13947815763453586857)
XLA Ops:
  0.6 3.4 %shard_map.76 = bf16[64,24,768]{2,1,0:T(8,128)(2,1)} custom-call(bf16[24,384]{1,0:T(8,128)(2,1)} %hid_ref.3, bf16[24,2048]{1,0:T(8,128)(2,1)} %hid_ref.2, bf16[2048,384]{1,0:T(8,128)(2,1)} %proj_ref.1), custom_call_target="tpu_custom_call" | custom-call | tf_op jit(solution)/shard_map/pallas_call | solution.py:33
  4.1 0.0 copy-start
  4.1 0.0 copy-start.1
  4.1 44.7 %all_to_all.25 = bf16[64,24,768]{2,1,0:T(8,128)(2,1)S(1)} all-to-all(bf16[64,24,768]{2,1,0:T(8,128)(2,1)} %shard_map.76), channel_id=1, replica_groups=mesh['z'=4,'y'=4,'x'=4,'c'=2] {'z','y','x'}, dimensions={0} | all-to-all | bytes 4718592 | tf_op jit(solution)/shard_map/all_to_all | solution.py:273
  48.8 0.0 collective-permute-start
  48.8 4.0 %shard_map.77 = (f32[1024,1536]{1,0:T(8,128)S(1)}, f32[1024,1536]{1,0:T(8,128)S(1)}, bf16[1024,384]{1,0:T(8,128)(2,1)S(1)}, bf16[1024,384]{1,0:T(8,128)(2,1)S(1)...) custom-call(bf16[384,1024]{1,0:T(8,128)(2,1)S(1)} %copy-done.1, ...), custom_call_target="tpu_custom_call" | custom-call | tf_op jit(solution)/shard_map/pallas_call | solution.py:33
  52.8 0.5 collective-permute-done.rows_ref.other_ref
  53.3 5.1 %shard_map.78 = (f32[1024,1536]{1,0:T(8,128)S(1)}, f32[1024,1536]{1,0:T(8,128)S(1)}, bf16[64,16,384]{2,1,0:T(8,128)(2,1)S(1)}) custom-call(bf16[1024,384]{1,0:T(8,128)(2,1)S(1)} %get-tuple-element.25.t_lhs, bf16[1024,384]{1,0:T(8,128)(2,1)S(1)} %get-tuple-element.26.s_lhs, bf16[1536,768]{1,0:T(8,128)(2,1)S(1)} %collective-permute-done.rows_ref.other_ref, ...), custom_call_target="tpu_custom_call" | custom-call | tf_op jit(solution)/shard_map/pallas_call | solution.py:33
  58.4 21.6 %all_to_all.26.got_ref = bf16[64,16,384]{2,1,0:T(8,128)(2,1)S(1)} all-to-all(bf16[64,16,384]{2,1,0:T(8,128)(2,1)S(1)} %get-tuple-element.32), channel_id=1, replica_groups=mesh['z'=4,'y'=4,'x'=4,'c'=2] {'z','y','x'}, dimensions={0} | all-to-all | bytes 1572864 | tf_op jit(solution)/shard_map/all_to_all | solution.py:273
  80.0 0.2 shard_map.79.mine_ref.first_a
  80.2 0.1 collective-permute-start.1
  80.3 1.2 collective-permute-done.1.theirs_ref.first_b
  81.5 2.7 %shard_map.80 = (bf16[64,8,384]{2,1,0:T(8,128)(2,1)S(1)}, f32[1024,1]{1,0:T(8,128)}) custom-call(f32[1024,1536]{1,0:T(8,128)S(1)} %get-tuple-element.24.e_own.own_ref, f32[1024,1536]{1,0:T(8,128)S(1)} %get-tuple-element.29.other_ref.e_other, f32[16,384]{1,0:T(8,128)S(1)} %shard_map.79.mine_ref.first_a, f32[16,384]{1,0:T(8,128)S(1)} %collective-permute-done.1.theirs_ref.first_b), custom_call_target="tpu_custom_call" | custom-call | tf_op jit(solution)/shard_map/pallas_call | solution.py:33
  84.1 16.9 %all_to_all.27.got_ref = bf16[64,8,384]{2,1,0:T(8,128)(2,1)S(1)} all-to-all(bf16[64,8,384]{2,1,0:T(8,128)(2,1)S(1)} %get-tuple-element.33), channel_id=1, replica_groups=mesh['z'=4,'y'=4,'x'=4,'c'=2] {'z','y','x'}, dimensions={0} | all-to-all | bytes 786432 | tf_op jit(solution)/shard_map/all_to_all | solution.py:273
  101.1 0.1 shard_map.81.mine_ref
  101.1 0.1 collective-permute-start.2
  101.2 1.2 collective-permute-done.2.theirs_ref
  102.4 2.0 %shard_map.82 = (bf16[64,8,384]{2,1,0:T(8,128)(2,1)S(1)}, f32[1024,1]{1,0:T(8,128)S(1)}) custom-call(f32[1024,1536]{1,0:T(8,128)S(1)} %get-tuple-element.24.e_own.own_ref, f32[1024,1536]{1,0:T(8,128)S(1)} %get-tuple-element.29.other_ref.e_other, f32[8,384]{1,0:T(8,128)S(1)} %shard_map.81.mine_ref, f32[8,384]{1,0:T(8,128)S(1)} %collective-permute-done.2.theirs_ref), custom_call_target="tpu_custom_call" | custom-call | tf_op jit(solution)/shard_map/pallas_call | solution.py:33
  104.4 16.9 %all_to_all.28.got_ref = bf16[64,8,384]{2,1,0:T(8,128)(2,1)S(1)} all-to-all(bf16[64,8,384]{2,1,0:T(8,128)(2,1)S(1)} %get-tuple-element.36), channel_id=1, replica_groups=mesh['z'=4,'y'=4,'x'=4,'c'=2] {'z','y','x'}, dimensions={0} | all-to-all | bytes 786432 | tf_op jit(solution)/shard_map/all_to_all | solution.py:273
  121.3 0.1 shard_map.83.last_a
  121.4 0.1 collective-permute-start.3
  121.4 1.2 collective-permute-done.3.last_b
  122.6 5.5 %shard_map.84 = (bf16[1024,1536]{1,0:T(8,128)(2,1)S(1)}, bf16[1024,1536]{1,0:T(8,128)(2,1)S(1)}, f32[1536,384]{1,0:T(8,128)S(1)}, f32[8,128]{1,0:T(8,128)S(1)}) custom-call(f32[1024,1536]{1,0:T(8,128)S(1)} %get-tuple-element.24.e_own.own_ref, f32[1024,1536]{1,0:T(8,128)S(1)} %get-tuple-element.29.other_ref.e_other, ...), custom_call_target="tpu_custom_call" | custom-call | tf_op jit(solution)/shard_map/pallas_call | solution.py:33
  128.1 0.2 collective-permute-start.4
  128.3 0.3 collective-permute-start.5
  128.7 5.3 %shard_map.85 = (f32[384,1024]{1,0:T(8,128)}, f32[1536,384]{1,0:T(8,128)S(1)}) custom-call(bf16[1024,1536]{1,0:T(8,128)(2,1)S(1)} %get-tuple-element.37.g_own, bf16[1024,1536]{1,0:T(8,128)(2,1)S(1)} %get-tuple-element.38.g_other, bf16[384,1024]{1,0:T(8,128)(2,1)S(1)} %get-tuple-element.35.cols_ref, bf16[384,1024]{1,0:T(8,128)(2,1)S(1)} %copy-done, ...), custom_call_target="tpu_custom_call" | custom-call | tf_op jit(solution)/shard_map/pallas_call | solution.py:33
  133.9 0.0 collective-permute-done.5.loss_b
  133.9 0.0 collective-permute-done.4.theirs_ref
  133.9 0.4 shard_map.86
  134.3 0.0 copy-start.2
  134.4 26.6 %all_to_all.29.got_ref = bf16[64,80,128]{2,1,0:T(8,128)(2,1)S(1)} all-to-all(bf16[64,80,128]{2,1,0:T(8,128)(2,1)S(1)} %shard_map.86), channel_id=1, replica_groups=mesh['z'=4,'y'=4,'x'=4,'c'=2] {'z','y','x'}, dimensions={0} | all-to-all | bytes 2621440 | tf_op jit(solution)/shard_map/all_to_all | solution.py:273
  160.9 0.9 shard_map.87
  (3 shorter events, 0.0 us)
Async XLA Ops:
  4.1 44.7 %copy-start = (bf16[384,1024]{1,0:T(8,128)(2,1)S(1)}, bf16[384,1024]{1,0:T(8,128)(2,1)}, u32[]{:S(2)}) copy-start(bf16[384,1024]{1,0:T(8,128)(2,1)} %w_ref.1) | copy-start | bytes 2359300
  4.1 44.7 %copy-start.1 = (bf16[384,1024]{1,0:T(8,128)(2,1)S(1)}, bf16[384,1024]{1,0:T(8,128)(2,1)}, u32[]{:S(2)}) copy-start(bf16[384,1024]{1,0:T(8,128)(2,1)} %tw_ref.1) | copy-start | bytes 2359300
  48.8 4.5 %collective-permute-start = (bf16[1536,768]{1,0:T(8,128)(2,1)S(1)}, bf16[1536,768]{1,0:T(8,128)(2,1)S(1)}, u32[]{:S(2)}, u32[]{:S(2)}) collective-permute-start(bf16[1536,768]{1,0:T(8,128)(2,1)S(1)} %bitcast.3), channel_id=1, source_target_pairs={{0,1},{1,0},{2,3},{3,2},{4,5},{5,4},{6,7},{7,6},{8,9},{9,8},{10,11... | collective-permute-start | bytes 7077896 | tf_op jit(solution)/shard_map/ppermute | solution.py:270
  80.2 1.3 collective-permute-start.1
  101.1 1.3 collective-permute-start.2
  121.4 1.3 collective-permute-start.3
  128.1 5.9 %collective-permute-start.4 = (f32[1536,384]{1,0:T(8,128)S(1)}, f32[1536,384]{1,0:T(8,128)S(1)}, u32[]{:S(2)}, u32[]{:S(2)}) collective-permute-start(f32[1536,384]{1,0:T(8,128)S(1)} %get-tuple-element.40), channel_id=1, source_target_pairs={{0,1},{1,0},{2,3},{3,2},{4,5},{5,4},{6,7},{7,6},{8,9},{9,8},{10,11... | collective-permute-start | bytes 7077896 | tf_op jit(solution)/shard_map/ppermute | solution.py:270
  128.3 5.6 %collective-permute-start.5 = (f32[8,128]{1,0:T(8,128)S(1)}, f32[8,128]{1,0:T(8,128)S(1)}, u32[]{:S(2)}, u32[]{:S(2)}) collective-permute-start(f32[8,128]{1,0:T(8,128)S(1)} %get-tuple-element.41.loss_a), channel_id=1, source_target_pairs={{0,1},{1,0},{2,3},{3,2},{4,5},{5,4},{6,7},{7,6},{8,9},{9,8},{10,11... | collective-permute-start | bytes 12296 | tf_op jit(solution)/shard_map/ppermute | solution.py:270
  134.3 26.6 %copy-start.2 = (bf16[24,384]{1,0:T(8,128)(2,1)S(1)}, bf16[24,384]{1,0:T(8,128)(2,1)}, u32[]{:S(2)}) copy-start(bf16[24,384]{1,0:T(8,128)(2,1)} %hid_ref.3) | copy-start | bytes 55300

commit v4 on v3

--- a/solution.py
+++ b/solution.py
@@ -53,7 +53,11 @@
 
 
 def flat(block):
-    return jnp.concatenate([block[j : j + 1, :] for j in range(8)], axis=1)
+    return jnp.concatenate([block[j : j + 1, :] for j in range(block.shape[0])], axis=1)
+
+
+def half_rows(mine, theirs):
+    return flat(jnp.concatenate([mine, theirs], axis=0))
 
 
 def total_row(mine, theirs):
@@ -123,20 +127,34 @@
     return jnp.sum(expo, axis=1, keepdims=True)
 
 
-def other_kernel(
-    total_cols, t_lhs, s_lhs, rows_ref, e_own, sums_ref, part_own, e_ref, lg_ref, out_ref, part, acc
-):
-    half = rows_ref.shape[0]
+def other_kernel(total_cols, t_lhs, s_lhs, rows_ref, sums_ref, e_ref, lg_ref, cs_ref, out_ref, part, acc):
     part[...] = jnp.zeros_like(part)
     acc[...] = jnp.zeros_like(acc)
     for at in chunks(t_lhs.shape[0], CHUNK):
         sums = sums_ref[at, :] + products(at, t_lhs, s_lhs, rows_ref, e_ref, lg_ref, part)
         scale = 1.0 / (total_cols * sums)
-        row_pass(e_own.at[at, :], scale, acc.at[:, :half])
-        row_pass(e_ref.at[at, :], scale, acc.at[:, half:])
-    parts = jnp.concatenate([part_own[...], part[...]], axis=1)
-    row = fold(jnp.sum(acc[...], axis=0, keepdims=True))
-    spread(jnp.concatenate([row, fold(jnp.sum(parts, axis=0, keepdims=True))], axis=0), out_ref)
+        cs_ref[at, :] = scale
+        row_pass(e_ref.at[at, :], scale, acc)
+    out_ref[...] = fold_pair(acc[...], part[...])
+
+
+def fold_pair(rows, parts):
+    both = jnp.concatenate([jnp.sum(rows, axis=0, keepdims=True), jnp.sum(parts, axis=0, keepdims=True)], axis=1)
+    return fold(both)
+
+
+def own_rows_kernel(e_ref, cs_ref, part_ref, out_ref, acc):
+    acc[...] = jnp.zeros_like(acc)
+    row_pass(e_ref, cs_ref[...], acc)
+    out_ref[...] = fold_pair(acc[...], part_ref[...])
+
+
+def send_kernel(mine_ref, theirs_ref, out_ref):
+    spread(mine_ref[...] + theirs_ref[...], out_ref)
+
+
+def turn_kernel(rows_ref, out_ref):
+    out_ref[...] = rows_ref[:, out_ref.shape[0] :].T
 
 
 def row_pass(block_ref, scale, acc):
@@ -147,8 +165,11 @@
         acc[:, lanes] += jnp.sum(block_ref[:, lanes].reshape(rows // 8, 8, 512) * scale, axis=0)
 
 
-def pass_kernel(total_cols, images, own_ref, other_ref, mine_ref, theirs_ref, out_ref, cs_ref, weight, acc):
-    total = total_row(mine_ref[0:8, :], theirs_ref[0:8, :])
+def pass_kernel(total_cols, images, first, own_ref, other_ref, mine_ref, theirs_ref, out_ref, cs_ref, weight, acc):
+    if first:
+        total = half_rows(mine_ref[0:4, :], theirs_ref[0:4, :])
+    else:
+        total = total_row(mine_ref[...], theirs_ref[...])
     weight[...] = jnp.broadcast_to(1.0 / (images * total), weight.shape)
     acc[...] = jnp.zeros_like(acc)
     protos, half = own_ref.shape
@@ -170,65 +191,82 @@
 
 
 STRIP = 32
-
-
-def grad_kernel(
-    devices, e_own, e_other, lg_own, lg_other, cs_ref, cols_ref, first_a, first_b, last_a, last_b,
-    g_own, g_other, other_ref, loss_ref, rows, acc
+DEPTH = 512
+
+
+def half_gradients(row, part, e_ref, lg_ref, cs_ref, cols_ref, turned_ref, db_ref, unit_sum, start, g, rows, cross):
+    protos, half = e_ref.shape
+    rows[0:8, :] = jnp.broadcast_to((1.0 / student_temp) / part, (8, half))
+    rows[8:16, :] = jnp.broadcast_to((1.0 / student_temp) / row, (8, half))
+    folded = (STRIP // 8, 8, CHUNK)
+    for _, _, acc in cross:
+        acc[...] = jnp.zeros_like(acc)
+
+    def elementwise(lanes):
+        for at in chunks(protos, STRIP):
+            for expo, logits, acc in cross:
+                scaled = expo[at, lanes] * cs_ref[at, :]
+                acc[:, lanes] += jnp.sum((scaled * logits[at, lanes]).reshape(folded), axis=0)
+            logits = lg_ref[at, lanes]
+            scaled = e_ref[at, lanes] * cs_ref[at, :]
+            powers = jnp.exp(logits).reshape(folded) * rows[0:8, lanes][None]
+            target = scaled.reshape(folded) * rows[8:16, lanes][None]
+            g[at, lanes] = (powers - target).reshape(logits.shape).astype(BF16)
+
+    def matmuls(lanes):
+        db_ref[lanes, :] = jnp.dot(cols_ref[...], g[:, lanes], preferred_element_type=F32).T
+        if lanes.stop % DEPTH == 0:
+            deep = slice(lanes.stop - DEPTH, lanes.stop)
+            term = lax.dot_general(turned_ref[:, deep], g[:, deep], NT, preferred_element_type=F32)
+            if lanes.stop > DEPTH:
+                unit_sum[...] += term
+            else:
+                unit_sum[...] = term if start is None else start[...] + term
+
+    before = None
+    for lanes in chunks(half, CHUNK):
+        elementwise(lanes)
+        if before is not None:
+            matmuls(before)
+        before = lanes
+    matmuls(before)
+
+
+def grad_other_kernel(
+    devices, e_ref, lg_ref, cs_ref, cols_ref, turned_ref, part_own, part_other, mine_ref, theirs_ref, e_own, lg_own,
+    db_ref, unit_sum, loss_ref, g, rows, acc, acc_own
 ):
-    protos, half = e_own.shape
-    n = 2 * half
-    part = total_row(first_a[8:16, :], first_b[8:16, :])
-    row = total_row(last_a[...], last_b[...])
-    rows[0:8, :] = jnp.broadcast_to((1.0 / student_temp) / part, (8, n))
-    rows[8:16, :] = jnp.broadcast_to((1.0 / student_temp) / row, (8, n))
-    acc[...] = jnp.zeros_like(acc)
-
-    def piece(at, lanes, wide, e_ref, lg_ref, g_ref):
-        logits = lg_ref[at, lanes]
-        scaled = e_ref[at, lanes] * cs_ref[at, :]
-        folded = (STRIP // 8, 8, logits.shape[1])
-        acc[:, wide] += jnp.sum((scaled * logits).reshape(folded), axis=0)
-        powers = jnp.exp(logits).reshape(folded) * rows[0:8, wide][None]
-        target = scaled.reshape(folded) * rows[8:16, wide][None]
-        g_ref[at, lanes] = (powers - target).reshape(logits.shape).astype(BF16)
-
-    def step(k, _):
-        at = pl.ds(pl.multiple_of(k * STRIP, STRIP), STRIP)
-        for lanes in chunks(half, half // 2):
-            piece(at, lanes, slice(half + lanes.start, half + lanes.stop), e_other, lg_other, g_other)
-        return 0
-
-    lax.fori_loop(0, protos // STRIP, step, 0, unroll=2)
-    for lanes in chunks(half, CHUNK):
-        for at in chunks(protos, STRIP):
-            piece(at, lanes, lanes, e_own, lg_own, g_own)
-        bottleneck(lanes, cols_ref, g_other, other_ref)
-    terms = jnp.log(part) * (1.0 / devices) - jnp.sum(acc[...], axis=0, keepdims=True) / row
-    pieces = fold(terms)
-    loss_ref[...] = sum(pieces[:, lanes] for lanes in chunks(n // 8, 128))
-
-
-def bottleneck(lanes, cols_ref, g_ref, out_ref):
-    out_ref[lanes, :] = jnp.dot(cols_ref[...], g_ref[:, lanes], preferred_element_type=F32).T
-
-
-def protos_kernel(g_own, g_other, cols_ref, w_ref, own_ref, other_ref, dp_ref, db_ref, rows):
-    bot = w_ref.shape[0]
-    half = own_ref.shape[0]
-    for lanes in chunks(half, CHUNK):
-        bottleneck(lanes, cols_ref, g_own, db_ref)
-    rows[:, :half] = own_ref[:, bot:].T
-    rows[:, half:] = other_ref[:, bot:].T
-    for at in chunks(w_ref.shape[1], CHUNK):
-        d_unit = lax.dot_general(rows[:, :half], g_own[at, :], NT, preferred_element_type=F32)
-        d_unit = d_unit + lax.dot_general(rows[:, half:], g_other[at, :], NT, preferred_element_type=F32)
+    row = flat(mine_ref[4:8, :] + theirs_ref[0:4, :])
+    part = flat(part_other[4:8, :])
+    cross = ((e_ref, lg_ref, acc), (e_own, lg_own, acc_own))
+    half_gradients(row, part, e_ref, lg_ref, cs_ref, cols_ref, turned_ref, db_ref, unit_sum, None, g, rows, cross)
+    parts = jnp.log(part) + jnp.log(flat(part_own[4:8, :]))
+    row_own = flat(mine_ref[0:4, :] + theirs_ref[4:8, :])
+    crossed = jnp.sum(acc[...], axis=0, keepdims=True) / row + jnp.sum(acc_own[...], axis=0, keepdims=True) / row_own
+    terms = parts * (1.0 / devices) - crossed
+    loss_ref[...] = sum(terms[:, lanes] for lanes in chunks(terms.shape[1], 128))
+
+
+def grad_own_kernel(
+    e_ref, lg_ref, cs_ref, cols_ref, turned_ref, part_ref, mine_ref, theirs_ref, other_sum, w_ref,
+    db_ref, dp_ref, g, rows, unit_sum, out_buf, sem
+):
+    row = flat(mine_ref[0:4, :] + theirs_ref[4:8, :])
+    part = flat(part_ref[4:8, :])
+    half_gradients(row, part, e_ref, lg_ref, cs_ref, cols_ref, turned_ref, db_ref, unit_sum, other_sum, g, rows, ())
+    copies = []
+    for j, at in enumerate(chunks(w_ref.shape[1], CHUNK)):
+        d_unit = unit_sum[:, at]
         unit, inv = columns(w_ref[:, at])
-        dp_ref[:, at] = inv * (d_unit - unit * jnp.sum(unit * d_unit, axis=0, keepdims=True))
+        out_buf[:, at] = inv * (d_unit - unit * jnp.sum(unit * d_unit, axis=0, keepdims=True))
+        copies.append(pltpu.make_async_copy(out_buf.at[:, at], dp_ref.at[:, at], sem.at[j]))
+        copies[j].start()
+    for copy in copies:
+        copy.wait()
 
 
 def pack_kernel(mine_ref, theirs_ref, loss_a, loss_b, out_ref):
-    total = jnp.sum(jnp.sum(loss_a[...] + loss_b[...], axis=0, keepdims=True), axis=1, keepdims=True)
+    total = jnp.sum(loss_a[...] + loss_b[...], axis=1, keepdims=True)
     high = total.astype(BF16).astype(F32)
     mid = (total - high).astype(BF16).astype(F32)
     low = total - high - mid
@@ -303,39 +341,55 @@
         (teacher_protos, student_protos, own),
         8,
     )
-    e_other, lg_other, sent = call(
+    half8 = sds((8, images // 8), F32)
+    send8 = sds((chips, 8, images // 8), BF16)
+    half_acc = pltpu.VMEM((8, half), F32)
+    part, own_late = lax.optimization_barrier((part, own))
+    turned_own = call(turn_kernel, sds((bot, half), BF16), (own_late,), 2)
+    other, turned_own = lax.optimization_barrier((other, turned_own))
+    e_other, lg_other, col_scale, pair_other = call(
         functools.partial(other_kernel, total_cols),
-        (matrix, matrix, sds((chips, 16, images // 8), BF16)),
-        (t_lhs, s_lhs, other, e_own, sums, part),
+        (matrix, matrix, column, half8),
+        (t_lhs, s_lhs, other, sums),
         8,
-        [pltpu.VMEM((8, half), F32), fold8],
-    )
-    first = row_sums(sent, 16)
+        [half_acc, half_acc],
+    )
+    theirs = swap(pair_other)
+    pair_own = call(own_rows_kernel, half8, (e_own, col_scale, part), 4, [half_acc])
+    first = row_sums(call(send_kernel, send8, (pair_own, theirs), 2), 8)
+    kept, late = lax.optimization_barrier((first[0], other))
+    turned_other = call(turn_kernel, sds((bot, half), BF16), (late,), 2)
+    theirs, turned_other = lax.optimization_barrier((first[1], turned_other))
+    first = (kept, theirs)
     sums = first
     for sweep in range(1, ITERS):
         sent, col_scale = call(
-            functools.partial(pass_kernel, total_cols, images),
-            (sds((chips, 8, images // 8), BF16), column),
+            functools.partial(pass_kernel, total_cols, images, sweep == 1),
+            (send8, column),
             (e_own, e_other) + sums,
             4,
             [fold8, fold8],
         )
         sums = row_sums(sent, 8)
-    g_own, g_other, d_other, loss_mine = call(
-        functools.partial(grad_kernel, 2 * chips),
-        (sds((protos, half), BF16), sds((protos, half), BF16), sds((half, bot), F32), sds((8, 128), F32)),
-        (e_own, e_other, lg_own, lg_other, col_scale, s_cols) + first + sums,
-        4,
-        [pltpu.VMEM((16, images), F32), fold8],
+    tile = sds((1, 128), F32)
+    grads = [pltpu.VMEM((protos, half), BF16), pltpu.VMEM((16, half), F32)]
+    d_other, unit_sum, loss_mine = call(
+        functools.partial(grad_other_kernel, 2 * chips),
+        (sds((half, bot), F32), sds((bot, protos), F32), tile),
+        (e_other, lg_other, col_scale, s_cols, turned_other) + first + sums + (e_own, lg_own),
+        8,
+        grads + [half_acc, half_acc],
     )
     d_theirs = swap(d_other)
     loss_theirs = swap(loss_mine)
-    d_protos, d_mine = call(
-        protos_kernel,
-        (sds((bot, protos), F32), sds((half, bot), F32)),
-        (g_own, g_other, s_cols, student_protos, own, other),
+    whole = pltpu.VMEM((bot, protos), F32)
+    d_mine, d_protos = call(
+        grad_own_kernel,
+        (sds((half, bot), F32), sds((bot, protos), F32)),
+        (e_own, lg_own, col_scale, s_cols, turned_own, first[0]) + sums + (unit_sum, student_protos),
         12,
-        [pltpu.VMEM((bot, images), BF16)],
+        grads + [whole, whole, pltpu.SemaphoreType.DMA((protos // CHUNK,))],
+        out_any=(1,),
     )
     packed = call(
         pack_kernel,

time: 162 us -> 157 us (0.969)
  blocking collectives: 127 us -> 123 us
    all_to_all x5, blocking collectives: 127 us -> 123 us  [exchange(): return lax.all_to_all(x, CHIPS, 0, 0)]
    pallas_call x12 -> x16, Pallas kernels: 29.5 us -> 28.1 us  [call(): pl.pallas_call(kernel, out_shape=out_shape, in_specs=[ANY if i in in_any...]
    ppermute x6 -> x7, waiting for transfers between devices: 4.05 us -> 3.61 us  [swap(): return lax.ppermute(x, 'c', SWAP)]
  transfers between devices with their start and end apart: 6 -> 7, of which waited for: 4 -> 5; matrix products, arithmetic and copies ran while one was open for 0% -> 0% of each run, Pallas kernels for 6% -> 6%
where the time goes in v4:
time: 157 us
  blocking collectives  123 us (78%)
  Pallas kernels  28.1 us (18%)
  waiting for transfers between devices  3.61 us (2%)
    all_to_all x5, blocking collectives, exchange(): return lax.all_to_all(x, CHIPS, 0, 0)  123 us
    pallas_call x16, Pallas kernels, call(): pl.pallas_call(kernel, out_shape=out_shape, in_specs=[ANY if i in in_any...  28.1 us
    ppermute x7, waiting for transfers between devices, swap(): return lax.ppermute(x, 'c', SWAP)  3.61 us
  transfers between devices with their start and end apart: 7, of which 5 were waited for; matrix products, arithmetic and copies ran while one was open for 0% of the time, Pallas kernels for 6%

profile of v4, /device:TPU:0, one launch (start us, length us, event | category | flops | bytes accessed | tf_op | source)
XLA Modules:
  0.0 156.7 jit_solution(6499998875457566409)
XLA Ops:
  0.6 3.5 %shard_map.76 = bf16[64,24,768]{2,1,0:T(8,128)(2,1)} custom-call(bf16[24,384]{1,0:T(8,128)(2,1)} %hid_ref.3, bf16[24,2048]{1,0:T(8,128)(2,1)} %hid_ref.2, bf16[2048,384]{1,0:T(8,128)(2,1)} %proj_ref.1), custom_call_target="tpu_custom_call" | custom-call | tf_op jit(solution)/shard_map/pallas_call | solution.py:33
  4.1 44.7 %all_to_all.25 = bf16[64,24,768]{2,1,0:T(8,128)(2,1)S(1)} all-to-all(bf16[64,24,768]{2,1,0:T(8,128)(2,1)} %shard_map.76), channel_id=1, replica_groups=mesh['z'=4,'y'=4,'x'=4,'c'=2] {'z','y','x'}, dimensions={0} | all-to-all | bytes 4718592 | tf_op jit(solution)/shard_map/all_to_all | solution.py:311
  48.8 4.0 %shard_map.77 = (f32[1024,1536]{1,0:T(8,128)S(1)}, f32[1024,1536]{1,0:T(8,128)S(1)}, bf16[1024,384]{1,0:T(8,128)(2,1)S(1)}, bf16[1024,384]{1,0:T(8,128)(2,1)S(1)...) custom-call(bf16[384,1024]{1,0:T(8,128)(2,1)S(1)} %copy-done.1, ...), custom_call_target="tpu_custom_call" | custom-call | tf_op jit(solution)/shard_map/pallas_call | solution.py:33
  52.8 0.4 shard_map.78.turned_ref
  53.2 0.2 collective-permute-done.rows_ref
  53.4 3.9 %shard_map.79 = (f32[1024,1536]{1,0:T(8,128)S(1)}, f32[1024,1536]{1,0:T(8,128)S(1)}, f32[1024,1]{1,0:T(8,128)S(1)}, f32[8,384]{1,0:T(8,128)S(1)}) custom-call(bf16[1024,384]{1,0:T(8,128)(2,1)S(1)} %get-tuple-element.34.t_lhs, bf16[1024,384]{1,0:T(8,128)(2,1)S(1)} %get-tuple-element.35.s_lhs, bf16[1536,768]{1,0:T(8,128)(2,1)S(1)} %collective-permute-done.rows_ref, ...), custom_call_target="tpu_custom_call" | custom-call | tf_op jit(solution)/shard_map/pallas_call | solution.py:33
  57.2 0.4 collective-permute-start.1
  57.7 0.5 shard_map.80.mine_ref
  58.2 0.3 collective-permute-done.1.theirs_ref
  58.5 17.7 %all_to_all.26.got_ref = bf16[64,8,384]{2,1,0:T(8,128)(2,1)S(1)} all-to-all(bf16[64,8,384]{2,1,0:T(8,128)(2,1)S(1)} %shard_map.81), channel_id=1, replica_groups=mesh['z'=4,'y'=4,'x'=4,'c'=2] {'z','y','x'}, dimensions={0} | all-to-all | bytes 786432 | tf_op jit(solution)/shard_map/all_to_all | solution.py:311
  76.2 0.1 shard_map.82.mine_ref.part_own.part_ref
  76.3 0.3 collective-permute-start.2
  76.6 0.4 shard_map.83.turned_ref
  76.9 0.8 collective-permute-done.2.theirs_ref.part_other
  77.7 2.6 %shard_map.84 = (bf16[64,8,384]{2,1,0:T(8,128)(2,1)S(1)}, f32[1024,1]{1,0:T(8,128)}) custom-call(f32[1024,1536]{1,0:T(8,128)S(1)} %get-tuple-element.32.e_ref.own_ref.e_own, f32[1024,1536]{1,0:T(8,128)S(1)} %get-tuple-element.40.other_ref.e_ref, f32[8,384]{1,0:T(8,128)S(1)} %shard_map.82.mine_ref.part_own.part_ref, ...), custom_call_target="tpu_custom_call" | custom-call | tf_op jit(solution)/shard_map/pallas_call | solution.py:33
  80.4 16.9 %all_to_all.27.got_ref = bf16[64,8,384]{2,1,0:T(8,128)(2,1)S(1)} all-to-all(bf16[64,8,384]{2,1,0:T(8,128)(2,1)S(1)} %get-tuple-element.47), channel_id=1, replica_groups=mesh['z'=4,'y'=4,'x'=4,'c'=2] {'z','y','x'}, dimensions={0} | all-to-all | bytes 786432 | tf_op jit(solution)/shard_map/all_to_all | solution.py:311
  97.3 0.1 shard_map.85.mine_ref
  97.4 0.1 collective-permute-start.3
  97.4 1.2 collective-permute-done.3.theirs_ref
  98.6 1.9 %shard_map.86 = (bf16[64,8,384]{2,1,0:T(8,128)(2,1)S(1)}, f32[1024,1]{1,0:T(8,128)S(1)}) custom-call(f32[1024,1536]{1,0:T(8,128)S(1)} %get-tuple-element.32.e_ref.own_ref.e_own, f32[1024,1536]{1,0:T(8,128)S(1)} %get-tuple-element.40.other_ref.e_ref, f32[8,384]{1,0:T(8,128)S(1)} %shard_map.85.mine_ref, f32[8,384]{1,0:T(8,128)S(1)} %collective-permute-done.3.theirs_ref), custom_call_target="tpu_custom_call" | custom-call | tf_op jit(solution)/shard_map/pallas_call | solution.py:33
  100.5 16.9 %all_to_all.28.got_ref = bf16[64,8,384]{2,1,0:T(8,128)(2,1)S(1)} all-to-all(bf16[64,8,384]{2,1,0:T(8,128)(2,1)S(1)} %get-tuple-element.51), channel_id=1, replica_groups=mesh['z'=4,'y'=4,'x'=4,'c'=2] {'z','y','x'}, dimensions={0} | all-to-all | bytes 786432 | tf_op jit(solution)/shard_map/all_to_all | solution.py:311
  117.4 0.1 shard_map.87.mine_ref
  117.5 0.1 collective-permute-start.4
  117.6 1.2 collective-permute-done.4.theirs_ref
  118.8 4.5 %shard_map.88 = (f32[1536,384]{1,0:T(8,128)S(1)}, f32[384,1024]{1,0:T(8,128)S(1)}, f32[1,128]{1,0:T(1,128)S(1)}) custom-call(f32[1024,1536]{1,0:T(8,128)S(1)} %get-tuple-element.40.other_ref.e_ref, f32[1024,1536]{1,0:T(8,128)S(1)} %get-tuple-element.52.lg_ref, f32[1024,1]{1,0:T(8,128)S(1)} %get-tuple-element.48.cs_ref, ...), custom_call_target="tpu_custom_call" | custom-call | tf_op jit(solution)/shard_map/pallas_call | solution.py:33
  123.3 0.2 collective-permute-start.5
  123.5 0.3 collective-permute-start.6
  123.9 4.7 %shard_map.89 = (f32[1536,384]{1,0:T(8,128)S(1)}, f32[384,1024]{1,0:T(8,128)}) custom-call(f32[1024,1536]{1,0:T(8,128)S(1)} %get-tuple-element.32.e_ref.own_ref.e_own, f32[1024,1536]{1,0:T(8,128)S(1)} %get-tuple-element.33.lg_own.lg_ref, f32[1024,1]{1,0:T(8,128)S(1)} %get-tuple-element.48.cs_ref, bf16[384,1024]{1,0:T(8,128)(2,1)S(1)} %get-tuple-element.49.cols_ref, ...), custom_call_target="tpu_custom_call" | custom-call | tf_op jit(solution)/shard_map/pallas_call | solution.py:33
  128.7 0.5 shard_map.90
  129.1 0.0 copy-start.2
  129.2 26.6 %all_to_all.29.got_ref = bf16[64,80,128]{2,1,0:T(8,128)(2,1)S(1)} all-to-all(bf16[64,80,128]{2,1,0:T(8,128)(2,1)S(1)} %shard_map.90), channel_id=1, replica_groups=mesh['z'=4,'y'=4,'x'=4,'c'=2] {'z','y','x'}, dimensions={0} | all-to-all | bytes 2621440 | tf_op jit(solution)/shard_map/all_to_all | solution.py:311
  155.7 0.9 shard_map.91
  (9 shorter events, 0.1 us)
Async XLA Ops:
  4.1 44.7 %copy-start = (bf16[384,1024]{1,0:T(8,128)(2,1)S(1)}, bf16[384,1024]{1,0:T(8,128)(2,1)}, u32[]{:S(2)}) copy-start(bf16[384,1024]{1,0:T(8,128)(2,1)} %w_ref.1) | copy-start | bytes 2359300
  4.1 44.7 %copy-start.1 = (bf16[384,1024]{1,0:T(8,128)(2,1)S(1)}, bf16[384,1024]{1,0:T(8,128)(2,1)}, u32[]{:S(2)}) copy-start(bf16[384,1024]{1,0:T(8,128)(2,1)} %tw_ref.1) | copy-start | bytes 2359300
  48.8 4.5 %collective-permute-start = (bf16[1536,768]{1,0:T(8,128)(2,1)S(1)}, bf16[1536,768]{1,0:T(8,128)(2,1)S(1)}, u32[]{:S(2)}, u32[]{:S(2)}) collective-permute-start(bf16[1536,768]{1,0:T(8,128)(2,1)S(1)} %bitcast.3), channel_id=1, source_target_pairs={{0,1},{1,0},{2,3},{3,2},{4,5},{5,4},{6,7},{7,6},{8,9},{9,8},{10,11... | collective-permute-start | bytes 7077896 | tf_op jit(solution)/shard_map/ppermute | solution.py:308
  57.2 1.3 collective-permute-start.1
  76.3 1.4 collective-permute-start.2
  97.4 1.3 collective-permute-start.3
  117.5 1.3 collective-permute-start.4
  123.3 5.4 %collective-permute-start.5 = (f32[1536,384]{1,0:T(8,128)S(1)}, f32[1536,384]{1,0:T(8,128)S(1)}, u32[]{:S(2)}, u32[]{:S(2)}) collective-permute-start(f32[1536,384]{1,0:T(8,128)S(1)} %get-tuple-element.56), channel_id=1, source_target_pairs={{0,1},{1,0},{2,3},{3,2},{4,5},{5,4},{6,7},{7,6},{8,9},{9,8},{10,11... | collective-permute-start | bytes 7077896 | tf_op jit(solution)/shard_map/ppermute | solution.py:308
  123.5 5.1 %collective-permute-start.6 = (f32[1,128]{1,0:T(1,128)S(1)}, f32[1,128]{1,0:T(1,128)S(1)}, u32[]{:S(2)}, u32[]{:S(2)}) collective-permute-start(f32[1,128]{1,0:T(1,128)S(1)} %get-tuple-element.57.loss_a), channel_id=1, source_target_pairs={{0,1},{1,0},{2,3},{3,2},{4,5},{5,4},{6,7},{7,6},{8,9},{9,8},{10,11... | collective-permute-start | bytes 1544 | tf_op jit(solution)/shard_map/ppermute | solution.py:308
  129.1 26.6 %copy-start.2 = (bf16[24,384]{1,0:T(8,128)(2,1)S(1)}, bf16[24,384]{1,0:T(8,128)(2,1)}, u32[]{:S(2)}) copy-start(bf16[24,384]{1,0:T(8,128)(2,1)} %hid_ref.3) | copy-start | bytes 55300

commit v5 on v4

--- a/solution.py
+++ b/solution.py
@@ -56,10 +56,6 @@
     return jnp.concatenate([block[j : j + 1, :] for j in range(block.shape[0])], axis=1)
 
 
-def half_rows(mine, theirs):
-    return flat(jnp.concatenate([mine, theirs], axis=0))
-
-
 def total_row(mine, theirs):
     return flat(mine + jnp.concatenate([theirs[4:8, :], theirs[0:4, :]], axis=0))
 
@@ -70,7 +66,7 @@
     return wide * inv, inv
 
 
-def rows_kernel(s_ref, hid_ref, proj_ref, send_ref, s_buf, hid_buf, proj_buf, sem):
+def rows_kernel(s_ref, hid_ref, proj_ref, send_ref, s_out_ref, s_buf, hid_buf, proj_buf, sem):
     parts = proj_buf.shape[0]
     depth = proj_buf.shape[1]
     first = pltpu.make_async_copy(s_ref, s_buf, sem.at[0])
@@ -86,6 +82,7 @@
     first.wait()
     wide = s_buf[...].astype(F32)
     unit = wide * lax.rsqrt(jnp.sum(wide * wide, axis=1, keepdims=True) + EPS)
+    s_out_ref[...] = unit.astype(BF16)
     second.wait()
     t_hid = jnp.zeros((hid_buf.shape[0], proj_buf.shape[2]), F32)
     for i, copy in enumerate(copies):
@@ -94,7 +91,7 @@
             hid_buf[:, i * depth : (i + 1) * depth], proj_buf[i], preferred_element_type=F32
         )
     t_bot = t_hid * lax.rsqrt(jnp.sum(t_hid * t_hid, axis=1, keepdims=True) + EPS)
-    spread(jnp.concatenate([t_bot, unit], axis=1), send_ref)
+    spread(t_bot, send_ref)
 
 
 def sum_kernel(got_ref, out_ref):
@@ -105,56 +102,80 @@
     return [slice(j, j + size) for j in range(0, total, size)]
 
 
-def own_kernel(tw_ref, sw_ref, rows_ref, e_ref, lg_ref, t_lhs, s_lhs, s_cols, sums_ref, part_ref):
-    part_ref[...] = jnp.zeros_like(part_ref)
-    for at in chunks(tw_ref.shape[1], CHUNK):
-        t_lhs[at, :] = columns(tw_ref[:, at])[0].T.astype(BF16)
-        unit = columns(sw_ref[:, at])[0]
-        s_cols[:, at] = unit.astype(BF16)
-        s_lhs[at, :] = unit.T.astype(BF16)
-        sums_ref[at, :] = products(at, t_lhs, s_lhs, rows_ref, e_ref, lg_ref, part_ref)
-
-
-def products(at, t_lhs, s_lhs, rows_ref, e_ref, lg_ref, part_ref):
-    bot = t_lhs.shape[1]
-    expo = jnp.exp(
-        lax.dot_general(t_lhs[at, :], rows_ref[:, :bot], NT, preferred_element_type=F32) * (1.0 / teacher_temp)
-    )
+def expo_block(at, lhs_ref, rows_ref, e_ref):
+    prod = lax.dot_general(lhs_ref[at, :], rows_ref[...], NT, preferred_element_type=F32)
+    expo = jnp.exp(prod * (1.0 / teacher_temp))
     e_ref[at, :] = expo
-    logits = lax.dot_general(s_lhs[at, :], rows_ref[:, bot:], NT, preferred_element_type=F32) * (1.0 / student_temp)
-    lg_ref[at, :] = logits
-    part_ref[...] += jnp.sum(jnp.exp(logits).reshape(CHUNK // 8, 8, logits.shape[1]), axis=0)
     return jnp.sum(expo, axis=1, keepdims=True)
 
 
-def other_kernel(total_cols, t_lhs, s_lhs, rows_ref, sums_ref, e_ref, lg_ref, cs_ref, out_ref, part, acc):
+def teacher_own_kernel(w_ref, rows_ref, e_ref, lhs_ref, sums_ref):
+    for at in chunks(w_ref.shape[1], CHUNK):
+        lhs_ref[at, :] = columns(w_ref[:, at])[0].T.astype(BF16)
+        sums_ref[at, :] = expo_block(at, lhs_ref, rows_ref, e_ref)
+
+
+def teacher_other_kernel(total_cols, lhs_ref, rows_ref, e_own, sums_ref, s_ref, e_ref, out_ref, acc):
+    half = rows_ref.shape[0]
+    acc[...] = jnp.zeros_like(acc)
+    for at in chunks(lhs_ref.shape[0], CHUNK):
+        scale = 1.0 / (total_cols * (sums_ref[at, :] + expo_block(at, lhs_ref, rows_ref, e_ref)))
+        row_pass(e_own.at[at, :], scale, acc.at[:, :half])
+        row_pass(e_ref.at[at, :], scale, acc.at[:, half:])
+    sums = fold(jnp.sum(acc[...], axis=0, keepdims=True))
+    spread(jnp.concatenate([sums, s_ref[...].astype(F32)], axis=0), out_ref)
+
+
+def open_kernel(got_ref, sums_ref, rows_ref):
+    total = jnp.zeros(sums_ref.shape, F32)
+    for i in range(got_ref.shape[0]):
+        piece = got_ref[i].astype(F32)
+        total = total + piece[0:8, :]
+        rows_ref[i] = piece[8:, :].astype(BF16)
+    sums_ref[...] = total
+
+
+def fold_half(part):
+    row = jnp.sum(part, axis=0, keepdims=True)
+    width = row.shape[1] // 4
+    return jnp.concatenate([row[:, j * width : (j + 1) * width] for j in range(4)], axis=0)
+
+
+def student_columns_kernel(w_ref, lhs_ref, cols_ref):
+    for at in chunks(w_ref.shape[1], CHUNK):
+        unit = columns(w_ref[:, at])[0]
+        cols_ref[:, at] = unit.astype(BF16)
+        lhs_ref[at, :] = unit.T.astype(BF16)
+
+
+def student_kernel(start, lhs_ref, rows_ref, lg_ref, out_ref, part):
     part[...] = jnp.zeros_like(part)
-    acc[...] = jnp.zeros_like(acc)
-    for at in chunks(t_lhs.shape[0], CHUNK):
-        sums = sums_ref[at, :] + products(at, t_lhs, s_lhs, rows_ref, e_ref, lg_ref, part)
-        scale = 1.0 / (total_cols * sums)
-        cs_ref[at, :] = scale
-        row_pass(e_ref.at[at, :], scale, acc)
-    out_ref[...] = fold_pair(acc[...], part[...])
-
-
-def fold_pair(rows, parts):
-    both = jnp.concatenate([jnp.sum(rows, axis=0, keepdims=True), jnp.sum(parts, axis=0, keepdims=True)], axis=1)
-    return fold(both)
-
-
-def own_rows_kernel(e_ref, cs_ref, part_ref, out_ref, acc):
-    acc[...] = jnp.zeros_like(acc)
-    row_pass(e_ref, cs_ref[...], acc)
-    out_ref[...] = fold_pair(acc[...], part_ref[...])
-
-
-def send_kernel(mine_ref, theirs_ref, out_ref):
-    spread(mine_ref[...] + theirs_ref[...], out_ref)
+    for at in chunks(lg_ref.shape[0], CHUNK):
+        lhs = lhs_ref[start + at.start : start + at.stop, :]
+        prod = lax.dot_general(lhs, rows_ref[...], NT, preferred_element_type=F32)
+        logits = prod * (1.0 / student_temp)
+        lg_ref[at, :] = logits
+        part[...] += jnp.sum(jnp.exp(logits).reshape(CHUNK // 8, 8, logits.shape[1]), axis=0)
+    out_ref[...] = fold_half(part[...])
+
+
+def pair_kernel(row_ref, part_a, part_b, out_ref):
+    out_ref[...] = jnp.concatenate([row_ref[4:8, :], part_a[...] + part_b[...]], axis=0)
+
+
+def send_kernel(row_ref, part_a, part_b, theirs_ref, out_ref):
+    spread(jnp.concatenate([row_ref[0:4, :], part_a[...] + part_b[...]], axis=0) + theirs_ref[...], out_ref)
+
+
+def pick(refs, at):
+    first = refs[0].shape[0]
+    if at.stop <= first:
+        return refs[0], at
+    return refs[1], slice(at.start - first, at.stop - first)
 
 
 def turn_kernel(rows_ref, out_ref):
-    out_ref[...] = rows_ref[:, out_ref.shape[0] :].T
+    out_ref[...] = rows_ref[...].T
 
 
 def row_pass(block_ref, scale, acc):
@@ -165,11 +186,8 @@
         acc[:, lanes] += jnp.sum(block_ref[:, lanes].reshape(rows // 8, 8, 512) * scale, axis=0)
 
 
-def pass_kernel(total_cols, images, first, own_ref, other_ref, mine_ref, theirs_ref, out_ref, cs_ref, weight, acc):
-    if first:
-        total = half_rows(mine_ref[0:4, :], theirs_ref[0:4, :])
-    else:
-        total = total_row(mine_ref[...], theirs_ref[...])
+def pass_kernel(total_cols, images, own_ref, other_ref, mine_ref, theirs_ref, out_ref, cs_ref, weight, acc):
+    total = total_row(mine_ref[...], theirs_ref[...])
     weight[...] = jnp.broadcast_to(1.0 / (images * total), weight.shape)
     acc[...] = jnp.zeros_like(acc)
     protos, half = own_ref.shape
@@ -187,7 +205,11 @@
         return 0
 
     lax.fori_loop(0, protos // BLOCK, step, 0)
-    spread(fold(jnp.sum(acc[...], axis=0, keepdims=True)), out_ref)
+    piece = fold(jnp.sum(acc[...], axis=0, keepdims=True))
+    if len(out_ref.shape) == 3:
+        spread(piece, out_ref)
+    else:
+        out_ref[...] = piece
 
 
 STRIP = 32
@@ -206,8 +228,10 @@
         for at in chunks(protos, STRIP):
             for expo, logits, acc in cross:
                 scaled = expo[at, lanes] * cs_ref[at, :]
-                acc[:, lanes] += jnp.sum((scaled * logits[at, lanes]).reshape(folded), axis=0)
-            logits = lg_ref[at, lanes]
+                ref, place = pick(logits, at)
+                acc[:, lanes] += jnp.sum((scaled * ref[place, lanes]).reshape(folded), axis=0)
+            ref, place = pick(lg_ref, at)
+            logits = ref[place, lanes]
             scaled = e_ref[at, lanes] * cs_ref[at, :]
             powers = jnp.exp(logits).reshape(folded) * rows[0:8, lanes][None]
             target = scaled.reshape(folded) * rows[8:16, lanes][None]
@@ -233,26 +257,28 @@
 
 
 def grad_other_kernel(
-    devices, e_ref, lg_ref, cs_ref, cols_ref, turned_ref, part_own, part_other, mine_ref, theirs_ref, e_own, lg_own,
+    devices, e_ref, lg_a, lg_b, cs_ref, cols_ref, turned_ref, mine_ref, theirs_ref, e_own, lg_own_a, lg_own_b,
     db_ref, unit_sum, loss_ref, g, rows, acc, acc_own
 ):
-    row = flat(mine_ref[4:8, :] + theirs_ref[0:4, :])
-    part = flat(part_other[4:8, :])
-    cross = ((e_ref, lg_ref, acc), (e_own, lg_own, acc_own))
+    row = flat(theirs_ref[0:4, :])
+    part = flat(theirs_ref[4:8, :])
+    lg_ref = (lg_a, lg_b)
+    cross = ((e_ref, lg_ref, acc), (e_own, (lg_own_a, lg_own_b), acc_own))
     half_gradients(row, part, e_ref, lg_ref, cs_ref, cols_ref, turned_ref, db_ref, unit_sum, None, g, rows, cross)
-    parts = jnp.log(part) + jnp.log(flat(part_own[4:8, :]))
-    row_own = flat(mine_ref[0:4, :] + theirs_ref[4:8, :])
+    parts = jnp.log(part) + jnp.log(flat(mine_ref[4:8, :]))
+    row_own = flat(mine_ref[0:4, :])
     crossed = jnp.sum(acc[...], axis=0, keepdims=True) / row + jnp.sum(acc_own[...], axis=0, keepdims=True) / row_own
     terms = parts * (1.0 / devices) - crossed
     loss_ref[...] = sum(terms[:, lanes] for lanes in chunks(terms.shape[1], 128))
 
 
 def grad_own_kernel(
-    e_ref, lg_ref, cs_ref, cols_ref, turned_ref, part_ref, mine_ref, theirs_ref, other_sum, w_ref,
+    e_ref, lg_a, lg_b, cs_ref, cols_ref, turned_ref, mine_ref, other_sum, w_ref,
     db_ref, dp_ref, g, rows, unit_sum, out_buf, sem
 ):
-    row = flat(mine_ref[0:4, :] + theirs_ref[4:8, :])
-    part = flat(part_ref[4:8, :])
+    row = flat(mine_ref[0:4, :])
+    part = flat(mine_ref[4:8, :])
+    lg_ref = (lg_a, lg_b)
     half_gradients(row, part, e_ref, lg_ref, cs_ref, cols_ref, turned_ref, db_ref, unit_sum, other_sum, g, rows, ())
     copies = []
     for j, at in enumerate(chunks(w_ref.shape[1], CHUNK)):
@@ -314,69 +340,92 @@
         mine = call(sum_kernel, sds((rows, images // 8), F32), (exchange(x),), 2)
         return mine, swap(mine)
 
-    both = call(
+    t_send, s_bot = call(
         rows_kernel,
-        sds((chips, rows_dev, 2 * bot), BF16),
+        (sds((chips, rows_dev, bot), BF16), sds((rows_dev, bot), BF16)),
         (student_hidden, teacher_hidden, teacher_proj),
         60,
         [
             pltpu.VMEM(student_hidden.shape, BF16),
             pltpu.VMEM(teacher_hidden.shape, BF16),
-            pltpu.VMEM((4, teacher_proj.shape[0] // 4, bot), BF16),
-            pltpu.SemaphoreType.DMA((6,)),
+            pltpu.VMEM((2, teacher_proj.shape[0] // 2, bot), BF16),
+            pltpu.SemaphoreType.DMA((4,)),
         ],
         in_any=(0, 1, 2),
     )
-    own = exchange(both).reshape(half, 2 * bot)
-    other = swap(own)
+    t_own = exchange(t_send).reshape(half, bot)
+    t_other = swap(t_own)
 
     matrix = sds((protos, half), F32)
     lhs = sds((protos, bot), BF16)
     column = sds((protos, 1), F32)
-    part8 = sds((8, half), F32)
+    turned = sds((bot, half), BF16)
+    vec8 = sds((8, images // 8), F32)
+    vec4 = sds((4, images // 8), F32)
+    send8 = sds((chips, 8, images // 8), BF16)
     fold8 = pltpu.VMEM((8, images), F32)
-    e_own, lg_own, t_lhs, s_lhs, s_cols, sums, part = call(
-        own_kernel,
-        (matrix, matrix, lhs, lhs, sds((bot, protos), BF16), column, part8),
-        (teacher_protos, student_protos, own),
+    half_acc = pltpu.VMEM((8, half), F32)
+    scales = pltpu.VMEM((protos, 1), F32)
+
+    e_own, t_lhs, sums = call(teacher_own_kernel, (matrix, lhs, column), (teacher_protos, t_own), 8)
+    sums, student_late = lax.optimization_barrier((sums, student_protos))
+    s_lhs, s_cols = call(student_columns_kernel, (lhs, sds((bot, protos), BF16)), (student_late,), 8)
+    t_other, s_lhs, s_cols = lax.optimization_barrier((t_other, s_lhs, s_cols))
+    e_other, sent = call(
+        functools.partial(teacher_other_kernel, total_cols),
+        (matrix, sds((chips, 8 + rows_dev, bot), BF16)),
+        (t_lhs, t_other, e_own, sums, s_bot),
         8,
-    )
-    half8 = sds((8, images // 8), F32)
-    send8 = sds((chips, 8, images // 8), BF16)
-    half_acc = pltpu.VMEM((8, half), F32)
-    part, own_late = lax.optimization_barrier((part, own))
-    turned_own = call(turn_kernel, sds((bot, half), BF16), (own_late,), 2)
-    other, turned_own = lax.optimization_barrier((other, turned_own))
-    e_other, lg_other, col_scale, pair_other = call(
-        functools.partial(other_kernel, total_cols),
-        (matrix, matrix, column, half8),
-        (t_lhs, s_lhs, other, sums),
-        8,
-        [half_acc, half_acc],
-    )
-    theirs = swap(pair_other)
-    pair_own = call(own_rows_kernel, half8, (e_own, col_scale, part), 4, [half_acc])
-    first = row_sums(call(send_kernel, send8, (pair_own, theirs), 2), 8)
-    kept, late = lax.optimization_barrier((first[0], other))
-    turned_other = call(turn_kernel, sds((bot, half), BF16), (late,), 2)
-    theirs, turned_other = lax.optimization_barrier((first[1], turned_other))
-    first = (kept, theirs)
-    sums = first
-    for sweep in range(1, ITERS):
-        sent, col_scale = call(
-            functools.partial(pass_kernel, total_cols, images, sweep == 1),
-            (send8, column),
-            (e_own, e_other) + sums,
-            4,
-            [fold8, fold8],
-        )
-        sums = row_sums(sent, 8)
+        [fold8],
+    )
+    mine, s_own = call(open_kernel, (vec8, sds((chips, rows_dev, bot), BF16)), (exchange(sent),), 4)
+    theirs = swap(mine)
+    s_own = s_own.reshape(half, bot)
+
+    def student(start, stop, rows):
+        shapes = (sds((stop - start, half), F32), vec4)
+        return call(functools.partial(student_kernel, start), shapes, (s_lhs, rows), 8, [half_acc])
+
+    split = protos * 3 // 4
+    lg_own_a, part_own = student(0, split, s_own)
+    theirs, part_own, s_late = lax.optimization_barrier((theirs, part_own, s_own))
+    s_other = swap(s_late)
+    (sent,) = call(
+        functools.partial(pass_kernel, total_cols, images),
+        (send8,),
+        (e_own, e_other, mine, theirs),
+        4,
+        [scales, fold8, fold8],
+    )
+    mine, theirs = row_sums(sent, 8)
+    late, s_late = lax.optimization_barrier((mine, s_other))
+    lg_a, part_other = student(0, split, s_late)
+    theirs, part_other = lax.optimization_barrier((theirs, part_other))
+    row, col_scale = call(
+        functools.partial(pass_kernel, total_cols, images),
+        (vec8, column),
+        (e_own, e_other, late, theirs),
+        4,
+        [fold8, fold8],
+    )
+    row, s_late = lax.optimization_barrier((row, s_late))
+    lg_b, part_rest = student(split, protos, s_late)
+    pair_other = call(pair_kernel, vec8, (row, part_other, part_rest), 2)
+    pair_theirs = swap(pair_other)
+    pair_other, own_late = lax.optimization_barrier((pair_other, s_own))
+    lg_own_b, part_own_rest = student(split, protos, own_late)
+    pair_theirs, part_own_rest = lax.optimization_barrier((pair_theirs, part_own_rest))
+    mine, theirs = row_sums(call(send_kernel, send8, (row, part_own, part_own_rest, pair_theirs), 2), 8)
+    mine, own_late, other_late = lax.optimization_barrier((mine, s_own, s_other))
+    turned_own = call(turn_kernel, turned, (own_late,), 2)
+    turned_other = call(turn_kernel, turned, (other_late,), 2)
+    theirs, turned_own, turned_other = lax.optimization_barrier((theirs, turned_own, turned_other))
     tile = sds((1, 128), F32)
     grads = [pltpu.VMEM((protos, half), BF16), pltpu.VMEM((16, half), F32)]
     d_other, unit_sum, loss_mine = call(
         functools.partial(grad_other_kernel, 2 * chips),
         (sds((half, bot), F32), sds((bot, protos), F32), tile),
-        (e_other, lg_other, col_scale, s_cols, turned_other) + first + sums + (e_own, lg_own),
+        (e_other, lg_a, lg_b, col_scale, s_cols, turned_other, mine, theirs, e_own, lg_own_a, lg_own_b),
         8,
         grads + [half_acc, half_acc],
     )
@@ -386,7 +435,7 @@
     d_mine, d_protos = call(
         grad_own_kernel,
         (sds((half, bot), F32), sds((bot, protos), F32)),
-        (e_own, lg_own, col_scale, s_cols, turned_own, first[0]) + sums + (unit_sum, student_protos),
+        (e_own, lg_own_a, lg_own_b, col_scale, s_cols, turned_own, mine, unit_sum, student_protos),
         12,
         grads + [whole, whole, pltpu.SemaphoreType.DMA((protos // CHUNK,))],
         out_any=(1,),

time: 157 us -> 155 us (0.987)
  waiting for transfers between devices: 3.61 us -> 0.98 us
    ppermute x7 -> x8, waiting for transfers between devices: 3.61 us -> 0.98 us  [swap(): return lax.ppermute(x, 'c', SWAP)]
    pallas_call x16 -> x21, Pallas kernels: 28.1 us -> 28.5 us  [call(): pl.pallas_call(kernel, out_shape=out_shape, in_specs=[ANY if i in in_any...]
  transfers between devices with their start and end apart: 7 -> 8, of which waited for: 5 -> 3; matrix products, arithmetic and copies ran while one was open for 0% -> 0% of each run, Pallas kernels for 6% -> 9%
where the time goes in v5:
time: 155 us
  blocking collectives  122 us (79%)
  Pallas kernels  28.5 us (18%)
  starting transfers between devices  2.15 us (1%)
    all_to_all x5, blocking collectives, exchange(): return lax.all_to_all(x, CHIPS, 0, 0)  122 us
    pallas_call x21, Pallas kernels, call(): pl.pallas_call(kernel, out_shape=out_shape, in_specs=[ANY if i in in_any...  28.5 us
  transfers between devices with their start and end apart: 8, of which 3 were waited for; matrix products, arithmetic and copies ran while one was open for 0% of the time, Pallas kernels for 9%

profile of v5, /device:TPU:0, one launch (start us, length us, event | category | flops | bytes accessed | tf_op | source)
XLA Modules:
  0.0 155.0 jit_solution(15746810735310870518)
XLA Ops:
  0.6 3.0 %shard_map.76 = (bf16[64,24,384]{2,1,0:T(8,128)(2,1)}, bf16[24,384]{1,0:T(8,128)(2,1)}) custom-call(bf16[24,384]{1,0:T(8,128)(2,1)} %hid_ref.3, bf16[24,2048]{1,0:T(8,128)(2,1)} %hid_ref.2, bf16[2048,384]{1,0:T(8,128)(2,1)} %proj_ref.1), custom_call_target="tpu_custom_call" | custom-call | tf_op jit(solution)/shard_map/pallas_call | solution.py:33
  3.7 31.9 %all_to_all.25 = bf16[64,24,384]{2,1,0:T(8,128)(2,1)S(1)} all-to-all(bf16[64,24,384]{2,1,0:T(8,128)(2,1)} %get-tuple-element.54), channel_id=1, replica_groups=mesh['z'=4,'y'=4,'x'=4,'c'=2] {'z','y','x'}, dimensions={0} | all-to-all | bytes 2359296 | tf_op jit(solution)/shard_map/all_to_all | solution.py:337
  35.6 2.1 %shard_map.77 = (f32[1024,1536]{1,0:T(8,128)S(1)}, bf16[1024,384]{1,0:T(8,128)(2,1)S(1)}, f32[1024,1]{1,0:T(8,128)S(1)}) custom-call(bf16[384,1024]{1,0:T(8,128)(2,1)S(1)} %copy-done.1, bf16[1536,384]{1,0:T(8,128)(2,1)S(1)} %bitcast.9), custom_call_target="tpu_custom_call" | custom-call | tf_op jit(solution)/shard_map/pallas_call | solution.py:33
  37.7 0.4 shard_map.78
  38.1 0.3 collective-permute-done.rows_ref
  38.4 3.1 %shard_map.79 = (f32[1024,1536]{1,0:T(8,128)S(1)}, bf16[64,32,384]{2,1,0:T(8,128)(2,1)S(1)}) custom-call(bf16[1024,384]{1,0:T(8,128)(2,1)S(1)} %get-tuple-element.61.lhs_ref, bf16[1536,384]{1,0:T(8,128)(2,1)S(1)} %collective-permute-done.rows_ref, f32[1024,1536]{1,0:T(8,128)S(1)} %get-tuple-element.55.e_own.own_ref.e_ref, ...), custom_call_target="tpu_custom_call" | custom-call | tf_op jit(solution)/shard_map/pallas_call | solution.py:33
  41.5 29.4 %all_to_all.26.got_ref = bf16[64,32,384]{2,1,0:T(8,128)(2,1)S(1)} all-to-all(bf16[64,32,384]{2,1,0:T(8,128)(2,1)S(1)} %get-tuple-element.65), channel_id=1, replica_groups=mesh['z'=4,'y'=4,'x'=4,'c'=2] {'z','y','x'}, dimensions={0} | all-to-all | bytes 3145728 | tf_op jit(solution)/shard_map/all_to_all | solution.py:337
  71.0 0.2 shard_map.80
  71.3 1.5 shard_map.81
  72.8 0.6 collective-permute-start.2
  73.3 2.0 %shard_map.82 = bf16[64,8,384]{2,1,0:T(8,128)(2,1)S(1)} custom-call(f32[1024,1536]{1,0:T(8,128)S(1)} %get-tuple-element.55.e_own.own_ref.e_ref, f32[1024,1536]{1,0:T(8,128)S(1)} %get-tuple-element.68.other_ref.e_ref, f32[8,384]{1,0:T(8,128)S(1)} %get-tuple-element.69.mine_ref, f32[8,384]{1,0:T(8,128)S(1)} %collective-permute-done.1.theirs_ref), custom_call_target="tpu_custom_call" | custom-call | tf_op jit(solution)/shard_map/pallas_call | solution.py:33
  75.3 17.3 %all_to_all.27.got_ref = bf16[64,8,384]{2,1,0:T(8,128)(2,1)S(1)} all-to-all(bf16[64,8,384]{2,1,0:T(8,128)(2,1)S(1)} %shard_map.82), channel_id=1, replica_groups=mesh['z'=4,'y'=4,'x'=4,'c'=2] {'z','y','x'}, dimensions={0} | all-to-all | bytes 786432 | tf_op jit(solution)/shard_map/all_to_all | solution.py:337
  92.6 0.1 shard_map.83.mine_ref
  92.7 0.3 collective-permute-start.3
  93.0 1.5 shard_map.84
  94.4 1.9 %shard_map.85 = (f32[8,384]{1,0:T(8,128)S(1)}, f32[1024,1]{1,0:T(8,128)S(1)}) custom-call(f32[1024,1536]{1,0:T(8,128)S(1)} %get-tuple-element.55.e_own.own_ref.e_ref, f32[1024,1536]{1,0:T(8,128)S(1)} %get-tuple-element.68.other_ref.e_ref, f32[8,384]{1,0:T(8,128)S(1)} %shard_map.83.mine_ref, f32[8,384]{1,0:T(8,128)S(1)} %collective-permute-done.3.theirs_ref), custom_call_target="tpu_custom_call" | custom-call | tf_op jit(solution)/shard_map/pallas_call | solution.py:33
  96.4 0.6 shard_map.86
  97.0 0.6 collective-permute-start.4
  97.6 0.6 shard_map.88
  98.2 0.2 collective-permute-done.4.theirs_ref
  98.5 17.1 %all_to_all.28.got_ref = bf16[64,8,384]{2,1,0:T(8,128)(2,1)S(1)} all-to-all(bf16[64,8,384]{2,1,0:T(8,128)(2,1)S(1)} %shard_map.89), channel_id=1, replica_groups=mesh['z'=4,'y'=4,'x'=4,'c'=2] {'z','y','x'}, dimensions={0} | all-to-all | bytes 786432 | tf_op jit(solution)/shard_map/all_to_all | solution.py:337
  115.6 0.1 shard_map.90.mine_ref
  115.7 0.4 shard_map.91.turned_ref
  116.1 0.4 shard_map.92.turned_ref
  116.5 0.4 collective-permute-done.5.theirs_ref
  116.9 4.7 %shard_map.93 = (f32[1536,384]{1,0:T(8,128)S(1)}, f32[384,1024]{1,0:T(8,128)S(1)}, f32[1,128]{1,0:T(1,128)S(1)}) custom-call(f32[1024,1536]{1,0:T(8,128)S(1)} %get-tuple-element.68.other_ref.e_ref, f32[768,1536]{1,0:T(8,128)S(1)} %get-tuple-element.94.lg_a, f32[256,1536]{1,0:T(8,128)S(1)} %get-tuple-element.95.lg_b, f32[1024,1]{1,0:T(8,128)S(1)} %get-tuple-element.84.cs_ref, ...), custom_call_target="tpu_custom_call" | custom-call | tf_op jit(solution)/shard_map/pallas_call | solution.py:33
  121.6 0.2 collective-permute-start.6
  121.8 0.3 collective-permute-start.7
  122.2 4.7 %shard_map.94 = (f32[1536,384]{1,0:T(8,128)S(1)}, f32[384,1024]{1,0:T(8,128)}) custom-call(f32[1024,1536]{1,0:T(8,128)S(1)} %get-tuple-element.55.e_own.own_ref.e_ref, f32[768,1536]{1,0:T(8,128)S(1)} %get-tuple-element.67.lg_own_a.lg_a, f32[256,1536]{1,0:T(8,128)S(1)} %get-tuple-element.83.lg_own_b.lg_b, f32[1024,1]{1,0:T(8,128)S(1)} %get-tuple-element.84.cs_ref, ...), custom_call_target="tpu_custom_call" | custom-call | tf_op jit(solution)/shard_map/pallas_call | solution.py:33
  126.9 0.4 shard_map.95
  127.3 26.7 %all_to_all.29.got_ref = bf16[64,80,128]{2,1,0:T(8,128)(2,1)S(1)} all-to-all(bf16[64,80,128]{2,1,0:T(8,128)(2,1)S(1)} %shard_map.95), channel_id=1, replica_groups=mesh['z'=4,'y'=4,'x'=4,'c'=2] {'z','y','x'}, dimensions={0} | all-to-all | bytes 2621440 | tf_op jit(solution)/shard_map/all_to_all | solution.py:337
  154.1 0.9 shard_map.96
  (18 shorter events, 0.2 us)
Async XLA Ops:
  3.7 31.9 %copy-start.1 = (bf16[384,1024]{1,0:T(8,128)(2,1)S(1)}, bf16[384,1024]{1,0:T(8,128)(2,1)}, u32[]{:S(2)}) copy-start(bf16[384,1024]{1,0:T(8,128)(2,1)} %w_ref.2) | copy-start | bytes 2359300
  35.6 2.1 %copy-start = (bf16[384,1024]{1,0:T(8,128)(2,1)S(1)}, bf16[384,1024]{1,0:T(8,128)(2,1)}, u32[]{:S(2)}) copy-start(bf16[384,1024]{1,0:T(8,128)(2,1)} %w_ref.4) | copy-start | bytes 2359300
  35.6 2.9 %copy-start.3 = (bf16[24,384]{1,0:T(8,128)(2,1)S(1)}, bf16[24,384]{1,0:T(8,128)(2,1)}, u32[]{:S(2)}) copy-start(bf16[24,384]{1,0:T(8,128)(2,1)} %get-tuple-element.64.s_ref) | copy-start | bytes 55300
  35.6 2.8 %collective-permute-start = (bf16[1536,384]{1,0:T(8,128)(2,1)S(1)}, bf16[1536,384]{1,0:T(8,128)(2,1)S(1)}, u32[]{:S(2)}, u32[]{:S(2)}) collective-permute-start(bf16[1536,384]{1,0:T(8,128)(2,1)S(1)} %bitcast.8), channel_id=1, source_target_pairs={{0,1},{1,0},{2,3},{3,2},{4,5},{5,4},{6,7},{7,6},{8,9},{9,8},{10,11... | collective-permute-start | bytes 3538952 | tf_op jit(solution)/shard_map/ppermute | solution.py:334
  71.2 1.6 %collective-permute-start.1 = (f32[8,384]{1,0:T(8,128)S(1)}, f32[8,384]{1,0:T(8,128)S(1)}, u32[]{:S(2)}, u32[]{:S(2)}) collective-permute-start(f32[8,384]{1,0:T(8,128)S(1)} %get-tuple-element.69.mine_ref), channel_id=1, source_target_pairs={{0,1},{1,0},{2,3},{3,2},{4,5},{5,4},{6,7},{7,6},{8,9},{9,8},{10,11... | collective-permute-start | bytes 36872 | tf_op jit(solution)/shard_map/ppermute | solution.py:334
  72.8 20.2 %collective-permute-start.2 = (bf16[1536,384]{1,0:T(8,128)(2,1)S(1)}, bf16[1536,384]{1,0:T(8,128)(2,1)S(1)}, u32[]{:S(2)}, u32[]{:S(2)}) collective-permute-start(bf16[1536,384]{1,0:T(8,128)(2,1)S(1)} %bitcast.5), channel_id=1, source_target_pairs={{0,1},{1,0},{2,3},{3,2},{4,5},{5,4},{6,7},{7,6},{8,9},{9,8},{10,11... | collective-permute-start | bytes 3538952 | tf_op jit(solution)/shard_map/ppermute | solution.py:334
  92.7 1.7 %collective-permute-start.3 = (f32[8,384]{1,0:T(8,128)S(1)}, f32[8,384]{1,0:T(8,128)S(1)}, u32[]{:S(2)}, u32[]{:S(2)}) collective-permute-start(f32[8,384]{1,0:T(8,128)S(1)} %shard_map.83.mine_ref), channel_id=1, source_target_pairs={{0,1},{1,0},{2,3},{3,2},{4,5},{5,4},{6,7},{7,6},{8,9},{9,8},{10,11... | collective-permute-start | bytes 36872 | tf_op jit(solution)/shard_map/ppermute | solution.py:334
  97.0 1.4 collective-permute-start.4
  115.6 1.3 collective-permute-start.5
  121.6 5.3 %collective-permute-start.6 = (f32[1536,384]{1,0:T(8,128)S(1)}, f32[1536,384]{1,0:T(8,128)S(1)}, u32[]{:S(2)}, u32[]{:S(2)}) collective-permute-start(f32[1536,384]{1,0:T(8,128)S(1)} %get-tuple-element.100), channel_id=1, source_target_pairs={{0,1},{1,0},{2,3},{3,2},{4,5},{5,4},{6,7},{7,6},{8,9},{9,8},{10,11... | collective-permute-start | bytes 7077896 | tf_op jit(solution)/shard_map/ppermute | solution.py:334
  121.8 5.1 %collective-permute-start.7 = (f32[1,128]{1,0:T(1,128)S(1)}, f32[1,128]{1,0:T(1,128)S(1)}, u32[]{:S(2)}, u32[]{:S(2)}) collective-permute-start(f32[1,128]{1,0:T(1,128)S(1)} %get-tuple-element.101.loss_a), channel_id=1, source_target_pairs={{0,1},{1,0},{2,3},{3,2},{4,5},{5,4},{6,7},{7,6},{8,9},{9,8},{10,11... | collective-permute-start | bytes 1544 | tf_op jit(solution)/shard_map/ppermute | solution.py:334
  127.3 26.7 %copy-start.2 = (bf16[24,384]{1,0:T(8,128)(2,1)S(1)}, bf16[24,384]{1,0:T(8,128)(2,1)}, u32[]{:S(2)}) copy-start(bf16[24,384]{1,0:T(8,128)(2,1)} %hid_ref.3) | copy-start | bytes 55300

commit v6 on v5

--- a/solution.py
+++ b/solution.py
@@ -159,8 +159,8 @@
     out_ref[...] = fold_half(part[...])
 
 
-def pair_kernel(row_ref, part_a, part_b, out_ref):
-    out_ref[...] = jnp.concatenate([row_ref[4:8, :], part_a[...] + part_b[...]], axis=0)
+def pair_kernel(row_ref, part_ref, out_ref):
+    out_ref[...] = jnp.concatenate([row_ref[4:8, :], part_ref[...]], axis=0)
 
 
 def send_kernel(row_ref, part_a, part_b, theirs_ref, out_ref):
@@ -168,6 +168,8 @@
 
 
 def pick(refs, at):
+    if len(refs) == 1:
+        return refs[0], at
     first = refs[0].shape[0]
     if at.stop <= first:
         return refs[0], at
@@ -216,7 +218,9 @@
 DEPTH = 512
 
 
-def half_gradients(row, part, e_ref, lg_ref, cs_ref, cols_ref, turned_ref, db_ref, unit_sum, start, g, rows, cross):
+def half_gradients(
+    row, part, e_ref, lg_ref, cs_ref, cols_ref, turned_ref, db_ref, unit_sum, start, g, rows, cross, last=None
+):
     protos, half = e_ref.shape
     rows[0:8, :] = jnp.broadcast_to((1.0 / student_temp) / part, (8, half))
     rows[8:16, :] = jnp.broadcast_to((1.0 / student_temp) / row, (8, half))
@@ -241,6 +245,11 @@
         db_ref[lanes, :] = jnp.dot(cols_ref[...], g[:, lanes], preferred_element_type=F32).T
         if lanes.stop % DEPTH == 0:
             deep = slice(lanes.stop - DEPTH, lanes.stop)
+            if last is not None and lanes.stop == half:
+                for at in chunks(protos, CHUNK):
+                    term = lax.dot_general(turned_ref[:, deep], g[at, deep], NT, preferred_element_type=F32)
+                    last(at, unit_sum[:, at] + term)
+                return
             term = lax.dot_general(turned_ref[:, deep], g[:, deep], NT, preferred_element_type=F32)
             if lanes.stop > DEPTH:
                 unit_sum[...] += term
@@ -257,19 +266,20 @@
 
 
 def grad_other_kernel(
-    devices, e_ref, lg_a, lg_b, cs_ref, cols_ref, turned_ref, mine_ref, theirs_ref, e_own, lg_own_a, lg_own_b,
+    devices, e_ref, lg_other, cs_ref, cols_ref, turned_ref, mine_ref, theirs_ref, e_own, lg_own_a, lg_own_b,
     db_ref, unit_sum, loss_ref, g, rows, acc, acc_own
 ):
     row = flat(theirs_ref[0:4, :])
     part = flat(theirs_ref[4:8, :])
-    lg_ref = (lg_a, lg_b)
+    lg_ref = (lg_other,)
     cross = ((e_ref, lg_ref, acc), (e_own, (lg_own_a, lg_own_b), acc_own))
     half_gradients(row, part, e_ref, lg_ref, cs_ref, cols_ref, turned_ref, db_ref, unit_sum, None, g, rows, cross)
     parts = jnp.log(part) + jnp.log(flat(mine_ref[4:8, :]))
     row_own = flat(mine_ref[0:4, :])
     crossed = jnp.sum(acc[...], axis=0, keepdims=True) / row + jnp.sum(acc_own[...], axis=0, keepdims=True) / row_own
     terms = parts * (1.0 / devices) - crossed
-    loss_ref[...] = sum(terms[:, lanes] for lanes in chunks(terms.shape[1], 128))
+    loss_ref[...] = sum(terms[:, lanes] for lanes in chunks(terms.shape[1], loss_ref.shape[1]))
+    db_ref[e_ref.shape[1] :, :] = jnp.broadcast_to(loss_ref[...], (8, loss_ref.shape[1]))
 
 
 def grad_own_kernel(
@@ -279,20 +289,25 @@
     row = flat(mine_ref[0:4, :])
     part = flat(mine_ref[4:8, :])
     lg_ref = (lg_a, lg_b)
-    half_gradients(row, part, e_ref, lg_ref, cs_ref, cols_ref, turned_ref, db_ref, unit_sum, other_sum, g, rows, ())
     copies = []
-    for j, at in enumerate(chunks(w_ref.shape[1], CHUNK)):
-        d_unit = unit_sum[:, at]
+
+    def project(at, d_unit):
         unit, inv = columns(w_ref[:, at])
         out_buf[:, at] = inv * (d_unit - unit * jnp.sum(unit * d_unit, axis=0, keepdims=True))
+        j = len(copies)
         copies.append(pltpu.make_async_copy(out_buf.at[:, at], dp_ref.at[:, at], sem.at[j]))
         copies[j].start()
+
+    half_gradients(
+        row, part, e_ref, lg_ref, cs_ref, cols_ref, turned_ref, db_ref, unit_sum, other_sum, g, rows, (), project
+    )
     for copy in copies:
         copy.wait()
 
 
-def pack_kernel(mine_ref, theirs_ref, loss_a, loss_b, out_ref):
-    total = jnp.sum(loss_a[...] + loss_b[...], axis=1, keepdims=True)
+def pack_kernel(mine_ref, theirs_ref, loss_ref, out_ref):
+    rows = mine_ref.shape[0]
+    total = jnp.sum(loss_ref[...] + theirs_ref[rows : rows + 1, :], axis=1, keepdims=True)
     high = total.astype(BF16).astype(F32)
     mid = (total - high).astype(BF16).astype(F32)
     low = total - high - mid
@@ -399,7 +414,7 @@
     )
     mine, theirs = row_sums(sent, 8)
     late, s_late = lax.optimization_barrier((mine, s_other))
-    lg_a, part_other = student(0, split, s_late)
+    lg_other, part_other = student(0, protos, s_late)
     theirs, part_other = lax.optimization_barrier((theirs, part_other))
     row, col_scale = call(
         functools.partial(pass_kernel, total_cols, images),
@@ -408,9 +423,7 @@
         4,
         [fold8, fold8],
     )
-    row, s_late = lax.optimization_barrier((row, s_late))
-    lg_b, part_rest = student(split, protos, s_late)
-    pair_other = call(pair_kernel, vec8, (row, part_other, part_rest), 2)
+    pair_other = call(pair_kernel, vec8, (row, part_other), 2)
     pair_theirs = swap(pair_other)
     pair_other, own_late = lax.optimization_barrier((pair_other, s_own))
     lg_own_b, part_own_rest = student(split, protos, own_late)
@@ -420,17 +433,16 @@
     turned_own = call(turn_kernel, turned, (own_late,), 2)
     turned_other = call(turn_kernel, turned, (other_late,), 2)
     theirs, turned_own, turned_other = lax.optimization_barrier((theirs, turned_own, turned_other))
-    tile = sds((1, 128), F32)
+    tile = sds((1, bot), F32)
     grads = [pltpu.VMEM((protos, half), BF16), pltpu.VMEM((16, half), F32)]
     d_other, unit_sum, loss_mine = call(
         functools.partial(grad_other_kernel, 2 * chips),
-        (sds((half, bot), F32), sds((bot, protos), F32), tile),
-        (e_other, lg_a, lg_b, col_scale, s_cols, turned_other, mine, theirs, e_own, lg_own_a, lg_own_b),
+        (sds((half + 8, bot), F32), sds((bot, protos), F32), tile),
+        (e_other, lg_other, col_scale, s_cols, turned_other, mine, theirs, e_own, lg_own_a, lg_own_b),
         8,
         grads + [half_acc, half_acc],
     )
     d_theirs = swap(d_other)
-    loss_theirs = swap(loss_mine)
     whole = pltpu.VMEM((bot, protos), F32)
     d_mine, d_protos = call(
         grad_own_kernel,
@@ -443,7 +455,7 @@
     packed = call(
         pack_kernel,
         sds((chips, 80, 128), BF16),
-        (d_mine, d_theirs, loss_mine, loss_theirs),
+        (d_mine, d_theirs, loss_mine),
         4,
     )
     got = exchange(packed)

time: 155 us -> 155 us (level)
    pallas_call x21 -> x20, Pallas kernels: 28.5 us -> 28.1 us  [call(): pl.pallas_call(kernel, out_shape=out_shape, in_specs=[ANY if i in in_any...]
  transfers between devices with their start and end apart: 8 -> 7, of which waited for: 3 -> 3; matrix products, arithmetic and copies ran while one was open for 0% -> 0% of each run, Pallas kernels for 9% -> 9%
where the time goes in v6:
time: 155 us; the launch traced here: 154 us
  blocking collectives  122 us (79%)
  Pallas kernels  28.1 us (18%)
  starting transfers between devices  2.03 us (1%)
    all_to_all x5, blocking collectives, exchange(): return lax.all_to_all(x, CHIPS, 0, 0)  122 us
    pallas_call x20, Pallas kernels, call(): pl.pallas_call(kernel, out_shape=out_shape, in_specs=[ANY if i in in_any...  28.1 us
  transfers between devices with their start and end apart: 7, of which 3 were waited for; matrix products, arithmetic and copies ran while one was open for 0% of the time, Pallas kernels for 9%

profile of v6, /device:TPU:0, one launch (start us, length us, event | category | flops | bytes accessed | tf_op | source)
XLA Modules:
  0.0 154.5 jit_solution(7871700156591436744)
XLA Ops:
  0.6 3.0 %shard_map.76 = (bf16[64,24,384]{2,1,0:T(8,128)(2,1)}, bf16[24,384]{1,0:T(8,128)(2,1)}) custom-call(bf16[24,384]{1,0:T(8,128)(2,1)} %hid_ref.3, bf16[24,2048]{1,0:T(8,128)(2,1)} %hid_ref.2, bf16[2048,384]{1,0:T(8,128)(2,1)} %proj_ref.1), custom_call_target="tpu_custom_call" | custom-call | tf_op jit(solution)/shard_map/pallas_call | solution.py:33
  3.7 31.9 %all_to_all.25 = bf16[64,24,384]{2,1,0:T(8,128)(2,1)S(1)} all-to-all(bf16[64,24,384]{2,1,0:T(8,128)(2,1)} %get-tuple-element.50), channel_id=1, replica_groups=mesh['z'=4,'y'=4,'x'=4,'c'=2] {'z','y','x'}, dimensions={0} | all-to-all | bytes 2359296 | tf_op jit(solution)/shard_map/all_to_all | solution.py:352
  35.6 2.1 %shard_map.77 = (f32[1024,1536]{1,0:T(8,128)S(1)}, bf16[1024,384]{1,0:T(8,128)(2,1)S(1)}, f32[1024,1]{1,0:T(8,128)S(1)}) custom-call(bf16[384,1024]{1,0:T(8,128)(2,1)S(1)} %copy-done.1, bf16[1536,384]{1,0:T(8,128)(2,1)S(1)} %bitcast.9), custom_call_target="tpu_custom_call" | custom-call | tf_op jit(solution)/shard_map/pallas_call | solution.py:33
  37.7 0.4 shard_map.78
  38.1 0.3 collective-permute-done.rows_ref
  38.4 3.1 %shard_map.79 = (f32[1024,1536]{1,0:T(8,128)S(1)}, bf16[64,32,384]{2,1,0:T(8,128)(2,1)S(1)}) custom-call(bf16[1024,384]{1,0:T(8,128)(2,1)S(1)} %get-tuple-element.57.lhs_ref, bf16[1536,384]{1,0:T(8,128)(2,1)S(1)} %collective-permute-done.rows_ref, f32[1024,1536]{1,0:T(8,128)S(1)} %get-tuple-element.51.e_own.own_ref.e_ref, ...), custom_call_target="tpu_custom_call" | custom-call | tf_op jit(solution)/shard_map/pallas_call | solution.py:33
  41.5 29.4 %all_to_all.26.got_ref = bf16[64,32,384]{2,1,0:T(8,128)(2,1)S(1)} all-to-all(bf16[64,32,384]{2,1,0:T(8,128)(2,1)S(1)} %get-tuple-element.61), channel_id=1, replica_groups=mesh['z'=4,'y'=4,'x'=4,'c'=2] {'z','y','x'}, dimensions={0} | all-to-all | bytes 3145728 | tf_op jit(solution)/shard_map/all_to_all | solution.py:352
  71.0 0.2 shard_map.80
  71.1 0.1 collective-permute-start.1
  71.2 1.5 shard_map.81
  72.7 0.6 collective-permute-start.2
  73.3 2.0 %shard_map.82 = bf16[64,8,384]{2,1,0:T(8,128)(2,1)S(1)} custom-call(f32[1024,1536]{1,0:T(8,128)S(1)} %get-tuple-element.51.e_own.own_ref.e_ref, f32[1024,1536]{1,0:T(8,128)S(1)} %get-tuple-element.64.other_ref.e_ref, f32[8,384]{1,0:T(8,128)S(1)} %get-tuple-element.65.mine_ref, f32[8,384]{1,0:T(8,128)S(1)} %collective-permute-done.1.theirs_ref), custom_call_target="tpu_custom_call" | custom-call | tf_op jit(solution)/shard_map/pallas_call | solution.py:33
  75.2 17.3 %all_to_all.27.got_ref = bf16[64,8,384]{2,1,0:T(8,128)(2,1)S(1)} all-to-all(bf16[64,8,384]{2,1,0:T(8,128)(2,1)S(1)} %shard_map.82), channel_id=1, replica_groups=mesh['z'=4,'y'=4,'x'=4,'c'=2] {'z','y','x'}, dimensions={0} | all-to-all | bytes 786432 | tf_op jit(solution)/shard_map/all_to_all | solution.py:352
  92.5 0.1 shard_map.83.mine_ref
  92.6 0.3 collective-permute-start.3
  92.9 1.9 %shard_map.84 = (f32[1024,1536]{1,0:T(8,128)S(1)}, f32[4,384]{1,0:T(4,128)S(1)}) custom-call(bf16[1024,384]{1,0:T(8,128)(2,1)S(1)} %get-tuple-element.56.lhs_ref, bf16[1536,384]{1,0:T(8,128)(2,1)S(1)} %collective-permute-done.2.rows_ref), custom_call_target="tpu_custom_call" | custom-call | tf_op jit(solution)/shard_map/pallas_call | solution.py:33
  94.8 1.9 %shard_map.85 = (f32[8,384]{1,0:T(8,128)S(1)}, f32[1024,1]{1,0:T(8,128)S(1)}) custom-call(f32[1024,1536]{1,0:T(8,128)S(1)} %get-tuple-element.51.e_own.own_ref.e_ref, f32[1024,1536]{1,0:T(8,128)S(1)} %get-tuple-element.64.other_ref.e_ref, f32[8,384]{1,0:T(8,128)S(1)} %shard_map.83.mine_ref, f32[8,384]{1,0:T(8,128)S(1)} %collective-permute-done.3.theirs_ref), custom_call_target="tpu_custom_call" | custom-call | tf_op jit(solution)/shard_map/pallas_call | solution.py:33
  96.8 0.6 collective-permute-start.4
  97.3 0.6 shard_map.87
  98.0 0.2 collective-permute-done.4.theirs_ref
  98.2 17.1 %all_to_all.28.got_ref = bf16[64,8,384]{2,1,0:T(8,128)(2,1)S(1)} all-to-all(bf16[64,8,384]{2,1,0:T(8,128)(2,1)S(1)} %shard_map.88), channel_id=1, replica_groups=mesh['z'=4,'y'=4,'x'=4,'c'=2] {'z','y','x'}, dimensions={0} | all-to-all | bytes 786432 | tf_op jit(solution)/shard_map/all_to_all | solution.py:352
  115.3 0.1 shard_map.89.mine_ref
  115.4 0.1 collective-permute-start.5
  115.5 0.4 shard_map.90.turned_ref
  115.8 0.4 shard_map.91.turned_ref
  116.2 0.4 collective-permute-done.5.theirs_ref
  116.7 4.5 %shard_map.92 = (f32[1544,384]{1,0:T(8,128)S(1)}, f32[384,1024]{1,0:T(8,128)S(1)}, f32[1,384]{1,0:T(1,128)S(1)}) custom-call(f32[1024,1536]{1,0:T(8,128)S(1)} %get-tuple-element.64.other_ref.e_ref, f32[1024,1536]{1,0:T(8,128)S(1)} %get-tuple-element.87.lg_other, f32[1024,1]{1,0:T(8,128)S(1)} %get-tuple-element.77.cs_ref, ...), custom_call_target="tpu_custom_call" | custom-call | tf_op jit(solution)/shard_map/pallas_call | solution.py:33
  121.2 0.5 collective-permute-start.6
  121.6 4.7 %shard_map.93 = (f32[1536,384]{1,0:T(8,128)S(1)}, f32[384,1024]{1,0:T(8,128)}) custom-call(f32[1024,1536]{1,0:T(8,128)S(1)} %get-tuple-element.51.e_own.own_ref.e_ref, f32[768,1536]{1,0:T(8,128)S(1)} %get-tuple-element.63.lg_own_a.lg_a, f32[256,1536]{1,0:T(8,128)S(1)} %get-tuple-element.76.lg_own_b.lg_b, f32[1024,1]{1,0:T(8,128)S(1)} %get-tuple-element.77.cs_ref, ...), custom_call_target="tpu_custom_call" | custom-call | tf_op jit(solution)/shard_map/pallas_call | solution.py:33
  126.3 0.4 shard_map.94
  126.8 26.8 %all_to_all.29.got_ref = bf16[64,80,128]{2,1,0:T(8,128)(2,1)S(1)} all-to-all(bf16[64,80,128]{2,1,0:T(8,128)(2,1)S(1)} %shard_map.94), channel_id=1, replica_groups=mesh['z'=4,'y'=4,'x'=4,'c'=2] {'z','y','x'}, dimensions={0} | all-to-all | bytes 2621440 | tf_op jit(solution)/shard_map/all_to_all | solution.py:352
  153.5 0.9 shard_map.95
  (15 shorter events, 0.1 us)
Async XLA Ops:
  3.7 31.9 %copy-start.1 = (bf16[384,1024]{1,0:T(8,128)(2,1)S(1)}, bf16[384,1024]{1,0:T(8,128)(2,1)}, u32[]{:S(2)}) copy-start(bf16[384,1024]{1,0:T(8,128)(2,1)} %w_ref.2) | copy-start | bytes 2359300
  35.6 2.1 %copy-start = (bf16[384,1024]{1,0:T(8,128)(2,1)S(1)}, bf16[384,1024]{1,0:T(8,128)(2,1)}, u32[]{:S(2)}) copy-start(bf16[384,1024]{1,0:T(8,128)(2,1)} %w_ref.4) | copy-start | bytes 2359300
  35.6 2.9 %copy-start.3 = (bf16[24,384]{1,0:T(8,128)(2,1)S(1)}, bf16[24,384]{1,0:T(8,128)(2,1)}, u32[]{:S(2)}) copy-start(bf16[24,384]{1,0:T(8,128)(2,1)} %get-tuple-element.60.s_ref) | copy-start | bytes 55300
  35.6 2.8 %collective-permute-start = (bf16[1536,384]{1,0:T(8,128)(2,1)S(1)}, bf16[1536,384]{1,0:T(8,128)(2,1)S(1)}, u32[]{:S(2)}, u32[]{:S(2)}) collective-permute-start(bf16[1536,384]{1,0:T(8,128)(2,1)S(1)} %bitcast.8), channel_id=1, source_target_pairs={{0,1},{1,0},{2,3},{3,2},{4,5},{5,4},{6,7},{7,6},{8,9},{9,8},{10,11... | collective-permute-start | bytes 3538952 | tf_op jit(solution)/shard_map/ppermute | solution.py:349
  71.1 1.6 %collective-permute-start.1 = (f32[8,384]{1,0:T(8,128)S(1)}, f32[8,384]{1,0:T(8,128)S(1)}, u32[]{:S(2)}, u32[]{:S(2)}) collective-permute-start(f32[8,384]{1,0:T(8,128)S(1)} %get-tuple-element.65.mine_ref), channel_id=1, source_target_pairs={{0,1},{1,0},{2,3},{3,2},{4,5},{5,4},{6,7},{7,6},{8,9},{9,8},{10,11... | collective-permute-start | bytes 36872 | tf_op jit(solution)/shard_map/ppermute | solution.py:349
  72.7 20.2 %collective-permute-start.2 = (bf16[1536,384]{1,0:T(8,128)(2,1)S(1)}, bf16[1536,384]{1,0:T(8,128)(2,1)S(1)}, u32[]{:S(2)}, u32[]{:S(2)}) collective-permute-start(bf16[1536,384]{1,0:T(8,128)(2,1)S(1)} %bitcast.5), channel_id=1, source_target_pairs={{0,1},{1,0},{2,3},{3,2},{4,5},{5,4},{6,7},{7,6},{8,9},{9,8},{10,11... | collective-permute-start | bytes 3538952 | tf_op jit(solution)/shard_map/ppermute | solution.py:349
  92.6 2.2 %collective-permute-start.3 = (f32[8,384]{1,0:T(8,128)S(1)}, f32[8,384]{1,0:T(8,128)S(1)}, u32[]{:S(2)}, u32[]{:S(2)}) collective-permute-start(f32[8,384]{1,0:T(8,128)S(1)} %shard_map.83.mine_ref), channel_id=1, source_target_pairs={{0,1},{1,0},{2,3},{3,2},{4,5},{5,4},{6,7},{7,6},{8,9},{9,8},{10,11... | collective-permute-start | bytes 36872 | tf_op jit(solution)/shard_map/ppermute | solution.py:349
  96.8 1.4 collective-permute-start.4
  115.4 1.3 collective-permute-start.5
  121.2 5.1 %collective-permute-start.6 = (f32[1544,384]{1,0:T(8,128)S(1)}, f32[1544,384]{1,0:T(8,128)S(1)}, u32[]{:S(2)}, u32[]{:S(2)}) collective-permute-start(f32[1544,384]{1,0:T(8,128)S(1)} %get-tuple-element.92), channel_id=1, source_target_pairs={{0,1},{1,0},{2,3},{3,2},{4,5},{5,4},{6,7},{7,6},{8,9},{9,8},{10,11... | collective-permute-start | bytes 7114760 | tf_op jit(solution)/shard_map/ppermute | solution.py:349
  126.7 26.8 %copy-start.2 = (bf16[24,384]{1,0:T(8,128)(2,1)S(1)}, bf16[24,384]{1,0:T(8,128)(2,1)}, u32[]{:S(2)}) copy-start(bf16[24,384]{1,0:T(8,128)(2,1)} %hid_ref.3) | copy-start | bytes 55300

commit v7 on v6

--- a/solution.py
+++ b/solution.py
@@ -115,14 +115,14 @@
         sums_ref[at, :] = expo_block(at, lhs_ref, rows_ref, e_ref)
 
 
-def teacher_other_kernel(total_cols, lhs_ref, rows_ref, e_own, sums_ref, s_ref, e_ref, out_ref, acc):
+def teacher_other_kernel(total_cols, expected, lhs_ref, rows_ref, e_own, sums_ref, s_ref, e_ref, out_ref, acc):
     half = rows_ref.shape[0]
     acc[...] = jnp.zeros_like(acc)
     for at in chunks(lhs_ref.shape[0], CHUNK):
         scale = 1.0 / (total_cols * (sums_ref[at, :] + expo_block(at, lhs_ref, rows_ref, e_ref)))
         row_pass(e_own.at[at, :], scale, acc.at[:, :half])
         row_pass(e_ref.at[at, :], scale, acc.at[:, half:])
-    sums = fold(jnp.sum(acc[...], axis=0, keepdims=True))
+    sums = fold(jnp.sum(acc[...], axis=0, keepdims=True)) - expected
     spread(jnp.concatenate([sums, s_ref[...].astype(F32)], axis=0), out_ref)
 
 
@@ -188,8 +188,11 @@
         acc[:, lanes] += jnp.sum(block_ref[:, lanes].reshape(rows // 8, 8, 512) * scale, axis=0)
 
 
-def pass_kernel(total_cols, images, own_ref, other_ref, mine_ref, theirs_ref, out_ref, cs_ref, weight, acc):
+def pass_kernel(total_cols, images, devices, own_ref, other_ref, mine_ref, theirs_ref, *rest):
+    *before, out_ref, total_ref, cs_ref, weight, acc = rest
     total = total_row(mine_ref[...], theirs_ref[...])
+    total = total + (flat(before[0][...]) if before else 1.0 / images)
+    total_ref[...] = fold(total)
     weight[...] = jnp.broadcast_to(1.0 / (images * total), weight.shape)
     acc[...] = jnp.zeros_like(acc)
     protos, half = own_ref.shape
@@ -207,7 +210,7 @@
         return 0
 
     lax.fori_loop(0, protos // BLOCK, step, 0)
-    piece = fold(jnp.sum(acc[...], axis=0, keepdims=True))
+    piece = fold(jnp.sum(acc[...], axis=0, keepdims=True)) - total_ref[...] * (1.0 / devices)
     if len(out_ref.shape) == 3:
         spread(piece, out_ref)
     else:
@@ -266,16 +269,16 @@
 
 
 def grad_other_kernel(
-    devices, e_ref, lg_other, cs_ref, cols_ref, turned_ref, mine_ref, theirs_ref, e_own, lg_own_a, lg_own_b,
+    devices, e_ref, lg_other, cs_ref, cols_ref, turned_ref, mine_ref, theirs_ref, base_ref, e_own, lg_own_a, lg_own_b,
     db_ref, unit_sum, loss_ref, g, rows, acc, acc_own
 ):
-    row = flat(theirs_ref[0:4, :])
+    row = flat(theirs_ref[0:4, :] + base_ref[4:8, :])
     part = flat(theirs_ref[4:8, :])
     lg_ref = (lg_other,)
     cross = ((e_ref, lg_ref, acc), (e_own, (lg_own_a, lg_own_b), acc_own))
     half_gradients(row, part, e_ref, lg_ref, cs_ref, cols_ref, turned_ref, db_ref, unit_sum, None, g, rows, cross)
     parts = jnp.log(part) + jnp.log(flat(mine_ref[4:8, :]))
-    row_own = flat(mine_ref[0:4, :])
+    row_own = flat(mine_ref[0:4, :] + base_ref[0:4, :])
     crossed = jnp.sum(acc[...], axis=0, keepdims=True) / row + jnp.sum(acc_own[...], axis=0, keepdims=True) / row_own
     terms = parts * (1.0 / devices) - crossed
     loss_ref[...] = sum(terms[:, lanes] for lanes in chunks(terms.shape[1], loss_ref.shape[1]))
@@ -283,10 +286,10 @@
 
 
 def grad_own_kernel(
-    e_ref, lg_a, lg_b, cs_ref, cols_ref, turned_ref, mine_ref, other_sum, w_ref,
+    e_ref, lg_a, lg_b, cs_ref, cols_ref, turned_ref, mine_ref, base_ref, other_sum, w_ref,
     db_ref, dp_ref, g, rows, unit_sum, out_buf, sem
 ):
-    row = flat(mine_ref[0:4, :])
+    row = flat(mine_ref[0:4, :] + base_ref[0:4, :])
     part = flat(mine_ref[4:8, :])
     lg_ref = (lg_a, lg_b)
     copies = []
@@ -305,35 +308,54 @@
         copy.wait()
 
 
-def pack_kernel(mine_ref, theirs_ref, loss_ref, out_ref):
+def parts_of(value):
+    high = value.astype(BF16).astype(F32)
+    mid = (value - high).astype(BF16).astype(F32)
+    return high, mid, value - high - mid
+
+
+def pack_kernel(mine_ref, theirs_ref, loss_ref, s_ref, out_ref):
     rows = mine_ref.shape[0]
+    lane = lax.broadcasted_iota(jnp.int32, (8, 128), 1)
     total = jnp.sum(loss_ref[...] + theirs_ref[rows : rows + 1, :], axis=1, keepdims=True)
-    high = total.astype(BF16).astype(F32)
-    mid = (total - high).astype(BF16).astype(F32)
-    low = total - high - mid
-    row = lax.broadcasted_iota(jnp.int32, (8, 128), 0)
-    tail = jnp.where(row == 0, high, jnp.where(row == 1, mid, jnp.where(row == 2, low, 0.0)))
-    tail = tail.astype(BF16)
+    loss = jnp.zeros((8, 128), F32)
+    for j, part in enumerate(parts_of(total)):
+        loss = jnp.where(lane == 9 + j, part, loss)
+
+    group = 8
 
     def step(i, _):
-        at = pl.ds(pl.multiple_of(i * 24, 8), 24)
+        at = pl.ds(pl.multiple_of(i * 24 * group, 8), 24 * group)
         block = mine_ref[at, :] + theirs_ref[at, :]
+        unit = s_ref[pl.ds(i * group, group)].astype(F32).reshape(block.shape)
+        along = jnp.sum(block * unit, axis=1, keepdims=True)
+        block = (block - unit * along).astype(BF16).reshape(group, 24, block.shape[1])
+        parts = [part.reshape(group, 24, 1) for part in parts_of(along)]
+        tail = jnp.broadcast_to(loss[None], (group, 8, 128))
+        for j, part in enumerate(parts):
+            for k in range(3):
+                tail = jnp.where((lane == 3 * j + k)[None], part[:, 8 * k : 8 * (k + 1), :], tail)
+        chips = pl.ds(i * group, group)
         for k in range(3):
-            out_ref[i, 24 * k : 24 * (k + 1), :] = block[:, 128 * k : 128 * (k + 1)].astype(BF16)
-        out_ref[i, 72:80, :] = tail
+            out_ref[chips, 24 * k : 24 * (k + 1), :] = block[:, :, 128 * k : 128 * (k + 1)]
+        out_ref[chips, 72:80, :] = tail.astype(BF16)
         return 0
 
-    lax.fori_loop(0, out_ref.shape[0], step, 0, unroll=4)
+    lax.fori_loop(0, out_ref.shape[0] // group, step, 0, unroll=2)
 
 
 def finish_kernel(images, got_ref, hid_ref, ds_ref, loss_ref):
     total = jnp.sum(got_ref[...].astype(F32), axis=0)
-    d_bot = jnp.concatenate([total[24 * k : 24 * (k + 1), :] for k in range(3)], axis=1)
+    tail = total[72:80, :]
+    along = jnp.concatenate([tail[:, k : k + 1] + tail[:, 3 + k : 4 + k] + tail[:, 6 + k : 7 + k] for k in range(3)], axis=0)
     wide = hid_ref[...].astype(F32)
     inv = lax.rsqrt(jnp.sum(wide * wide, axis=1, keepdims=True) + EPS)
     unit = wide * inv
+    d_bot = jnp.concatenate([total[24 * k : 24 * (k + 1), :] for k in range(3)], axis=1)
+    d_bot = d_bot + unit.astype(BF16).astype(F32) * along
     ds_ref[...] = inv * (d_bot - unit * jnp.sum(unit * d_bot, axis=1, keepdims=True))
-    loss_ref[...] = (total[72:73, :] + total[73:74, :] + total[74:75, :]) * (1.0 / images)
+    loss = tail[0:1, 9:10] + tail[0:1, 10:11] + tail[0:1, 11:12]
+    loss_ref[...] = jnp.broadcast_to(loss * (1.0 / images), loss_ref.shape)
 
 
 def body(teacher_hidden, teacher_proj, student_hidden, teacher_protos, student_protos):
@@ -387,7 +409,7 @@
     s_lhs, s_cols = call(student_columns_kernel, (lhs, sds((bot, protos), BF16)), (student_late,), 8)
     t_other, s_lhs, s_cols = lax.optimization_barrier((t_other, s_lhs, s_cols))
     e_other, sent = call(
-        functools.partial(teacher_other_kernel, total_cols),
+        functools.partial(teacher_other_kernel, total_cols, 1.0 / (2 * chips * images)),
         (matrix, sds((chips, 8 + rows_dev, bot), BF16)),
         (t_lhs, t_other, e_own, sums, s_bot),
         8,
@@ -405,9 +427,10 @@
     lg_own_a, part_own = student(0, split, s_own)
     theirs, part_own, s_late = lax.optimization_barrier((theirs, part_own, s_own))
     s_other = swap(s_late)
-    (sent,) = call(
-        functools.partial(pass_kernel, total_cols, images),
-        (send8,),
+    one_pass = functools.partial(pass_kernel, total_cols, images, 2 * chips)
+    sent, before = call(
+        one_pass,
+        (send8, vec8),
         (e_own, e_other, mine, theirs),
         4,
         [scales, fold8, fold8],
@@ -416,10 +439,10 @@
     late, s_late = lax.optimization_barrier((mine, s_other))
     lg_other, part_other = student(0, protos, s_late)
     theirs, part_other = lax.optimization_barrier((theirs, part_other))
-    row, col_scale = call(
-        functools.partial(pass_kernel, total_cols, images),
-        (vec8, column),
-        (e_own, e_other, late, theirs),
+    row, before, col_scale = call(
+        one_pass,
+        (vec8, vec8, column),
+        (e_own, e_other, late, theirs, before),
         4,
         [fold8, fold8],
     )
@@ -438,7 +461,7 @@
     d_other, unit_sum, loss_mine = call(
         functools.partial(grad_other_kernel, 2 * chips),
         (sds((half + 8, bot), F32), sds((bot, protos), F32), tile),
-        (e_other, lg_other, col_scale, s_cols, turned_other, mine, theirs, e_own, lg_own_a, lg_own_b),
+        (e_other, lg_other, col_scale, s_cols, turned_other, mine, theirs, before, e_own, lg_own_a, lg_own_b),
         8,
         grads + [half_acc, half_acc],
     )
@@ -447,7 +470,7 @@
     d_mine, d_protos = call(
         grad_own_kernel,
         (sds((half, bot), F32), sds((bot, protos), F32)),
-        (e_own, lg_own_a, lg_own_b, col_scale, s_cols, turned_own, mine, unit_sum, student_protos),
+        (e_own, lg_own_a, lg_own_b, col_scale, s_cols, turned_own, mine, before, unit_sum, student_protos),
         12,
         grads + [whole, whole, pltpu.SemaphoreType.DMA((protos // CHUNK,))],
         out_any=(1,),
@@ -455,7 +478,7 @@
     packed = call(
         pack_kernel,
         sds((chips, 80, 128), BF16),
-        (d_mine, d_theirs, loss_mine),
+        (d_mine, d_theirs, loss_mine, s_own.reshape(chips, rows_dev, bot)),
         4,
     )
     got = exchange(packed)

time: 155 us -> 156 us (level)
  no operation moved by 1% of the time
where the time goes in v7:
time: 156 us; the launch traced here: 155 us
  blocking collectives  122 us (78%)
  Pallas kernels  29.1 us (19%)
  starting transfers between devices  2.02 us (1%)
    all_to_all x5, blocking collectives, exchange(): return lax.all_to_all(x, CHIPS, 0, 0)  122 us
    pallas_call x20, Pallas kernels, call(): pl.pallas_call(kernel, out_shape=out_shape, in_specs=[ANY if i in in_any...  29.1 us
  transfers between devices with their start and end apart: 7, of which 3 were waited for; matrix products, arithmetic and copies ran while one was open for 0% of the time, Pallas kernels for 9%

profile of v7, /device:TPU:0, one launch (start us, length us, event | category | flops | bytes accessed | tf_op | source)
XLA Modules:
  0.0 155.4 jit_solution(16071652090226878949)
XLA Ops:
  0.6 3.0 %shard_map.76 = (bf16[64,24,384]{2,1,0:T(8,128)(2,1)}, bf16[24,384]{1,0:T(8,128)(2,1)}) custom-call(bf16[24,384]{1,0:T(8,128)(2,1)} %hid_ref.3, bf16[24,2048]{1,0:T(8,128)(2,1)} %hid_ref.2, bf16[2048,384]{1,0:T(8,128)(2,1)} %proj_ref.1), custom_call_target="tpu_custom_call" | custom-call | tf_op jit(solution)/shard_map/pallas_call | solution.py:33
  3.7 31.9 %all_to_all.25 = bf16[64,24,384]{2,1,0:T(8,128)(2,1)S(1)} all-to-all(bf16[64,24,384]{2,1,0:T(8,128)(2,1)} %get-tuple-element.53), channel_id=1, replica_groups=mesh['z'=4,'y'=4,'x'=4,'c'=2] {'z','y','x'}, dimensions={0} | all-to-all | bytes 2359296 | tf_op jit(solution)/shard_map/all_to_all | solution.py:374
  35.6 2.1 %shard_map.77 = (f32[1024,1536]{1,0:T(8,128)S(1)}, bf16[1024,384]{1,0:T(8,128)(2,1)S(1)}, f32[1024,1]{1,0:T(8,128)S(1)}) custom-call(bf16[384,1024]{1,0:T(8,128)(2,1)S(1)} %copy-done.1, bf16[1536,384]{1,0:T(8,128)(2,1)S(1)} %bitcast.9), custom_call_target="tpu_custom_call" | custom-call | tf_op jit(solution)/shard_map/pallas_call | solution.py:33
  37.7 0.4 shard_map.78
  38.1 0.3 collective-permute-done.rows_ref
  38.4 3.1 %shard_map.79 = (f32[1024,1536]{1,0:T(8,128)S(1)}, bf16[64,32,384]{2,1,0:T(8,128)(2,1)S(1)}) custom-call(bf16[1024,384]{1,0:T(8,128)(2,1)S(1)} %get-tuple-element.60.lhs_ref, bf16[1536,384]{1,0:T(8,128)(2,1)S(1)} %collective-permute-done.rows_ref, f32[1024,1536]{1,0:T(8,128)S(1)} %get-tuple-element.54.e_own.own_ref.e_ref, ...), custom_call_target="tpu_custom_call" | custom-call | tf_op jit(solution)/shard_map/pallas_call | solution.py:33
  41.5 29.4 %all_to_all.26.got_ref = bf16[64,32,384]{2,1,0:T(8,128)(2,1)S(1)} all-to-all(bf16[64,32,384]{2,1,0:T(8,128)(2,1)S(1)} %get-tuple-element.64), channel_id=1, replica_groups=mesh['z'=4,'y'=4,'x'=4,'c'=2] {'z','y','x'}, dimensions={0} | all-to-all | bytes 3145728 | tf_op jit(solution)/shard_map/all_to_all | solution.py:374
  71.0 0.2 shard_map.80
  71.2 0.1 collective-permute-start.1
  71.3 1.4 shard_map.81
  72.7 0.6 collective-permute-start.2
  73.3 1.9 %shard_map.82 = (bf16[64,8,384]{2,1,0:T(8,128)(2,1)S(1)}, f32[8,384]{1,0:T(8,128)S(1)}) custom-call(f32[1024,1536]{1,0:T(8,128)S(1)} %get-tuple-element.54.e_own.own_ref.e_ref, f32[1024,1536]{1,0:T(8,128)S(1)} %get-tuple-element.67.other_ref.e_ref, f32[8,384]{1,0:T(8,128)S(1)} %get-tuple-element.68.mine_ref, f32[8,384]{1,0:T(8,128)S(1)} %collective-permute-done.1.theirs_ref), custom_call_target="tpu_custom_call" | custom-call | tf_op jit(solution)/shard_map/pallas_call | solution.py:33
  75.2 17.3 %all_to_all.27.got_ref = bf16[64,8,384]{2,1,0:T(8,128)(2,1)S(1)} all-to-all(bf16[64,8,384]{2,1,0:T(8,128)(2,1)S(1)} %get-tuple-element.71), channel_id=1, replica_groups=mesh['z'=4,'y'=4,'x'=4,'c'=2] {'z','y','x'}, dimensions={0} | all-to-all | bytes 786432 | tf_op jit(solution)/shard_map/all_to_all | solution.py:374
  92.5 0.1 shard_map.83.mine_ref
  92.6 0.3 collective-permute-start.3
  92.8 1.9 %shard_map.84 = (f32[1024,1536]{1,0:T(8,128)S(1)}, f32[4,384]{1,0:T(4,128)S(1)}) custom-call(bf16[1024,384]{1,0:T(8,128)(2,1)S(1)} %get-tuple-element.59.lhs_ref, bf16[1536,384]{1,0:T(8,128)(2,1)S(1)} %collective-permute-done.2.rows_ref), custom_call_target="tpu_custom_call" | custom-call | tf_op jit(solution)/shard_map/pallas_call | solution.py:33
  94.8 1.9 %shard_map.85 = (f32[8,384]{1,0:T(8,128)S(1)}, f32[8,384]{1,0:T(8,128)S(1)}, f32[1024,1]{1,0:T(8,128)S(1)}) custom-call(f32[1024,1536]{1,0:T(8,128)S(1)} %get-tuple-element.54.e_own.own_ref.e_ref, f32[1024,1536]{1,0:T(8,128)S(1)} %get-tuple-element.67.other_ref.e_ref, f32[8,384]{1,0:T(8,128)S(1)} %shard_map.83.mine_ref, ...), custom_call_target="tpu_custom_call" | custom-call | tf_op jit(solution)/shard_map/pallas_call | solution.py:33
  96.7 0.6 collective-permute-start.4
  97.2 0.6 shard_map.87
  97.9 0.2 collective-permute-done.4.theirs_ref
  98.1 17.1 %all_to_all.28.got_ref = bf16[64,8,384]{2,1,0:T(8,128)(2,1)S(1)} all-to-all(bf16[64,8,384]{2,1,0:T(8,128)(2,1)S(1)} %shard_map.88), channel_id=1, replica_groups=mesh['z'=4,'y'=4,'x'=4,'c'=2] {'z','y','x'}, dimensions={0} | all-to-all | bytes 786432 | tf_op jit(solution)/shard_map/all_to_all | solution.py:374
  115.2 0.1 shard_map.89.mine_ref
  115.3 0.1 collective-permute-start.5
  115.4 0.4 shard_map.90.turned_ref
  115.8 0.4 shard_map.91.turned_ref
  116.1 0.4 collective-permute-done.5.theirs_ref
  116.6 4.7 %shard_map.92 = (f32[1544,384]{1,0:T(8,128)S(1)}, f32[384,1024]{1,0:T(8,128)S(1)}, f32[1,384]{1,0:T(1,128)S(1)}) custom-call(f32[1024,1536]{1,0:T(8,128)S(1)} %get-tuple-element.67.other_ref.e_ref, f32[1024,1536]{1,0:T(8,128)S(1)} %get-tuple-element.93.lg_other, f32[1024,1]{1,0:T(8,128)S(1)} %get-tuple-element.82.cs_ref, ...), custom_call_target="tpu_custom_call" | custom-call | tf_op jit(solution)/shard_map/pallas_call | solution.py:33
  121.3 0.5 collective-permute-start.6
  121.8 4.7 %shard_map.93 = (f32[1536,384]{1,0:T(8,128)S(1)}, f32[384,1024]{1,0:T(8,128)}) custom-call(f32[1024,1536]{1,0:T(8,128)S(1)} %get-tuple-element.54.e_own.own_ref.e_ref, f32[768,1536]{1,0:T(8,128)S(1)} %get-tuple-element.66.lg_own_a.lg_a, f32[256,1536]{1,0:T(8,128)S(1)} %get-tuple-element.81.lg_own_b.lg_b, f32[1024,1]{1,0:T(8,128)S(1)} %get-tuple-element.82.cs_ref, ...), custom_call_target="tpu_custom_call" | custom-call | tf_op jit(solution)/shard_map/pallas_call | solution.py:33
  126.5 1.1 shard_map.94
  127.6 26.8 %all_to_all.29.got_ref = bf16[64,80,128]{2,1,0:T(8,128)(2,1)S(1)} all-to-all(bf16[64,80,128]{2,1,0:T(8,128)(2,1)S(1)} %shard_map.94), channel_id=1, replica_groups=mesh['z'=4,'y'=4,'x'=4,'c'=2] {'z','y','x'}, dimensions={0} | all-to-all | bytes 2621440 | tf_op jit(solution)/shard_map/all_to_all | solution.py:374
  154.4 1.0 shard_map.95
  (15 shorter events, 0.1 us)
Async XLA Ops:
  3.7 31.9 %copy-start.1 = (bf16[384,1024]{1,0:T(8,128)(2,1)S(1)}, bf16[384,1024]{1,0:T(8,128)(2,1)}, u32[]{:S(2)}) copy-start(bf16[384,1024]{1,0:T(8,128)(2,1)} %w_ref.2) | copy-start | bytes 2359300
  35.6 2.1 %copy-start = (bf16[384,1024]{1,0:T(8,128)(2,1)S(1)}, bf16[384,1024]{1,0:T(8,128)(2,1)}, u32[]{:S(2)}) copy-start(bf16[384,1024]{1,0:T(8,128)(2,1)} %w_ref.4) | copy-start | bytes 2359300
  35.6 2.9 %copy-start.3 = (bf16[24,384]{1,0:T(8,128)(2,1)S(1)}, bf16[24,384]{1,0:T(8,128)(2,1)}, u32[]{:S(2)}) copy-start(bf16[24,384]{1,0:T(8,128)(2,1)} %get-tuple-element.63.s_ref) | copy-start | bytes 55300
  35.6 2.8 %collective-permute-start = (bf16[1536,384]{1,0:T(8,128)(2,1)S(1)}, bf16[1536,384]{1,0:T(8,128)(2,1)S(1)}, u32[]{:S(2)}, u32[]{:S(2)}) collective-permute-start(bf16[1536,384]{1,0:T(8,128)(2,1)S(1)} %bitcast.8), channel_id=1, source_target_pairs={{0,1},{1,0},{2,3},{3,2},{4,5},{5,4},{6,7},{7,6},{8,9},{9,8},{10,11... | collective-permute-start | bytes 3538952 | tf_op jit(solution)/shard_map/ppermute | solution.py:371
  71.2 1.5 collective-permute-start.1
  72.7 20.1 %collective-permute-start.2 = (bf16[1536,384]{1,0:T(8,128)(2,1)S(1)}, bf16[1536,384]{1,0:T(8,128)(2,1)S(1)}, u32[]{:S(2)}, u32[]{:S(2)}) collective-permute-start(bf16[1536,384]{1,0:T(8,128)(2,1)S(1)} %bitcast.5), channel_id=1, source_target_pairs={{0,1},{1,0},{2,3},{3,2},{4,5},{5,4},{6,7},{7,6},{8,9},{9,8},{10,11... | collective-permute-start | bytes 3538952 | tf_op jit(solution)/shard_map/ppermute | solution.py:371
  92.6 2.2 %collective-permute-start.3 = (f32[8,384]{1,0:T(8,128)S(1)}, f32[8,384]{1,0:T(8,128)S(1)}, u32[]{:S(2)}, u32[]{:S(2)}) collective-permute-start(f32[8,384]{1,0:T(8,128)S(1)} %shard_map.83.mine_ref), channel_id=1, source_target_pairs={{0,1},{1,0},{2,3},{3,2},{4,5},{5,4},{6,7},{7,6},{8,9},{9,8},{10,11... | collective-permute-start | bytes 36872 | tf_op jit(solution)/shard_map/ppermute | solution.py:371
  96.7 1.4 collective-permute-start.4
  115.3 1.3 collective-permute-start.5
  121.3 5.2 %collective-permute-start.6 = (f32[1544,384]{1,0:T(8,128)S(1)}, f32[1544,384]{1,0:T(8,128)S(1)}, u32[]{:S(2)}, u32[]{:S(2)}) collective-permute-start(f32[1544,384]{1,0:T(8,128)S(1)} %get-tuple-element.98), channel_id=1, source_target_pairs={{0,1},{1,0},{2,3},{3,2},{4,5},{5,4},{6,7},{7,6},{8,9},{9,8},{10,11... | collective-permute-start | bytes 7114760 | tf_op jit(solution)/shard_map/ppermute | solution.py:371
  127.6 26.8 %copy-start.2 = (bf16[24,384]{1,0:T(8,128)(2,1)S(1)}, bf16[24,384]{1,0:T(8,128)(2,1)}, u32[]{:S(2)}) copy-start(bf16[24,384]{1,0:T(8,128)(2,1)} %hid_ref.3) | copy-start | bytes 55300

commit v8 on v7

--- a/solution.py
+++ b/solution.py
@@ -14,7 +14,7 @@
 student_temp = 0.1
 
 ALL = ("z", "y", "x", "c")
-CHIPS = ("z", "y", "x")
+CHIPS = ("x", "y", "z")
 SWAP = [(0, 1), (1, 0)]
 F32 = jnp.float32
 BF16 = jnp.bfloat16

time: 156 us -> 154 us (0.987)
    all_to_all x5, blocking collectives: 122 us -> 121 us  [exchange(): return lax.all_to_all(x, CHIPS, 0, 0)]
where the time goes in v8:
time: 154 us
  blocking collectives  121 us (79%)
  Pallas kernels  29.1 us (19%)
  starting transfers between devices  2.03 us (1%)
    all_to_all x5, blocking collectives, exchange(): return lax.all_to_all(x, CHIPS, 0, 0)  121 us
    pallas_call x20, Pallas kernels, call(): pl.pallas_call(kernel, out_shape=out_shape, in_specs=[ANY if i in in_any...  29.1 us
  transfers between devices with their start and end apart: 7, of which 3 were waited for; matrix products, arithmetic and copies ran while one was open for 0% of the time, Pallas kernels for 9%

profile of v8, /device:TPU:0, one launch (start us, length us, event | category | flops | bytes accessed | tf_op | source)
XLA Modules:
  0.0 153.7 jit_solution(16577066408051017975)
XLA Ops:
  0.6 3.0 %shard_map.76 = (bf16[64,24,384]{2,1,0:T(8,128)(2,1)}, bf16[24,384]{1,0:T(8,128)(2,1)}) custom-call(bf16[24,384]{1,0:T(8,128)(2,1)} %hid_ref.3, bf16[24,2048]{1,0:T(8,128)(2,1)} %hid_ref.2, bf16[2048,384]{1,0:T(8,128)(2,1)} %proj_ref.1), custom_call_target="tpu_custom_call" | custom-call | tf_op jit(solution)/shard_map/pallas_call | solution.py:33
  3.7 31.7 %all_to_all.25 = bf16[64,24,384]{2,1,0:T(8,128)(2,1)S(1)} all-to-all(bf16[64,24,384]{2,1,0:T(8,128)(2,1)} %get-tuple-element.53), channel_id=1, replica_groups=mesh['z'=4,'y'=4,'x'=4,'c'=2] {'x','y','z'}, dimensions={0} | all-to-all | bytes 2359296 | tf_op jit(solution)/shard_map/all_to_all | solution.py:374
  35.4 2.1 %shard_map.77 = (f32[1024,1536]{1,0:T(8,128)S(1)}, bf16[1024,384]{1,0:T(8,128)(2,1)S(1)}, f32[1024,1]{1,0:T(8,128)S(1)}) custom-call(bf16[384,1024]{1,0:T(8,128)(2,1)S(1)} %copy-done.1, bf16[1536,384]{1,0:T(8,128)(2,1)S(1)} %bitcast.9), custom_call_target="tpu_custom_call" | custom-call | tf_op jit(solution)/shard_map/pallas_call | solution.py:33
  37.5 0.4 shard_map.78
  37.9 0.3 collective-permute-done.rows_ref
  38.2 3.1 %shard_map.79 = (f32[1024,1536]{1,0:T(8,128)S(1)}, bf16[64,32,384]{2,1,0:T(8,128)(2,1)S(1)}) custom-call(bf16[1024,384]{1,0:T(8,128)(2,1)S(1)} %get-tuple-element.60.lhs_ref, bf16[1536,384]{1,0:T(8,128)(2,1)S(1)} %collective-permute-done.rows_ref, f32[1024,1536]{1,0:T(8,128)S(1)} %get-tuple-element.54.e_own.own_ref.e_ref, ...), custom_call_target="tpu_custom_call" | custom-call | tf_op jit(solution)/shard_map/pallas_call | solution.py:33
  41.4 28.9 %all_to_all.26.got_ref = bf16[64,32,384]{2,1,0:T(8,128)(2,1)S(1)} all-to-all(bf16[64,32,384]{2,1,0:T(8,128)(2,1)S(1)} %get-tuple-element.64), channel_id=1, replica_groups=mesh['z'=4,'y'=4,'x'=4,'c'=2] {'x','y','z'}, dimensions={0} | all-to-all | bytes 3145728 | tf_op jit(solution)/shard_map/all_to_all | solution.py:374
  70.2 0.2 shard_map.80
  70.4 0.1 collective-permute-start.1
  70.5 1.4 shard_map.81
  72.0 0.6 collective-permute-start.2
  72.6 1.9 %shard_map.82 = (bf16[64,8,384]{2,1,0:T(8,128)(2,1)S(1)}, f32[8,384]{1,0:T(8,128)S(1)}) custom-call(f32[1024,1536]{1,0:T(8,128)S(1)} %get-tuple-element.54.e_own.own_ref.e_ref, f32[1024,1536]{1,0:T(8,128)S(1)} %get-tuple-element.67.other_ref.e_ref, f32[8,384]{1,0:T(8,128)S(1)} %get-tuple-element.68.mine_ref, f32[8,384]{1,0:T(8,128)S(1)} %collective-permute-done.1.theirs_ref), custom_call_target="tpu_custom_call" | custom-call | tf_op jit(solution)/shard_map/pallas_call | solution.py:33
  74.5 16.4 %all_to_all.27.got_ref = bf16[64,8,384]{2,1,0:T(8,128)(2,1)S(1)} all-to-all(bf16[64,8,384]{2,1,0:T(8,128)(2,1)S(1)} %get-tuple-element.71), channel_id=1, replica_groups=mesh['z'=4,'y'=4,'x'=4,'c'=2] {'x','y','z'}, dimensions={0} | all-to-all | bytes 786432 | tf_op jit(solution)/shard_map/all_to_all | solution.py:374
  90.9 0.1 shard_map.83.mine_ref
  91.0 0.3 collective-permute-start.3
  91.3 1.9 %shard_map.84 = (f32[1024,1536]{1,0:T(8,128)S(1)}, f32[4,384]{1,0:T(4,128)S(1)}) custom-call(bf16[1024,384]{1,0:T(8,128)(2,1)S(1)} %get-tuple-element.59.lhs_ref, bf16[1536,384]{1,0:T(8,128)(2,1)S(1)} %collective-permute-done.2.rows_ref), custom_call_target="tpu_custom_call" | custom-call | tf_op jit(solution)/shard_map/pallas_call | solution.py:33
  93.2 1.9 %shard_map.85 = (f32[8,384]{1,0:T(8,128)S(1)}, f32[8,384]{1,0:T(8,128)S(1)}, f32[1024,1]{1,0:T(8,128)S(1)}) custom-call(f32[1024,1536]{1,0:T(8,128)S(1)} %get-tuple-element.54.e_own.own_ref.e_ref, f32[1024,1536]{1,0:T(8,128)S(1)} %get-tuple-element.67.other_ref.e_ref, f32[8,384]{1,0:T(8,128)S(1)} %shard_map.83.mine_ref, ...), custom_call_target="tpu_custom_call" | custom-call | tf_op jit(solution)/shard_map/pallas_call | solution.py:33
  95.1 0.6 collective-permute-start.4
  95.7 0.6 shard_map.87
  96.3 0.2 collective-permute-done.4.theirs_ref
  96.6 17.0 %all_to_all.28.got_ref = bf16[64,8,384]{2,1,0:T(8,128)(2,1)S(1)} all-to-all(bf16[64,8,384]{2,1,0:T(8,128)(2,1)S(1)} %shard_map.88), channel_id=1, replica_groups=mesh['z'=4,'y'=4,'x'=4,'c'=2] {'x','y','z'}, dimensions={0} | all-to-all | bytes 786432 | tf_op jit(solution)/shard_map/all_to_all | solution.py:374
  113.6 0.1 shard_map.89.mine_ref
  113.7 0.1 collective-permute-start.5
  113.8 0.4 shard_map.90.turned_ref
  114.1 0.4 shard_map.91.turned_ref
  114.5 0.4 collective-permute-done.5.theirs_ref
  114.9 4.7 %shard_map.92 = (f32[1544,384]{1,0:T(8,128)S(1)}, f32[384,1024]{1,0:T(8,128)S(1)}, f32[1,384]{1,0:T(1,128)S(1)}) custom-call(f32[1024,1536]{1,0:T(8,128)S(1)} %get-tuple-element.67.other_ref.e_ref, f32[1024,1536]{1,0:T(8,128)S(1)} %get-tuple-element.93.lg_other, f32[1024,1]{1,0:T(8,128)S(1)} %get-tuple-element.82.cs_ref, ...), custom_call_target="tpu_custom_call" | custom-call | tf_op jit(solution)/shard_map/pallas_call | solution.py:33
  119.7 0.5 collective-permute-start.6
  120.1 4.7 %shard_map.93 = (f32[1536,384]{1,0:T(8,128)S(1)}, f32[384,1024]{1,0:T(8,128)}) custom-call(f32[1024,1536]{1,0:T(8,128)S(1)} %get-tuple-element.54.e_own.own_ref.e_ref, f32[768,1536]{1,0:T(8,128)S(1)} %get-tuple-element.66.lg_own_a.lg_a, f32[256,1536]{1,0:T(8,128)S(1)} %get-tuple-element.81.lg_own_b.lg_b, f32[1024,1]{1,0:T(8,128)S(1)} %get-tuple-element.82.cs_ref, ...), custom_call_target="tpu_custom_call" | custom-call | tf_op jit(solution)/shard_map/pallas_call | solution.py:33
  124.9 1.1 shard_map.94
  126.0 26.7 %all_to_all.29.got_ref = bf16[64,80,128]{2,1,0:T(8,128)(2,1)S(1)} all-to-all(bf16[64,80,128]{2,1,0:T(8,128)(2,1)S(1)} %shard_map.94), channel_id=1, replica_groups=mesh['z'=4,'y'=4,'x'=4,'c'=2] {'x','y','z'}, dimensions={0} | all-to-all | bytes 2621440 | tf_op jit(solution)/shard_map/all_to_all | solution.py:374
  152.7 1.0 shard_map.95
  (15 shorter events, 0.1 us)
Async XLA Ops:
  3.7 31.7 %copy-start.1 = (bf16[384,1024]{1,0:T(8,128)(2,1)S(1)}, bf16[384,1024]{1,0:T(8,128)(2,1)}, u32[]{:S(2)}) copy-start(bf16[384,1024]{1,0:T(8,128)(2,1)} %w_ref.2) | copy-start | bytes 2359300
  35.4 2.1 %copy-start = (bf16[384,1024]{1,0:T(8,128)(2,1)S(1)}, bf16[384,1024]{1,0:T(8,128)(2,1)}, u32[]{:S(2)}) copy-start(bf16[384,1024]{1,0:T(8,128)(2,1)} %w_ref.4) | copy-start | bytes 2359300
  35.4 2.9 %copy-start.3 = (bf16[24,384]{1,0:T(8,128)(2,1)S(1)}, bf16[24,384]{1,0:T(8,128)(2,1)}, u32[]{:S(2)}) copy-start(bf16[24,384]{1,0:T(8,128)(2,1)} %get-tuple-element.63.s_ref) | copy-start | bytes 55300
  35.4 2.8 %collective-permute-start = (bf16[1536,384]{1,0:T(8,128)(2,1)S(1)}, bf16[1536,384]{1,0:T(8,128)(2,1)S(1)}, u32[]{:S(2)}, u32[]{:S(2)}) collective-permute-start(bf16[1536,384]{1,0:T(8,128)(2,1)S(1)} %bitcast.8), channel_id=1, source_target_pairs={{0,1},{1,0},{2,3},{3,2},{4,5},{5,4},{6,7},{7,6},{8,9},{9,8},{10,11... | collective-permute-start | bytes 3538952 | tf_op jit(solution)/shard_map/ppermute | solution.py:371
  70.4 1.5 %collective-permute-start.1 = (f32[8,384]{1,0:T(8,128)S(1)}, f32[8,384]{1,0:T(8,128)S(1)}, u32[]{:S(2)}, u32[]{:S(2)}) collective-permute-start(f32[8,384]{1,0:T(8,128)S(1)} %get-tuple-element.68.mine_ref), channel_id=1, source_target_pairs={{0,1},{1,0},{2,3},{3,2},{4,5},{5,4},{6,7},{7,6},{8,9},{9,8},{10,11... | collective-permute-start | bytes 36872 | tf_op jit(solution)/shard_map/ppermute | solution.py:371
  72.0 19.3 %collective-permute-start.2 = (bf16[1536,384]{1,0:T(8,128)(2,1)S(1)}, bf16[1536,384]{1,0:T(8,128)(2,1)S(1)}, u32[]{:S(2)}, u32[]{:S(2)}) collective-permute-start(bf16[1536,384]{1,0:T(8,128)(2,1)S(1)} %bitcast.5), channel_id=1, source_target_pairs={{0,1},{1,0},{2,3},{3,2},{4,5},{5,4},{6,7},{7,6},{8,9},{9,8},{10,11... | collective-permute-start | bytes 3538952 | tf_op jit(solution)/shard_map/ppermute | solution.py:371
  91.0 2.2 %collective-permute-start.3 = (f32[8,384]{1,0:T(8,128)S(1)}, f32[8,384]{1,0:T(8,128)S(1)}, u32[]{:S(2)}, u32[]{:S(2)}) collective-permute-start(f32[8,384]{1,0:T(8,128)S(1)} %shard_map.83.mine_ref), channel_id=1, source_target_pairs={{0,1},{1,0},{2,3},{3,2},{4,5},{5,4},{6,7},{7,6},{8,9},{9,8},{10,11... | collective-permute-start | bytes 36872 | tf_op jit(solution)/shard_map/ppermute | solution.py:371
  95.1 1.4 collective-permute-start.4
  113.7 1.3 collective-permute-start.5
  119.7 5.2 %collective-permute-start.6 = (f32[1544,384]{1,0:T(8,128)S(1)}, f32[1544,384]{1,0:T(8,128)S(1)}, u32[]{:S(2)}, u32[]{:S(2)}) collective-permute-start(f32[1544,384]{1,0:T(8,128)S(1)} %get-tuple-element.98), channel_id=1, source_target_pairs={{0,1},{1,0},{2,3},{3,2},{4,5},{5,4},{6,7},{7,6},{8,9},{9,8},{10,11... | collective-permute-start | bytes 7114760 | tf_op jit(solution)/shard_map/ppermute | solution.py:371
  126.0 26.7 %copy-start.2 = (bf16[24,384]{1,0:T(8,128)(2,1)S(1)}, bf16[24,384]{1,0:T(8,128)(2,1)}, u32[]{:S(2)}) copy-start(bf16[24,384]{1,0:T(8,128)(2,1)} %hid_ref.3) | copy-start | bytes 55300

commit v9 on v8

--- a/solution.py
+++ b/solution.py
@@ -423,7 +423,7 @@
         shapes = (sds((stop - start, half), F32), vec4)
         return call(functools.partial(student_kernel, start), shapes, (s_lhs, rows), 8, [half_acc])
 
-    split = protos * 3 // 4
+    split = protos // 2
     lg_own_a, part_own = student(0, split, s_own)
     theirs, part_own, s_late = lax.optimization_barrier((theirs, part_own, s_own))
     s_other = swap(s_late)

time: 154 us -> 154 us (level)
  no operation moved by 1% of the time
where the time goes in v9:
time: 154 us; the launch traced here: 153 us
  blocking collectives  121 us (79%)
  Pallas kernels  29 us (19%)
  starting transfers between devices  1.92 us (1%)
    all_to_all x5, blocking collectives, exchange(): return lax.all_to_all(x, CHIPS, 0, 0)  121 us
    pallas_call x20, Pallas kernels, call(): pl.pallas_call(kernel, out_shape=out_shape, in_specs=[ANY if i in in_any...  29 us
  transfers between devices with their start and end apart: 7, of which 3 were waited for; matrix products, arithmetic and copies ran while one was open for 0% of the time, Pallas kernels for 9%

profile of v9, /device:TPU:0, one launch (start us, length us, event | category | flops | bytes accessed | tf_op | source)
XLA Modules:
  0.0 153.3 jit_solution(4336936281671835005)
XLA Ops:
  0.6 3.0 %shard_map.76 = (bf16[64,24,384]{2,1,0:T(8,128)(2,1)}, bf16[24,384]{1,0:T(8,128)(2,1)}) custom-call(bf16[24,384]{1,0:T(8,128)(2,1)} %hid_ref.3, bf16[24,2048]{1,0:T(8,128)(2,1)} %hid_ref.2, bf16[2048,384]{1,0:T(8,128)(2,1)} %proj_ref.1), custom_call_target="tpu_custom_call" | custom-call | tf_op jit(solution)/shard_map/pallas_call | solution.py:33
  3.7 31.7 %all_to_all.25 = bf16[64,24,384]{2,1,0:T(8,128)(2,1)S(1)} all-to-all(bf16[64,24,384]{2,1,0:T(8,128)(2,1)} %get-tuple-element.53), channel_id=1, replica_groups=mesh['z'=4,'y'=4,'x'=4,'c'=2] {'x','y','z'}, dimensions={0} | all-to-all | bytes 2359296 | tf_op jit(solution)/shard_map/all_to_all | solution.py:374
  35.4 2.1 %shard_map.77 = (f32[1024,1536]{1,0:T(8,128)S(1)}, bf16[1024,384]{1,0:T(8,128)(2,1)S(1)}, f32[1024,1]{1,0:T(8,128)S(1)}) custom-call(bf16[384,1024]{1,0:T(8,128)(2,1)S(1)} %copy-done.1, bf16[1536,384]{1,0:T(8,128)(2,1)S(1)} %bitcast.9), custom_call_target="tpu_custom_call" | custom-call | tf_op jit(solution)/shard_map/pallas_call | solution.py:33
  37.5 0.4 shard_map.78
  37.9 0.3 collective-permute-done.rows_ref
  38.2 3.1 %shard_map.79 = (f32[1024,1536]{1,0:T(8,128)S(1)}, bf16[64,32,384]{2,1,0:T(8,128)(2,1)S(1)}) custom-call(bf16[1024,384]{1,0:T(8,128)(2,1)S(1)} %get-tuple-element.60.lhs_ref, bf16[1536,384]{1,0:T(8,128)(2,1)S(1)} %collective-permute-done.rows_ref, f32[1024,1536]{1,0:T(8,128)S(1)} %get-tuple-element.54.e_own.own_ref.e_ref, ...), custom_call_target="tpu_custom_call" | custom-call | tf_op jit(solution)/shard_map/pallas_call | solution.py:33
  41.4 28.9 %all_to_all.26.got_ref = bf16[64,32,384]{2,1,0:T(8,128)(2,1)S(1)} all-to-all(bf16[64,32,384]{2,1,0:T(8,128)(2,1)S(1)} %get-tuple-element.64), channel_id=1, replica_groups=mesh['z'=4,'y'=4,'x'=4,'c'=2] {'x','y','z'}, dimensions={0} | all-to-all | bytes 3145728 | tf_op jit(solution)/shard_map/all_to_all | solution.py:374
  70.2 0.2 shard_map.80
  70.4 0.1 collective-permute-start.1
  70.5 1.0 shard_map.81
  71.6 0.1 collective-permute-done.1.theirs_ref
  71.7 0.5 collective-permute-start.2
  72.1 1.9 %shard_map.82 = (bf16[64,8,384]{2,1,0:T(8,128)(2,1)S(1)}, f32[8,384]{1,0:T(8,128)S(1)}) custom-call(f32[1024,1536]{1,0:T(8,128)S(1)} %get-tuple-element.54.e_own.own_ref.e_ref, f32[1024,1536]{1,0:T(8,128)S(1)} %get-tuple-element.67.other_ref.e_ref, f32[8,384]{1,0:T(8,128)S(1)} %get-tuple-element.68.mine_ref, f32[8,384]{1,0:T(8,128)S(1)} %collective-permute-done.1.theirs_ref), custom_call_target="tpu_custom_call" | custom-call | tf_op jit(solution)/shard_map/pallas_call | solution.py:33
  74.1 16.5 %all_to_all.27.got_ref = bf16[64,8,384]{2,1,0:T(8,128)(2,1)S(1)} all-to-all(bf16[64,8,384]{2,1,0:T(8,128)(2,1)S(1)} %get-tuple-element.71), channel_id=1, replica_groups=mesh['z'=4,'y'=4,'x'=4,'c'=2] {'x','y','z'}, dimensions={0} | all-to-all | bytes 786432 | tf_op jit(solution)/shard_map/all_to_all | solution.py:374
  90.5 0.1 shard_map.83.mine_ref
  90.6 0.3 collective-permute-start.3
  90.9 1.9 %shard_map.84 = (f32[1024,1536]{1,0:T(8,128)S(1)}, f32[4,384]{1,0:T(4,128)S(1)}) custom-call(bf16[1024,384]{1,0:T(8,128)(2,1)S(1)} %get-tuple-element.59.lhs_ref, bf16[1536,384]{1,0:T(8,128)(2,1)S(1)} %collective-permute-done.2.rows_ref), custom_call_target="tpu_custom_call" | custom-call | tf_op jit(solution)/shard_map/pallas_call | solution.py:33
  92.9 1.9 %shard_map.85 = (f32[8,384]{1,0:T(8,128)S(1)}, f32[8,384]{1,0:T(8,128)S(1)}, f32[1024,1]{1,0:T(8,128)S(1)}) custom-call(f32[1024,1536]{1,0:T(8,128)S(1)} %get-tuple-element.54.e_own.own_ref.e_ref, f32[1024,1536]{1,0:T(8,128)S(1)} %get-tuple-element.67.other_ref.e_ref, f32[8,384]{1,0:T(8,128)S(1)} %shard_map.83.mine_ref, ...), custom_call_target="tpu_custom_call" | custom-call | tf_op jit(solution)/shard_map/pallas_call | solution.py:33
  94.8 0.6 collective-permute-start.4
  95.3 1.0 shard_map.87
  96.4 16.8 %all_to_all.28.got_ref = bf16[64,8,384]{2,1,0:T(8,128)(2,1)S(1)} all-to-all(bf16[64,8,384]{2,1,0:T(8,128)(2,1)S(1)} %shard_map.88), channel_id=1, replica_groups=mesh['z'=4,'y'=4,'x'=4,'c'=2] {'x','y','z'}, dimensions={0} | all-to-all | bytes 786432 | tf_op jit(solution)/shard_map/all_to_all | solution.py:374
  113.2 0.1 shard_map.89.mine_ref
  113.3 0.1 collective-permute-start.5
  113.4 0.4 shard_map.90.turned_ref
  113.8 0.4 shard_map.91.turned_ref
  114.1 0.4 collective-permute-done.5.theirs_ref
  114.6 4.7 %shard_map.92 = (f32[1544,384]{1,0:T(8,128)S(1)}, f32[384,1024]{1,0:T(8,128)S(1)}, f32[1,384]{1,0:T(1,128)S(1)}) custom-call(f32[1024,1536]{1,0:T(8,128)S(1)} %get-tuple-element.67.other_ref.e_ref, f32[1024,1536]{1,0:T(8,128)S(1)} %get-tuple-element.93.lg_other, f32[1024,1]{1,0:T(8,128)S(1)} %get-tuple-element.82.cs_ref, ...), custom_call_target="tpu_custom_call" | custom-call | tf_op jit(solution)/shard_map/pallas_call | solution.py:33
  119.3 0.5 collective-permute-start.6
  119.8 4.7 %shard_map.93 = (f32[1536,384]{1,0:T(8,128)S(1)}, f32[384,1024]{1,0:T(8,128)}) custom-call(f32[1024,1536]{1,0:T(8,128)S(1)} %get-tuple-element.54.e_own.own_ref.e_ref, f32[512,1536]{1,0:T(8,128)S(1)} %get-tuple-element.66.lg_own_a.lg_a, f32[512,1536]{1,0:T(8,128)S(1)} %get-tuple-element.81.lg_own_b.lg_b, f32[1024,1]{1,0:T(8,128)S(1)} %get-tuple-element.82.cs_ref, ...), custom_call_target="tpu_custom_call" | custom-call | tf_op jit(solution)/shard_map/pallas_call | solution.py:33
  124.5 1.1 shard_map.94
  125.5 26.7 %all_to_all.29.got_ref = bf16[64,80,128]{2,1,0:T(8,128)(2,1)S(1)} all-to-all(bf16[64,80,128]{2,1,0:T(8,128)(2,1)S(1)} %shard_map.94), channel_id=1, replica_groups=mesh['z'=4,'y'=4,'x'=4,'c'=2] {'x','y','z'}, dimensions={0} | all-to-all | bytes 2621440 | tf_op jit(solution)/shard_map/all_to_all | solution.py:374
  152.2 1.0 shard_map.95
  (15 shorter events, 0.1 us)
Async XLA Ops:
  3.7 31.7 %copy-start.1 = (bf16[384,1024]{1,0:T(8,128)(2,1)S(1)}, bf16[384,1024]{1,0:T(8,128)(2,1)}, u32[]{:S(2)}) copy-start(bf16[384,1024]{1,0:T(8,128)(2,1)} %w_ref.2) | copy-start | bytes 2359300
  35.4 2.1 %copy-start = (bf16[384,1024]{1,0:T(8,128)(2,1)S(1)}, bf16[384,1024]{1,0:T(8,128)(2,1)}, u32[]{:S(2)}) copy-start(bf16[384,1024]{1,0:T(8,128)(2,1)} %w_ref.4) | copy-start | bytes 2359300
  35.4 2.9 %copy-start.3 = (bf16[24,384]{1,0:T(8,128)(2,1)S(1)}, bf16[24,384]{1,0:T(8,128)(2,1)}, u32[]{:S(2)}) copy-start(bf16[24,384]{1,0:T(8,128)(2,1)} %get-tuple-element.63.s_ref) | copy-start | bytes 55300
  35.4 2.8 %collective-permute-start = (bf16[1536,384]{1,0:T(8,128)(2,1)S(1)}, bf16[1536,384]{1,0:T(8,128)(2,1)S(1)}, u32[]{:S(2)}, u32[]{:S(2)}) collective-permute-start(bf16[1536,384]{1,0:T(8,128)(2,1)S(1)} %bitcast.8), channel_id=1, source_target_pairs={{0,1},{1,0},{2,3},{3,2},{4,5},{5,4},{6,7},{7,6},{8,9},{9,8},{10,11... | collective-permute-start | bytes 3538952 | tf_op jit(solution)/shard_map/ppermute | solution.py:371
  70.4 1.3 collective-permute-start.1
  71.7 19.2 %collective-permute-start.2 = (bf16[1536,384]{1,0:T(8,128)(2,1)S(1)}, bf16[1536,384]{1,0:T(8,128)(2,1)S(1)}, u32[]{:S(2)}, u32[]{:S(2)}) collective-permute-start(bf16[1536,384]{1,0:T(8,128)(2,1)S(1)} %bitcast.5), channel_id=1, source_target_pairs={{0,1},{1,0},{2,3},{3,2},{4,5},{5,4},{6,7},{7,6},{8,9},{9,8},{10,11... | collective-permute-start | bytes 3538952 | tf_op jit(solution)/shard_map/ppermute | solution.py:371
  90.6 2.2 %collective-permute-start.3 = (f32[8,384]{1,0:T(8,128)S(1)}, f32[8,384]{1,0:T(8,128)S(1)}, u32[]{:S(2)}, u32[]{:S(2)}) collective-permute-start(f32[8,384]{1,0:T(8,128)S(1)} %shard_map.83.mine_ref), channel_id=1, source_target_pairs={{0,1},{1,0},{2,3},{3,2},{4,5},{5,4},{6,7},{7,6},{8,9},{9,8},{10,11... | collective-permute-start | bytes 36872 | tf_op jit(solution)/shard_map/ppermute | solution.py:371
  94.8 1.6 %collective-permute-start.4 = (f32[8,384]{1,0:T(8,128)S(1)}, f32[8,384]{1,0:T(8,128)S(1)}, u32[]{:S(2)}, u32[]{:S(2)}) collective-permute-start(f32[8,384]{1,0:T(8,128)S(1)} %shard_map.86), channel_id=1, source_target_pairs={{0,1},{1,0},{2,3},{3,2},{4,5},{5,4},{6,7},{7,6},{8,9},{9,8},{10,11... | collective-permute-start | bytes 36872 | tf_op jit(solution)/shard_map/ppermute | solution.py:371
  113.3 1.3 collective-permute-start.5
  119.3 5.1 %collective-permute-start.6 = (f32[1544,384]{1,0:T(8,128)S(1)}, f32[1544,384]{1,0:T(8,128)S(1)}, u32[]{:S(2)}, u32[]{:S(2)}) collective-permute-start(f32[1544,384]{1,0:T(8,128)S(1)} %get-tuple-element.98), channel_id=1, source_target_pairs={{0,1},{1,0},{2,3},{3,2},{4,5},{5,4},{6,7},{7,6},{8,9},{9,8},{10,11... | collective-permute-start | bytes 7114760 | tf_op jit(solution)/shard_map/ppermute | solution.py:371
  125.5 26.7 %copy-start.2 = (bf16[24,384]{1,0:T(8,128)(2,1)S(1)}, bf16[24,384]{1,0:T(8,128)(2,1)}, u32[]{:S(2)}) copy-start(bf16[24,384]{1,0:T(8,128)(2,1)} %hid_ref.3) | copy-start | bytes 55300
